TPU v7x, 32 devices: a whole 2x2x4 slice. The times are simulated.
32 devices in a mesh: groups: 2 (over x), wide: 8 (over z, y), narrow: 2 (over core).
Axes of the slice: x: 2, y: 2, z: 4, core: 2. Of those that a mesh axis runs over, the one named last changes fastest.
Arguments:
- first_input: bfloat16 [64, 8192], P('groups', 'wide'), parts along dimension 0, may hold values from -6 to 6
- second_input: bfloat16 [64, 8192], P('groups', 'wide'), parts along dimension 0, may hold values from -6 to 6
- norm_gain: bfloat16 [8192], P('wide'), may hold values from 0.099609375 to 1.8984375
- w_query: bfloat16 [8192, 8192], P('wide', 'narrow'), may hold values from -0.05 to 0.05
- w_key: bfloat16 [8192, 512], P('wide', 'narrow'), may hold values from -0.05 to 0.05
- w_value: bfloat16 [8192, 512], P('wide', 'narrow'), may hold values from -0.0625 to 0.0625
- w_output: bfloat16 [8192, 8192], P('narrow', 'wide'), may hold values from -0.0625 to 0.0625
- key_cache: bfloat16 [64, 4, 2048, 128], P(('groups', 'wide'), 'narrow'), parts along dimension 0, may hold values from -400 to 400
- value_cache: bfloat16 [64, 4, 2048, 128], P(('groups', 'wide'), 'narrow'), parts along dimension 0, may hold values from -12 to 12
- lengths: int32 [64], P(('groups', 'wide')), parts along dimension 0, may hold values from 2 to 2048, as said below
- positions: int32 [64], P(('groups', 'wide')), parts along dimension 0, may hold values from 0 to 4095
Outputs:
- first_output: bfloat16 [64, 8192], P('groups', 'wide'), parts along dimension 0
- second_output: bfloat16 [64, 8192], P('groups', 'wide'), parts along dimension 0
There are 2 independent parts, one for each index of `groups`. A program takes and returns all parts, laid end to end along the dimension named above; an argument that names none is the same for every part. Nothing has to cross between parts.
Inputs may be any that keep to these rules, and one draw needn't show every extreme that they name: A request's cache holds lengths of its 2048 slots, from slot 0 on; the other slots are not part of it.
All inputs are finite; a program needn't handle non-finite values.
Results may differ from a plain program's by a relative error of at most 0.012.
Values may be sent and summed in bfloat16 or wider, within the bound.
No kernel may reach another device: no remote copies, remote signals or barrier semaphores. Data moves between devices by JAX's collectives and lax.ppermute only.
A program may use at most 128 MiB of HBM per device.

v0:
```python
import math

import jax
import jax.numpy as jnp
from jax import lax
from jax.sharding import PartitionSpec as P

D = 8192
MAXLEN = 2048
BLOCK = 512


EPSILON = 1e-05
THETA = 500000.0
NEGATIVE = -1e30


def rotate(values, where_at):
    half = values.shape[-1] // 2
    inverse = jnp.exp(
        jnp.arange(half, dtype=jnp.float32) * (-2.0 * math.log(THETA) / values.shape[-1])
    )
    angle = where_at.astype(jnp.float32)[:, None, None] * inverse
    cosine = jnp.cos(angle)
    sine = jnp.sin(angle)
    first = values[..., :half]
    second = values[..., half:]
    return jnp.concatenate(
        [first * cosine - second * sine, second * cosine + first * sine], axis=-1
    )


def make_terms(sources, norm_gain, w_query, w_key, w_value):
    gain_wide = norm_gain.astype(jnp.float32)

    def term(start, count):
        pieces = []
        for source in sources:
            scaled = (source.astype(jnp.float32) * gain_wide).astype(jnp.bfloat16)
            pieces.append(jnp.dot(scaled, w_query, preferred_element_type=jnp.float32))
            pieces.append(jnp.dot(scaled, w_key, preferred_element_type=jnp.float32))
            pieces.append(jnp.dot(scaled, w_value, preferred_element_type=jnp.float32))
        return jnp.concatenate(pieces, axis=1)

    return term


def reduce_projection(sources, norm_gain, w_query, w_key, w_value, rows_dev, mine):
    local_sums = jnp.stack(
        [jnp.sum(jnp.square(source.astype(jnp.float32)), axis=1) for source in sources]
    )
    squares = lax.psum(local_sums, "wide")
    term = make_terms(sources, norm_gain, w_query, w_key, w_value)
    summed = lax.psum_scatter(
        term(jnp.int32(0), rows_dev * lax.axis_size("wide")),
        "wide",
        scatter_dimension=0,
        tiled=True,
    )
    scales = lax.rsqrt(squares / D + EPSILON)
    own = lax.dynamic_slice_in_dim(scales, mine, rows_dev, 1)
    span = summed.shape[1] // len(sources)
    return [
        summed[:, index * span : (index + 1) * span] * own[index][:, None]
        for index in range(len(sources))
    ]


def split_heads(projected, where_at, heads, kv_heads, width):
    rows = projected.shape[0]
    query = projected[:, : heads * width].reshape(rows, heads, width)
    keys = projected[:, heads * width : (heads + kv_heads) * width].reshape(rows, kv_heads, width)
    values = projected[:, (heads + kv_heads) * width :].reshape(rows, kv_heads, width)
    return (
        rotate(query, where_at).astype(jnp.bfloat16),
        rotate(keys, where_at).astype(jnp.bfloat16),
        values.astype(jnp.bfloat16),
    )


def attend(query, new_keys, new_values, key_cache, value_cache, lengths, block_count):
    rows, heads, width = query.shape
    kv_heads = key_cache.shape[1]
    grouped = query.reshape(rows, kv_heads, heads // kv_heads, width)
    scale = 1.0 / math.sqrt(width)
    fresh = (
        jnp.einsum("rkgd,rknd->rkgn", grouped, new_keys, preferred_element_type=jnp.float32) * scale
    )
    top = jnp.max(fresh, axis=-1)
    weight = jnp.exp(fresh - top[..., None])
    total = jnp.sum(weight, axis=-1)
    mixed = jnp.einsum(
        "rkgn,rknd->rkgd",
        weight.astype(jnp.bfloat16),
        new_values,
        preferred_element_type=jnp.float32,
    )

    def advance(index, carry):
        top, total, mixed = carry
        begin = index * BLOCK
        block_keys = lax.dynamic_slice_in_dim(key_cache, begin, BLOCK, 2)
        block_values = lax.dynamic_slice_in_dim(value_cache, begin, BLOCK, 2)
        scores = (
            jnp.einsum("rkgd,rktd->rkgt", grouped, block_keys, preferred_element_type=jnp.float32)
            * scale
        )
        live = ((begin + jnp.arange(BLOCK))[None, :] < lengths[:, None])[:, None, None, :]
        scores = jnp.where(live, scores, NEGATIVE)
        new_top = jnp.maximum(top, jnp.max(scores, axis=-1))
        factor = jnp.exp(top - new_top)
        weight = jnp.where(live, jnp.exp(scores - new_top[..., None]), 0.0)
        total = total * factor + jnp.sum(weight, axis=-1)
        mixed = mixed * factor[..., None] + jnp.einsum(
            "rkgt,rktd->rkgd",
            weight.astype(jnp.bfloat16),
            block_values,
            preferred_element_type=jnp.float32,
        )
        return (new_top, total, mixed)

    top, total, mixed = lax.fori_loop(0, block_count, advance, (top, total, mixed))
    return (mixed / total[..., None]).astype(jnp.bfloat16).reshape(rows, heads * width)


def combine_output(stacked, sources, w_output):
    terms = jnp.einsum(
        "srk,kd->srd",
        lax.all_gather(stacked, "wide", axis=1, tiled=True),
        w_output,
        preferred_element_type=jnp.float32,
    )
    total = lax.psum(terms.astype(jnp.bfloat16), "narrow").astype(jnp.float32)
    return [
        (source.astype(jnp.float32) + total[index]).astype(jnp.bfloat16)
        for index, source in enumerate(sources)
    ]


def on_device(
    first_input,
    second_input,
    norm_gain,
    w_query,
    w_key,
    w_value,
    w_output,
    key_cache,
    value_cache,
    lengths,
    positions,
):
    rows_dev = key_cache.shape[0]
    mine = lax.axis_index("wide") * rows_dev
    width = key_cache.shape[3]
    kv_heads = key_cache.shape[1]
    heads = w_query.shape[1] // width
    block_count = MAXLEN // BLOCK
    first_proj, second_proj = reduce_projection(
        (first_input, second_input), norm_gain, w_query, w_key, w_value, rows_dev, mine
    )
    query_one, key_one, value_one = split_heads(first_proj, positions, heads, kv_heads, width)
    query_two, key_two, value_two = split_heads(second_proj, positions + 1, heads, kv_heads, width)
    attended_one = attend(
        query_one,
        key_one[:, :, None, :],
        value_one[:, :, None, :],
        key_cache,
        value_cache,
        lengths,
        block_count,
    )
    attended_two = attend(
        query_two,
        jnp.stack([key_one, key_two], axis=2),
        jnp.stack([value_one, value_two], axis=2),
        key_cache,
        value_cache,
        lengths,
        block_count,
    )
    first_output, second_output = combine_output(
        jnp.stack([attended_one, attended_two]), (first_input, second_input), w_output
    )
    return (first_output, second_output)


def solution(mesh):
    return jax.shard_map(
        on_device,
        mesh=mesh,
        in_specs=(
            P("groups", "wide"),
            P("groups", "wide"),
            P("wide"),
            P("wide", "narrow"),
            P("wide", "narrow"),
            P("wide", "narrow"),
            P("narrow", "wide"),
            P(("groups", "wide"), "narrow", None, None),
            P(("groups", "wide"), "narrow", None, None),
            P(("groups", "wide")),
            P(("groups", "wide")),
        ),
        out_specs=(P("groups", "wide"), P("groups", "wide")),
        check_vma=False,
    )
```

profile of v0, /device:TPU:0, one launch (start us, length us, event | category | flops | bytes accessed | tf_op | source)
XLA Modules:
  0.0 194.7 jit_solution(2282613608611497337)
XLA Ops:
  8.0 5.1 %convolution_dynamic-update-slice_fusion.1 = f32[32,9216]{1,0:T(8,128)S(1)} fusion(bf16[1024,4096]{1,0:T(8,128)(2,1)} %param.18, bf16[32,1024]{1,0:T(8,128)(2,1)} %param.15, f32[1024]{0:T(1024)S(1)} %convert_element_type.114), kind=kOutput, calls=%fused_computation.41 | convolution fusion | flops 268533760 | bytes 8982528 | tf_op jit(solution)/shard_map/dot_general | solution.py:40
  14.0 1.5 convolution_dynamic-update-slice_fusion
  18.6 23.6 %psum.14 = f32[2,32]{1,0:T(2,128)S(1)} all-reduce(f32[2,32]{1,0:T(2,128)S(1)} %pad_maximum_fusion.3), channel_id=1, replica_groups=mesh['groups'=2,'wide'=8,'narrow'=2] {'wide'}, use_global_device_ids=true, to_apply=%region_3.0 | all-reduce | flops 64 | bytes 512 | tf_op jit(solution)/shard_map/psum | solution.py:52
  42.5 57.7 %all-reduce.6.cloned.1.call-done = f32[32,9216]{1,0:T(8,128)} async-done(((f32[32,9216]{1,0:T(8,128)}), f32[32,9216]{1,0:T(8,128)}) %all-reduce.6.cloned.1.call-update) | async-done | bytes 1179664
  101.9 14.4 %while.34 = (s32[]{:T(128)}, f32[4,2,16]{2,1,0:T(2,128)S(1)}, f32[4,2,16]{2,1,0:T(2,128)S(1)}, f32[4,2,16,128]{3,2,1,0:T(8,128)S(1)}, s32[4]{0:T(128)S(1)}, /*in...) while((s32[]{:T(128)}, f32[4,2,16]{2,1,0:T(2,128)S(1)}, ...), condition=%wide.region_7.0_spmd, body=%wide.region_4.7_spmd.sunk | while | flops 34179844 | bytes 3068095 | solution.py:122
  102.0 1.7 fusion.95
  103.9 1.5 convolution_add_fusion.4
  105.6 1.7 fusion.95
  107.5 1.5 convolution_add_fusion.4
  109.2 1.7 fusion.95
  111.1 1.5 convolution_add_fusion.4
  112.8 1.7 fusion.95
  114.7 1.5 convolution_add_fusion.4
  117.2 14.3 %while.35 = (s32[]{:T(128)}, f32[4,2,16]{2,1,0:T(2,128)S(1)}, f32[4,2,16]{2,1,0:T(2,128)S(1)}, f32[4,2,16,128]{3,2,1,0:T(8,128)S(1)}, s32[4]{0:T(128)S(1)}, /*in...) while((s32[]{:T(128)}, f32[4,2,16]{2,1,0:T(2,128)S(1)}, ...), condition=%wide.region_13.0_spmd, body=%wide.region_10.13_spmd.sunk | while | flops 34179844 | bytes 3068095 | solution.py:122
  117.3 1.7 fusion.100
  119.2 1.5 convolution_add_fusion.5
  120.9 1.7 fusion.100
  122.8 1.5 convolution_add_fusion.5
  124.5 1.7 fusion.100
  126.4 1.5 convolution_add_fusion.5
  128.1 1.7 fusion.100
  131.8 31.5 %all_gather.3 = bf16[2,32,4096]{2,0,1:T(2,128)(2,1)S(1)} all-gather(bf16[2,4,4096]{2,0,1:T(2,128)(2,1)S(1)} %copy.38), channel_id=1, replica_groups=mesh['groups'=2,'wide'=8,'narrow'=2] {'wide'}, dimensions={1}, use_global_device_ids=true | all-gather | bytes 589824 | tf_op jit(solution)/shard_map/all_gather | solution.py:129
  163.4 5.8 %fusion.28 = bf16[2,32,1024]{2,1,0:T(8,128)(2,1)} fusion(bf16[4096,1024]{1,0:T(8,128)(2,1)} %param.21, bf16[2,32,4096]{2,0,1:T(2,128)(2,1)S(1)} %all_gather.3), kind=kOutput, calls=%fused_computation.42 | convolution fusion | flops 536936448 | bytes 9043968 | tf_op jit(solution)/shard_map/srk,kd->srd/dot_general | solution.py:127
  169.2 17.1 %all-reduce.4.cloned.1.call-done = bf16[2,32,1024]{2,1,0:T(8,128)(2,1)} async-done(((bf16[2,32,1024]{2,1,0:T(8,128)(2,1)}), bf16[2,32,1024]{2,1,0:T(8,128)(2,1)}) %all-reduce.4.cloned.1.call-update) | async-done | bytes 131088 | tf_op jit(solution)/shard_map/psum | solution.py:133
  (124 shorter events, 12.6 us)
Async XLA Ops:
  7.2 5.9 %copy-start = (bf16[1024,256]{1,0:T(8,128)(2,1)S(1)}, bf16[1024,256]{1,0:T(8,128)(2,1)}, u32[]{:S(2)}) copy-start(bf16[1024,256]{1,0:T(8,128)(2,1)} %param.19) | copy-start | bytes 1572868
  7.2 92.9 %all-reduce.6.cloned.1.call-start = ((), (), s32[]{:S(2)}) async-start(), calls=%async_computation.1 | async-start | bytes 2359296
  8.0 5.1 %copy-start.4 = (bf16[32,1024]{1,0:T(8,128)(2,1)S(1)}, bf16[32,1024]{1,0:T(8,128)(2,1)}, u32[]{:S(2)}) copy-start(bf16[32,1024]{1,0:T(8,128)(2,1)} %param.15) | copy-start | bytes 196612
  8.0 5.3 %copy-start.5 = (bf16[1024,256]{1,0:T(8,128)(2,1)S(1)}, bf16[1024,256]{1,0:T(8,128)(2,1)}, u32[]{:S(2)}) copy-start(bf16[1024,256]{1,0:T(8,128)(2,1)} %param.20) | copy-start | bytes 1572868
  8.0 6.0 %copy-start.1 = (bf16[1024,4096]{1,0:T(8,128)(2,1)S(1)}, bf16[1024,4096]{1,0:T(8,128)(2,1)}, u32[]{:S(2)}) copy-start(bf16[1024,4096]{1,0:T(8,128)(2,1)} %param.18) | copy-start | bytes 25165828
  8.0 6.0 %copy-start.3 = (bf16[32,1024]{1,0:T(8,128)(2,1)S(1)}, bf16[32,1024]{1,0:T(8,128)(2,1)}, u32[]{:S(2)}) copy-start(bf16[32,1024]{1,0:T(8,128)(2,1)} %param.16) | copy-start | bytes 196612
  14.0 3.3 %copy-start.8 = (u32[32]{0:T(128)S(1)}, u32[32]{0:T(128)}, u32[]{:S(2)}) copy-start(u32[32]{0:T(128)} %constant.138) | copy-start | bytes 388
  14.0 28.3 %copy-start.7 = (s32[4]{0:T(128)S(1)}, s32[4]{0:T(128)}, u32[]{:S(2)}) copy-start(s32[4]{0:T(128)} %param.25) | copy-start | bytes 52
  14.0 87.9 %copy-start.6 = (s32[4]{0:T(128)S(1)}, s32[4]{0:T(128)}, u32[]{:S(2)}) copy-start(s32[4]{0:T(128)} %param.24) | copy-start | bytes 52
  15.9 1.1 copy-start.2
  17.0 169.2 %all-reduce.4.cloned.1.call-start = ((), (), s32[]{:S(2)}) async-start(), calls=%async_computation | async-start | bytes 262144 | tf_op jit(solution)/shard_map/psum | solution.py:133
Sparse Core Ops, SparseCore 0:
  17.2 82.9 all-reduce.5
  169.3 16.9 all-reduce.3
where the time goes:
time: 196 us; the launch traced here: 195 us
  waiting for transfers between devices  74.8 us (38%)
  blocking collectives  55.2 us (28%)
  matrix products  39.6 us (20%)
  between operations  15 us (8%)
  other arithmetic  7.16 us (4%)
  local copies, waits for them, and re-layouts  2.49 us (1%)
    unnamed x3, waiting for transfers between devices  57.7 us
    all_gather x1, blocking collectives, combine_output(): lax.all_gather(stacked, 'wide', axis=1, tiled=True)  31.5 us
    psum x1, blocking collectives, reduce_projection(): squares = lax.psum(local_sums, 'wide')  23.6 us
    psum x1, waiting for transfers between devices, combine_output(): total = lax.psum(terms.astype(jnp.bfloat16), 'narrow').astype(jnp.float32)  17.1 us
    dot_general x8, matrix products, advance(): jnp.einsum('rkgd,rktd->rkgt', grouped, block_keys, preferred_element_type...  13.5 us
    dot_general x8, matrix products, advance(): jnp.einsum('rkgt,rktd->rkgd', weight.astype(jnp.bfloat16), block_values,...  12.3 us
    dot_general x2, matrix products, term(): pieces.append(jnp.dot(scaled, w_query, preferred_element_type=jnp.float32))  6.65 us
    dot_general x1, matrix products, combine_output(): jnp.einsum('srk,kd->srd', lax.all_gather(stacked, 'wide', axis=1, tiled=T...  5.75 us
  transfers between devices with their start and end apart: 2, of which 2 were waited for; matrix products, arithmetic and copies ran while one was open for 1% of the time, Pallas kernels for 0%

commit v1 on v0

v1 whole, which is shorter than its diff:
```python
import functools
import math

import jax
import jax.numpy as jnp
from jax import lax
from jax.experimental import pallas as pl
from jax.experimental.pallas import tpu as pltpu
from jax.sharding import PartitionSpec as P

EPSILON = 1e-05
THETA = 500000.0
NEGATIVE = -1e30
LANES = 128
CHUNK = 512
BLOCK = 512
MIB = 1 << 20

F32 = jnp.float32
BF16 = jnp.bfloat16


def one_hot(shape, order_axis, place, order, outer, rows_dev, rows):
    inner = order.shape[0]
    ranked = lax.broadcasted_iota(jnp.int32, shape, order_axis)
    row = lax.broadcasted_iota(jnp.int32, shape, 1 - order_axis)
    request = lax.rem(ranked, rows_dev)
    token = lax.rem(ranked // rows_dev, 2)
    step = ranked // (2 * rows_dev)
    outer_step = lax.rem(step, outer)
    inner_step = step // outer
    offset = jnp.zeros(shape, jnp.int32)
    for index in range(inner):
        offset = jnp.where(inner_step == index, order[index], offset)
    device = jnp.bitwise_xor(place, offset + inner * outer_step)
    source = token * rows + device * rows_dev + request
    return (row == source).astype(BF16)


def project_kernel(
    rows_dev, outer, place, order, first, second, gain, w_query, w_key, w_value, keep, *rest
):
    sends, (chunks, scaled, sems) = rest[:-3], rest[-3:]
    rows, depth = first.shape
    count = chunks.shape[0]
    heads_width = w_query.shape[1]
    kv_width = w_key.shape[1]

    def fetch(index):
        return pltpu.make_async_copy(
            w_query.at[:, pl.ds(index * CHUNK, CHUNK)], chunks.at[index], sems.at[index]
        )

    for index in range(count):
        fetch(index).start()
    block = keep.shape[0]
    pick = one_hot((2 * rows, 2 * rows), 0, place[0], order, outer, rows_dev, rows)
    stacked = jnp.concatenate([first[...], second[...]], axis=0)
    ordered = jnp.dot(pick, stacked, preferred_element_type=F32)
    squares = jnp.sum(ordered * ordered, axis=1, keepdims=True)
    scaled[...] = (ordered * gain[...].astype(F32)).astype(BF16)

    def put(start, width, value):
        keep[:, start : start + width] = value[:block]
        for index, send in enumerate(sends):
            begin = (index + 1) * block
            send[:, start : start + width] = value[begin : begin + block].astype(BF16)

    end = heads_width + 2 * kv_width
    high = squares.astype(BF16).astype(F32)
    lane = lax.broadcasted_iota(jnp.int32, (2 * rows, LANES), 1)
    coded = jnp.where(lax.rem(lane, 2) == 0, high, squares - high)
    keep[:, end : end + LANES] = jnp.broadcast_to(squares[:block], (block, LANES))
    for index, send in enumerate(sends):
        begin = (index + 1) * block
        send[:, end : end + LANES] = coded[begin : begin + block].astype(BF16)
    put(heads_width, kv_width, jnp.dot(scaled[...], w_key[...], preferred_element_type=F32))
    put(
        heads_width + kv_width,
        kv_width,
        jnp.dot(scaled[...], w_value[...], preferred_element_type=F32),
    )
    for index in range(count):
        fetch(index).wait()
        put(
            index * CHUNK,
            CHUNK,
            jnp.dot(scaled[...], chunks[index], preferred_element_type=F32),
        )


def decoded(tail):
    wide = tail.astype(F32)
    return wide + pltpu.roll(wide, 1, 1)


def combine_kernel(parts, outer, keep, *refs):
    received, (mine, *sends) = refs[:parts], refs[parts:]
    width = keep.shape[1] - LANES
    block = keep.shape[0] // outer
    total = keep[:, :width]
    tail = keep[:, width:]
    for part in received:
        total = total + part[:, :width].astype(F32)
        tail = tail + decoded(part[:, width:])
    mine[:, :width] = total[:block]
    mine[:, width:] = tail[:block]
    high = tail.astype(BF16).astype(F32)
    lane = lax.broadcasted_iota(jnp.int32, tail.shape, 1)
    coded = jnp.where(lax.rem(lane, 2) == 0, high, tail - high)
    for index, send in enumerate(sends):
        begin = (index + 1) * block
        send[:, :width] = total[begin : begin + block].astype(BF16)
        send[:, width:] = coded[begin : begin + block].astype(BF16)


def attend_kernel(parts, model_width, lengths, mine, *refs):
    received = refs[:parts]
    cosine, sine, key_cache, value_cache, attended, queries, new_keys, new_values, results = refs[
        parts:
    ]
    rows_dev, kv_heads, max_length, width = key_cache.shape
    heads = queries.shape[0]
    group = heads // kv_heads
    both = mine.shape[0]
    end = mine.shape[1] - LANES
    tail = mine[:, end:]
    for part in received:
        tail = tail + decoded(part[:, end:])
    scale = lax.rsqrt(tail / model_width + EPSILON)

    def head(index):
        columns = slice(index * width, (index + 1) * width)
        value = mine[:, columns]
        for part in received:
            value = value + part[:, columns].astype(F32)
        return value * scale

    def rotate(value):
        return value * cosine[...] + pltpu.roll(value, width // 2, 1) * sine[...]

    for index in range(heads):
        queries[index] = rotate(head(index))
    blank = jnp.zeros((both, width), F32)
    for index in range(kv_heads):
        new_keys[index] = jnp.concatenate([rotate(head(heads + index)), blank], axis=0).astype(BF16)
        new_values[index] = jnp.concatenate(
            [head(heads + kv_heads + index), blank], axis=0
        ).astype(BF16)

    factor = 1.0 / math.sqrt(width)
    contract = (((1,), (1,)), ((), ()))

    def request(row, blocks):
        length = lengths[row]
        span = blocks * BLOCK
        for index in range(kv_heads):
            pick = pl.ds(index * group, group)
            query = jnp.concatenate(
                [queries[pick, row, :], queries[pick, rows_dev + row, :]], axis=0
            ).astype(BF16)
            fresh = (
                lax.dot_general(query, new_keys[index], contract, preferred_element_type=F32)
                * factor
            )
            slot = lax.broadcasted_iota(jnp.int32, fresh.shape, 1)
            token = lax.broadcasted_iota(jnp.int32, fresh.shape, 0) // group
            seen = (
                (lax.rem(slot, rows_dev) == row) & (slot // rows_dev <= token) & (slot < both)
            )
            fresh = jnp.where(seen, fresh, NEGATIVE)
            scores = (
                lax.dot_general(
                    query, key_cache[row, index, :span, :], contract, preferred_element_type=F32
                )
                * factor
            )
            live = lax.broadcasted_iota(jnp.int32, scores.shape, 1) < length
            scores = jnp.where(live, scores, NEGATIVE)
            top = jnp.maximum(
                jnp.max(scores, axis=1, keepdims=True), jnp.max(fresh, axis=1, keepdims=True)
            )
            weight = jnp.exp(scores - top)
            fresh = jnp.exp(fresh - top)
            total = jnp.sum(weight, axis=1, keepdims=True) + jnp.sum(fresh, axis=1, keepdims=True)
            mixed = jnp.dot(
                weight.astype(BF16), value_cache[row, index, :span, :], preferred_element_type=F32
            ) + jnp.dot(fresh.astype(BF16), new_values[index], preferred_element_type=F32)
            mixed = mixed / total
            results[pick, row, :] = mixed[:group]
            results[pick, rows_dev + row, :] = mixed[group:]

    limit = max_length // BLOCK

    @pl.loop(0, rows_dev)
    def _(row):
        needed = pl.cdiv(lengths[row], BLOCK)
        for blocks in range(1, limit + 1):

            @pl.when(needed == blocks)
            def _():
                request(row, blocks)

    for index in range(heads):
        attended[:, index * width : (index + 1) * width] = results[index].astype(BF16)


def output_kernel(rows_dev, outer, place, order, *refs):
    gathered, (w_output, out) = refs[:-2], refs[-2:]
    count = out.shape[0]
    stacked = jnp.concatenate([part[...] for part in gathered], axis=0)
    back = one_hot((count, count), 1, place[0], order, outer, rows_dev, count // 2)
    attended = jnp.dot(back, stacked, preferred_element_type=F32).astype(BF16)
    out[...] = jnp.dot(attended, w_output[...], preferred_element_type=F32)


def whole(space=pltpu.VMEM):
    return pl.BlockSpec(memory_space=space)


def rotary(positions, width):
    half = width // 2
    inverse = jnp.exp(jnp.arange(half, dtype=F32) * (-2.0 * math.log(THETA) / width))
    where_at = jnp.concatenate([positions, positions + 1]).astype(F32)
    angle = where_at[:, None] * inverse
    cosine = jnp.cos(angle)
    sine = jnp.sin(angle)
    return (
        jnp.concatenate([cosine, cosine], axis=1),
        jnp.concatenate([-sine, sine], axis=1),
    )


def on_device(
    first_input,
    second_input,
    norm_gain,
    w_query,
    w_key,
    w_value,
    w_output,
    key_cache,
    value_cache,
    lengths,
    positions,
):
    devices = lax.axis_size("wide")
    cores = lax.axis_size("narrow")
    rows_dev, kv_heads, _, width = key_cache.shape
    rows, depth = first_input.shape
    inner = math.gcd(devices, 4)
    outer = devices // inner
    both = 2 * rows_dev
    block = outer * both
    heads = w_query.shape[1] // width
    columns = w_query.shape[1] + 2 * w_key.shape[1] + LANES

    plans = ([0, 1, 3, 2], [0, 2, 3, 1]) if inner == 4 else (list(range(inner)),) * 2
    gather_plans = ([0, 3, 1, 2], [0, 3, 2, 1]) if inner == 4 else plans
    core = lax.axis_index("narrow")
    place = lax.axis_index("wide").reshape(1).astype(jnp.int32)

    def order_of(plan):
        return jnp.where(core == 0, jnp.array(plan[0], jnp.int32), jnp.array(plan[1], jnp.int32))

    def exchange(value, steps):
        pairs = [
            (place_from * cores + c, (place_from ^ steps[min(c, 1)]) * cores + c)
            for c in range(cores)
            for place_from in range(devices)
        ]
        return lax.ppermute(value, ("wide", "narrow"), pairs)

    order = order_of(plans)
    chunks = w_query.shape[1] // CHUNK
    keep, *sends = pl.pallas_call(
        functools.partial(project_kernel, rows_dev, outer),
        out_shape=[jax.ShapeDtypeStruct((block, columns), F32)]
        + [jax.ShapeDtypeStruct((block, columns), BF16)] * (inner - 1),
        in_specs=[whole(pltpu.SMEM)] * 2
        + [whole()] * 3
        + [whole(pltpu.HBM)]
        + [whole()] * 2,
        out_specs=[whole()] * inner,
        scratch_shapes=[
            pltpu.VMEM((chunks, depth, CHUNK), BF16),
            pltpu.VMEM((2 * rows, depth), BF16),
            pltpu.SemaphoreType.DMA((chunks,)),
        ],
        compiler_params=pltpu.CompilerParams(vmem_limit_bytes=24 * MIB),
        cost_estimate=pl.CostEstimate(
            flops=4 * rows * depth * columns,
            bytes_accessed=2 * depth * columns,
            transcendentals=0,
        ),
        name="project",
    )(place, order, first_input, second_input, norm_gain[None, :], w_query, w_key, w_value)

    received = [
        exchange(send, (plans[0][index + 1], plans[1][index + 1]))
        for index, send in enumerate(sends)
    ]
    mine, *sends = pl.pallas_call(
        functools.partial(combine_kernel, inner - 1, outer),
        out_shape=[jax.ShapeDtypeStruct((both, columns), F32)]
        + [jax.ShapeDtypeStruct((both, columns), BF16)] * (outer - 1),
        in_specs=[whole()] * inner,
        out_specs=[whole()] * outer,
        compiler_params=pltpu.CompilerParams(vmem_limit_bytes=16 * MIB),
        name="combine",
    )(keep, *received)
    received = [
        exchange(send, (inner * (index + 1),) * 2) for index, send in enumerate(sends)
    ]

    cosine, sine = rotary(positions, width)
    attended = pl.pallas_call(
        functools.partial(attend_kernel, outer - 1, devices * depth),
        out_shape=jax.ShapeDtypeStruct((both, heads * width), BF16),
        in_specs=[whole(pltpu.SMEM)] + [whole()] * (outer + 4),
        out_specs=whole(),
        scratch_shapes=[
            pltpu.VMEM((heads, both, width), F32),
            pltpu.VMEM((kv_heads, 2 * both, width), BF16),
            pltpu.VMEM((kv_heads, 2 * both, width), BF16),
            pltpu.VMEM((heads, both, width), F32),
        ],
        compiler_params=pltpu.CompilerParams(vmem_limit_bytes=32 * MIB),
        name="attend",
    )(lengths, mine, *received, cosine, sine, key_cache, value_cache)

    near = jnp.concatenate(
        [attended] + [exchange(attended, (inner * step,) * 2) for step in range(1, outer)], axis=0
    )
    gathered = [near] + [
        exchange(near, (gather_plans[0][index], gather_plans[1][index]))
        for index in range(1, inner)
    ]
    part = pl.pallas_call(
        functools.partial(output_kernel, rows_dev, outer),
        out_shape=jax.ShapeDtypeStruct((2 * rows, w_output.shape[1]), F32),
        in_specs=[whole(pltpu.SMEM)] * 2 + [whole()] * (inner + 1),
        out_specs=whole(),
        compiler_params=pltpu.CompilerParams(vmem_limit_bytes=24 * MIB),
        name="output",
    )(place, order_of(gather_plans), *gathered, w_output)
    total = part + lax.ppermute(part, "narrow", [(c, c ^ 1) for c in range(cores)])
    return (
        (first_input.astype(F32) + total[:rows]).astype(BF16),
        (second_input.astype(F32) + total[rows:]).astype(BF16),
    )


def solution(mesh):
    return jax.shard_map(
        on_device,
        mesh=mesh,
        in_specs=(
            P("groups", "wide"),
            P("groups", "wide"),
            P("wide"),
            P("wide", "narrow"),
            P("wide", "narrow"),
            P("wide", "narrow"),
            P("narrow", "wide"),
            P(("groups", "wide"), "narrow", None, None),
            P(("groups", "wide"), "narrow", None, None),
            P(("groups", "wide")),
            P(("groups", "wide")),
        ),
        out_specs=(P("groups", "wide"), P("groups", "wide")),
        check_vma=False,
    )
```

time: 196 us -> 57.1 us (0.29)
  blocking collectives: 55.2 us -> 0 us
  waiting for transfers between devices: 74.8 us -> 20.9 us
  matrix products: 39.6 us -> 0 us
  between operations: 15 us -> 0.74 us
  starting transfers between devices: 0.08 us -> 12.2 us
  Pallas kernels: 0 us -> 10.9 us
  local copies, waits for them, and re-layouts: 2.49 us -> 10.1 us
  other arithmetic: 7.16 us -> 1.66 us
    unnamed x3 -> x0, waiting for transfers between devices: 57.7 us -> none
    dot_general x26 -> x0, matrix products: 39.6 us -> none  [the longest x8 13.5 us: advance(): jnp.einsum('rkgd,rktd->rkgt', grouped, block_keys, preferred_element_type...]
    all_gather x1 -> x0, blocking collectives: 31.5 us -> none  [combine_output(): lax.all_gather(stacked, 'wide', axis=1, tiled=True)]
    psum x1 -> x0, blocking collectives: 23.6 us -> none  [reduce_projection(): squares = lax.psum(local_sums, 'wide')]
    ppermute x0 -> x9, waiting for transfers between devices: none -> 20.9 us  [the longest x8 19.4 us: exchange(): return lax.ppermute(value, ('wide', 'narrow'), pairs)]
    psum x1 -> x0, waiting for transfers between devices: 17.1 us -> none  [combine_output(): total = lax.psum(terms.astype(jnp.bfloat16), 'narrow').astype(jnp.float32)]
    ppermute x0 -> x9, starting transfers between devices: none -> 12.2 us  [the longest x8 12.2 us: exchange(): return lax.ppermute(value, ('wide', 'narrow'), pairs)]
    pallas_call x0 -> x4, Pallas kernels: none -> 10.9 us  [the longest x1 4.55 us: on_device(): pl.pallas_call(functools.partial(project_kernel, rows_dev, outer), out_sh...]
  transfers between devices with their start and end apart: 2 -> 9, of which waited for: 2 -> 8; matrix products, arithmetic and copies ran while one was open for 1% -> 0% of each run, Pallas kernels for 0% -> 0%
where the time goes in v1:
time: 57.1 us; the launch traced here: 56.5 us
  waiting for transfers between devices  20.9 us (37%)
  starting transfers between devices  12.2 us (21%)
  Pallas kernels  10.9 us (19%)
  local copies, waits for them, and re-layouts  10.1 us (18%)
  other arithmetic  1.66 us (3%)
  between operations  0.74 us (1%)
    ppermute x8, waiting for transfers between devices, exchange(): return lax.ppermute(value, ('wide', 'narrow'), pairs)  19.4 us
    ppermute x8, starting transfers between devices, exchange(): return lax.ppermute(value, ('wide', 'narrow'), pairs)  12.2 us
    unnamed x30, local copies, waits for them, and re-layouts  9.36 us
    pallas_call x1, Pallas kernels, on_device(): pl.pallas_call(functools.partial(project_kernel, rows_dev, outer), out_sh...  4.55 us
    pallas_call x1, Pallas kernels, on_device(): pl.pallas_call(functools.partial(attend_kernel, outer - 1, devices * dept...  3.95 us
    pallas_call x1, Pallas kernels, on_device(): pl.pallas_call(functools.partial(output_kernel, rows_dev, outer), out_sha...  2.29 us
    ppermute x1, waiting for transfers between devices, on_device(): lax.ppermute(part, 'narrow', [(c, c ^ 1) for c in range(cores)])  1.52 us
  transfers between devices with their start and end apart: 9, of which 8 were waited for; matrix products, arithmetic and copies ran while one was open for 0% of the time, Pallas kernels for 0%

profile of v1, /device:TPU:0, one launch (start us, length us, event | category | flops | bytes accessed | tf_op | source)
XLA Modules:
  0.0 56.5 jit_solution(12238121773535037271)
XLA Ops:
  0.7 0.7 %broadcast_in_dim.2.gain = bf16[1,1024]{1,0:T(2,128)(2,1)S(1)} reshape(bf16[1024]{0:T(1024)(128)(2,1)} %param.17) | data formatting | bytes 4096 | tf_op jit(solution)/shard_map/broadcast_in_dim | solution.py:297
  2.0 3.4 %copy-done = bf16[1024,4096]{1,0:T(8,128)(2,1)S(1)} copy-done((bf16[1024,4096]{1,0:T(8,128)(2,1)S(1)}, bf16[1024,4096]{1,0:T(8,128)(2,1)}, u32[]{:S(2)}) %copy-start) | copy-done | bytes 8388632
  5.4 1.0 %copy-done.3 = bf16[1024,256]{1,0:T(8,128)(2,1)S(1)} copy-done((bf16[1024,256]{1,0:T(8,128)(2,1)S(1)}, bf16[1024,256]{1,0:T(8,128)(2,1)}, u32[]{:S(2)}) %copy-start.3) | copy-done | bytes 524312
  6.4 1.0 %copy-done.4 = bf16[1024,256]{1,0:T(8,128)(2,1)S(1)} copy-done((bf16[1024,256]{1,0:T(8,128)(2,1)S(1)}, bf16[1024,256]{1,0:T(8,128)(2,1)}, u32[]{:S(2)}) %copy-start.4) | copy-done | bytes 524312
  7.5 0.8 %copy-done.5 = bf16[32,1024]{1,0:T(8,128)(2,1)S(1)} copy-done((bf16[32,1024]{1,0:T(8,128)(2,1)S(1)}, bf16[32,1024]{1,0:T(8,128)(2,1)}, u32[]{:S(2)}) %copy-start.5) | copy-done | bytes 65560
  8.3 0.8 %copy-done.7 = bf16[32,1024]{1,0:T(8,128)(2,1)S(1)} copy-done((bf16[32,1024]{1,0:T(8,128)(2,1)S(1)}, bf16[32,1024]{1,0:T(8,128)(2,1)}, u32[]{:S(2)}) %copy-start.7) | copy-done | bytes 65560
  9.2 4.5 %project.1 = (f32[16,4736]{1,0:T(8,128)S(1)}, bf16[16,4736]{1,0:T(8,128)(2,1)S(1)}, bf16[16,4736]{1,0:T(8,128)(2,1)S(1)}, bf16[16,4736]{1,0:T(8,128)(2,1)S(1)}) custom-call(s32[1]{0:T(128)} %bitcast.place, s32[4]{0:T(128)S(1)} %broadcast_select_fusion.order, bf16[32,1024]{1,0:T(8,128)(2,1)S(1)} %copy-done.5, bf16[32,1024]{1,0:T(8,128)(2,1)S(1)} %copy-done.7, ...), custom_call_target="tpu_custom_call" | custom-call | flops 620756992 | bytes 9699328 | tf_op jit(solution)/shard_map/project/pallas_call | solution.py:276
  13.7 3.0 %collective-permute-start = (bf16[16,4736]{1,0:T(8,128)(2,1)S(1)}, bf16[16,4736]{1,0:T(8,128)(2,1)S(1)}, u32[]{:S(2)}, u32[]{:S(2)}) collective-permute-start(bf16[16,4736]{1,0:T(8,128)(2,1)S(1)} %get-tuple-element.9), channel_id=1, source_target_pairs={{0,2},{2,0},{4,6},{6,4},{8,10},{10,8},{12,14},{14,12},{1,5},{3,7},... | collective-permute-start | bytes 454664 | tf_op jit(solution)/shard_map/ppermute | solution.py:272
  16.8 1.5 %collective-permute-start.1 = (bf16[16,4736]{1,0:T(8,128)(2,1)S(1)}, bf16[16,4736]{1,0:T(8,128)(2,1)S(1)}, u32[]{:S(2)}, u32[]{:S(2)}) collective-permute-start(bf16[16,4736]{1,0:T(8,128)(2,1)S(1)} %get-tuple-element.10), channel_id=1, source_target_pairs={{0,6},{2,4},{4,2},{6,0},{8,14},{10,12},{12,10},{14,8},{1,7},{3,5},... | collective-permute-start | bytes 454664 | tf_op jit(solution)/shard_map/ppermute | solution.py:272
  18.6 5.6 %collective-permute-done.refs_0_ = bf16[16,4736]{1,0:T(8,128)(2,1)S(1)} collective-permute-done((bf16[16,4736]{1,0:T(8,128)(2,1)S(1)}, bf16[16,4736]{1,0:T(8,128)(2,1)S(1)}, u32[]{:S(2)}, u32[]{:S(2)}) %collective-permute-start) | collective-permute-done | bytes 151584 | tf_op jit(solution)/shard_map/ppermute | solution.py:272
  24.9 2.7 %collective-permute-start.3 = (bf16[8,4736]{1,0:T(8,128)(2,1)S(1)}, bf16[8,4736]{1,0:T(8,128)(2,1)S(1)}, u32[]{:S(2)}, u32[]{:S(2)}) collective-permute-start(bf16[8,4736]{1,0:T(8,128)(2,1)S(1)} %get-tuple-element.13), channel_id=1, source_target_pairs={{0,8},{2,10},{4,12},{6,14},{8,0},{10,2},{12,4},{14,6},{1,9},{3,11}... | collective-permute-start | bytes 227336 | tf_op jit(solution)/shard_map/ppermute | solution.py:272
  27.7 4.3 %collective-permute-done.3.refs_0_ = bf16[8,4736]{1,0:T(8,128)(2,1)S(1)} collective-permute-done((bf16[8,4736]{1,0:T(8,128)(2,1)S(1)}, bf16[8,4736]{1,0:T(8,128)(2,1)S(1)}, u32[]{:S(2)}, u32[]{:S(2)}) %collective-permute-start.3) | collective-permute-done | bytes 75808 | tf_op jit(solution)/shard_map/ppermute | solution.py:272
  32.0 2.2 %copy-done.2 = bf16[4,2,2048,128]{3,2,1,0:T(8,128)(2,1)S(1)} copy-done((bf16[4,2,2048,128]{3,2,1,0:T(8,128)(2,1)S(1)}, bf16[4,2,2048,128]{3,2,1,0:T(8,128)(2,1)}, u32[]{:S(2)}) %copy-start.2) | copy-done | bytes 4194328
  34.2 4.0 %attend.1 = bf16[8,4096]{1,0:T(8,128)(2,1)S(1)} custom-call(s32[4]{0:T(128)S(1)} %copy-done.9, f32[8,4736]{1,0:T(8,128)S(1)} %get-tuple-element.12.mine, bf16[8,4736]{1,0:T(8,128)(2,1)S(1)} %collective-permute-done.3.refs_0_, f32[8,128]{1,0:T(8,128)S(1)} %get-tuple-element.19.refs_1_, f32[8,128]{1,0:T(8,128)S(1)} %get-tuple-element.20.refs_2_, ...), custom_call_target="tpu_custom_call" | custom-call | tf_op jit(solution)/shard_map/attend/pallas_call | solution.py:317
  38.1 1.3 %collective-permute-start.4 = (bf16[8,4096]{1,0:T(8,128)(2,1)S(1)}, bf16[8,4096]{1,0:T(8,128)(2,1)S(1)}, u32[]{:S(2)}, u32[]{:S(2)}) collective-permute-start(bf16[8,4096]{1,0:T(8,128)(2,1)S(1)} %attend.1), channel_id=1, source_target_pairs={{0,8},{2,10},{4,12},{6,14},{8,0},{10,2},{12,4},{14,6},{1,9},{3,11}... | collective-permute-start | bytes 196616 | tf_op jit(solution)/shard_map/ppermute | solution.py:272
  39.4 5.2 %collective-permute-done.4 = bf16[8,4096]{1,0:T(8,128)(2,1)S(1)} collective-permute-done((bf16[8,4096]{1,0:T(8,128)(2,1)S(1)}, bf16[8,4096]{1,0:T(8,128)(2,1)S(1)}, u32[]{:S(2)}, u32[]{:S(2)}) %collective-permute-start.4) | collective-permute-done | bytes 65568 | tf_op jit(solution)/shard_map/ppermute | solution.py:272
  44.6 0.8 %collective-permute-start.5 = (bf16[16,4096]{1,0:T(8,128)(2,1)S(1)}, bf16[16,4096]{1,0:T(8,128)(2,1)S(1)}, u32[]{:S(2)}, u32[]{:S(2)}) collective-permute-start(bf16[16,4096]{1,0:T(8,128)(2,1)S(1)} %pad_maximum_fusion.refs_0_), channel_id=1, source_target_pairs={{0,6},{2,4},{4,2},{6,0},{8,14},{10,12},{12,10},{14,8},{1,7},{3,5},... | collective-permute-start | bytes 393224 | tf_op jit(solution)/shard_map/ppermute | solution.py:272
  45.4 0.7 %collective-permute-start.6 = (bf16[16,4096]{1,0:T(8,128)(2,1)S(1)}, bf16[16,4096]{1,0:T(8,128)(2,1)S(1)}, u32[]{:S(2)}, u32[]{:S(2)}) collective-permute-start(bf16[16,4096]{1,0:T(8,128)(2,1)S(1)} %pad_maximum_fusion.refs_0_), channel_id=1, source_target_pairs={{0,2},{2,0},{4,6},{6,4},{8,10},{10,8},{12,14},{14,12},{1,5},{3,7},... | collective-permute-start | bytes 393224 | tf_op jit(solution)/shard_map/ppermute | solution.py:272
  46.1 2.1 %collective-permute-start.7 = (bf16[16,4096]{1,0:T(8,128)(2,1)S(1)}, bf16[16,4096]{1,0:T(8,128)(2,1)S(1)}, u32[]{:S(2)}, u32[]{:S(2)}) collective-permute-start(bf16[16,4096]{1,0:T(8,128)(2,1)S(1)} %pad_maximum_fusion.refs_0_), channel_id=1, source_target_pairs={{0,4},{2,6},{4,0},{6,2},{8,12},{10,14},{12,8},{14,10},{1,3},{3,1},... | collective-permute-start | bytes 393224 | tf_op jit(solution)/shard_map/ppermute | solution.py:272
  48.2 2.5 %collective-permute-done.5.refs_1_ = bf16[16,4096]{1,0:T(8,128)(2,1)S(1)} collective-permute-done((bf16[16,4096]{1,0:T(8,128)(2,1)S(1)}, bf16[16,4096]{1,0:T(8,128)(2,1)S(1)}, u32[]{:S(2)}, u32[]{:S(2)}) %collective-permute-start.5) | collective-permute-done | bytes 131104 | tf_op jit(solution)/shard_map/ppermute | solution.py:272
  50.7 1.1 %collective-permute-done.6.refs_2_ = bf16[16,4096]{1,0:T(8,128)(2,1)S(1)} collective-permute-done((bf16[16,4096]{1,0:T(8,128)(2,1)S(1)}, bf16[16,4096]{1,0:T(8,128)(2,1)S(1)}, u32[]{:S(2)}, u32[]{:S(2)}) %collective-permute-start.6) | collective-permute-done | bytes 131104 | tf_op jit(solution)/shard_map/ppermute | solution.py:272
  51.9 2.3 %output.1 = f32[64,1024]{1,0:T(8,128)S(1)} custom-call(s32[1]{0:T(128)} %bitcast.place, s32[4]{0:T(128)S(1)} %broadcast_select_fusion.1.order, bf16[16,4096]{1,0:T(8,128)(2,1)S(1)} %pad_maximum_fusion.refs_0_, bf16[16,4096]{1,0:T(8,128)(2,1)S(1)} %collective-permute-done.5.refs_1_, bf16[16,4096]{1,0:T(8,128)(2,1)S(1)} %collective-permute-done.6.refs_2_, ...), custom_call_target="tpu_custom_call" | custom-call | tf_op jit(solution)/shard_map/output/pallas_call | solution.py:339
  54.3 1.5 %collective-permute-done.8 = f32[64,1024]{1,0:T(8,128)S(1)} collective-permute-done((f32[64,1024]{1,0:T(8,128)S(1)}, f32[64,1024]{1,0:T(8,128)S(1)}, u32[]{:S(2)}, u32[]{:S(2)}) %collective-permute-start.8) | collective-permute-done | bytes 262176 | tf_op jit(solution)/shard_map/ppermute | solution.py:347
  55.8 0.7 %fusion = (bf16[32,1024]{1,0:T(8,128)(2,1)}, bf16[32,1024]{1,0:T(8,128)(2,1)}) fusion(f32[64,1024]{1,0:T(8,128)S(1)} %add.13, bf16[32,1024]{1,0:T(8,128)(2,1)S(1)} %copy-done.8, bf16[32,1024]{1,0:T(8,128)(2,1)S(1)} %copy-done.6), kind=kLoop, calls=%fused_computation.1 | loop fusion | flops 196608 | bytes 524288 | tf_op jit(solution)/shard_map/convert_element_type | solution.py:350
  (40 shorter events, 2.0 us)
Async XLA Ops:
  0.6 17.7 %copy-start.12 = (s32[4]{0:T(128)S(1)}, s32[4]{0:T(128)}, u32[]{:S(2)}) copy-start(s32[4]{0:T(128)} %param.25) | copy-start | bytes 52
  0.6 31.3 %copy-start.9 = (s32[4]{0:T(128)S(1)}, s32[4]{0:T(128)}, u32[]{:S(2)}) copy-start(s32[4]{0:T(128)} %lengths.1) | copy-start | bytes 52
  2.0 3.4 %copy-start = (bf16[1024,4096]{1,0:T(8,128)(2,1)S(1)}, bf16[1024,4096]{1,0:T(8,128)(2,1)}, u32[]{:S(2)}) copy-start(bf16[1024,4096]{1,0:T(8,128)(2,1)} %w_query.1) | copy-start | bytes 25165828
  5.4 1.0 %copy-start.3 = (bf16[1024,256]{1,0:T(8,128)(2,1)S(1)}, bf16[1024,256]{1,0:T(8,128)(2,1)}, u32[]{:S(2)}) copy-start(bf16[1024,256]{1,0:T(8,128)(2,1)} %w_key.1) | copy-start | bytes 1572868
  6.4 1.0 %copy-start.4 = (bf16[1024,256]{1,0:T(8,128)(2,1)S(1)}, bf16[1024,256]{1,0:T(8,128)(2,1)}, u32[]{:S(2)}) copy-start(bf16[1024,256]{1,0:T(8,128)(2,1)} %w_value.1) | copy-start | bytes 1572868
  7.5 0.8 %copy-start.5 = (bf16[32,1024]{1,0:T(8,128)(2,1)S(1)}, bf16[32,1024]{1,0:T(8,128)(2,1)}, u32[]{:S(2)}) copy-start(bf16[32,1024]{1,0:T(8,128)(2,1)} %first.1) | copy-start | bytes 196612
  8.3 0.8 %copy-start.7 = (bf16[32,1024]{1,0:T(8,128)(2,1)S(1)}, bf16[32,1024]{1,0:T(8,128)(2,1)}, u32[]{:S(2)}) copy-start(bf16[32,1024]{1,0:T(8,128)(2,1)} %second.1) | copy-start | bytes 196612
  9.2 22.8 %copy-start.1 = (bf16[4,2,2048,128]{3,2,1,0:T(8,128)(2,1)S(1)}, bf16[4,2,2048,128]{3,2,1,0:T(8,128)(2,1)}, u32[]{:S(2)}) copy-start(bf16[4,2,2048,128]{3,2,1,0:T(8,128)(2,1)} %refs_3_.1) | copy-start | bytes 12582916
  9.2 39.0 %copy-start.10 = (s32[4]{0:T(128)S(1)}, s32[4]{0:T(128)}, u32[]{:S(2)}) copy-start(s32[4]{0:T(128)} %constant.24.clone) | copy-start | bytes 52
  9.2 39.0 %copy-start.11 = (s32[4]{0:T(128)S(1)}, s32[4]{0:T(128)}, u32[]{:S(2)}) copy-start(s32[4]{0:T(128)} %constant.25.clone) | copy-start | bytes 52
  9.2 42.7 %slice-start = ((s8[8388608]{0:T(1024)(128)(4,1)}), s8[4194304]{0:T(1024)(128)(4,1)S(1)}, s32[]{:S(2)}) async-start(s8[8388608]{0:T(1024)(128)(4,1)} %bitcast.1), calls=%async_computation | async-start | bytes 8388608
  13.7 10.4 %collective-permute-start = (bf16[16,4736]{1,0:T(8,128)(2,1)S(1)}, bf16[16,4736]{1,0:T(8,128)(2,1)S(1)}, u32[]{:S(2)}, u32[]{:S(2)}) collective-permute-start(bf16[16,4736]{1,0:T(8,128)(2,1)S(1)} %get-tuple-element.9), channel_id=1, source_target_pairs={{0,2},{2,0},{4,6},{6,4},{8,10},{10,8},{12,14},{14,12},{1,5},{3,7},... | collective-permute-start | bytes 454664 | tf_op jit(solution)/shard_map/ppermute | solution.py:272
  16.8 7.4 %collective-permute-start.1 = (bf16[16,4736]{1,0:T(8,128)(2,1)S(1)}, bf16[16,4736]{1,0:T(8,128)(2,1)S(1)}, u32[]{:S(2)}, u32[]{:S(2)}) collective-permute-start(bf16[16,4736]{1,0:T(8,128)(2,1)S(1)} %get-tuple-element.10), channel_id=1, source_target_pairs={{0,6},{2,4},{4,2},{6,0},{8,14},{10,12},{12,10},{14,8},{1,7},{3,5},... | collective-permute-start | bytes 454664 | tf_op jit(solution)/shard_map/ppermute | solution.py:272
  18.3 6.5 %collective-permute-start.2 = (bf16[16,4736]{1,0:T(8,128)(2,1)S(1)}, bf16[16,4736]{1,0:T(8,128)(2,1)S(1)}, u32[]{:S(2)}, u32[]{:S(2)}) collective-permute-start(bf16[16,4736]{1,0:T(8,128)(2,1)S(1)} %get-tuple-element.11), channel_id=1, source_target_pairs={{0,4},{2,6},{4,0},{6,2},{8,12},{10,14},{12,8},{14,10},{1,3},{3,1},... | collective-permute-start | bytes 454664 | tf_op jit(solution)/shard_map/ppermute | solution.py:272
  24.8 27.1 %slice-start.1 = ((s8[8388608]{0:T(1024)(128)(4,1)}), s8[4194304]{0:T(1024)(128)(4,1)S(1)}, s32[]{:S(2)}) async-start(s8[8388608]{0:T(1024)(128)(4,1)} %bitcast.1), calls=%async_computation.1 | async-start | bytes 8388608
  24.9 7.1 %collective-permute-start.3 = (bf16[8,4736]{1,0:T(8,128)(2,1)S(1)}, bf16[8,4736]{1,0:T(8,128)(2,1)S(1)}, u32[]{:S(2)}, u32[]{:S(2)}) collective-permute-start(bf16[8,4736]{1,0:T(8,128)(2,1)S(1)} %get-tuple-element.13), channel_id=1, source_target_pairs={{0,8},{2,10},{4,12},{6,14},{8,0},{10,2},{12,4},{14,6},{1,9},{3,11}... | collective-permute-start | bytes 227336 | tf_op jit(solution)/shard_map/ppermute | solution.py:272
  32.0 2.2 %copy-start.2 = (bf16[4,2,2048,128]{3,2,1,0:T(8,128)(2,1)S(1)}, bf16[4,2,2048,128]{3,2,1,0:T(8,128)(2,1)}, u32[]{:S(2)}) copy-start(bf16[4,2,2048,128]{3,2,1,0:T(8,128)(2,1)} %refs_4_.2) | copy-start | bytes 12582916
  34.2 21.7 %copy-start.6 = (bf16[32,1024]{1,0:T(8,128)(2,1)S(1)}, bf16[32,1024]{1,0:T(8,128)(2,1)}, u32[]{:S(2)}) copy-start(bf16[32,1024]{1,0:T(8,128)(2,1)} %first.1) | copy-start | bytes 196612
  34.2 21.7 %copy-start.8 = (bf16[32,1024]{1,0:T(8,128)(2,1)S(1)}, bf16[32,1024]{1,0:T(8,128)(2,1)}, u32[]{:S(2)}) copy-start(bf16[32,1024]{1,0:T(8,128)(2,1)} %second.1) | copy-start | bytes 196612
  38.1 6.5 %collective-permute-start.4 = (bf16[8,4096]{1,0:T(8,128)(2,1)S(1)}, bf16[8,4096]{1,0:T(8,128)(2,1)S(1)}, u32[]{:S(2)}, u32[]{:S(2)}) collective-permute-start(bf16[8,4096]{1,0:T(8,128)(2,1)S(1)} %attend.1), channel_id=1, source_target_pairs={{0,8},{2,10},{4,12},{6,14},{8,0},{10,2},{12,4},{14,6},{1,9},{3,11}... | collective-permute-start | bytes 196616 | tf_op jit(solution)/shard_map/ppermute | solution.py:272
  44.6 6.0 %collective-permute-start.5 = (bf16[16,4096]{1,0:T(8,128)(2,1)S(1)}, bf16[16,4096]{1,0:T(8,128)(2,1)S(1)}, u32[]{:S(2)}, u32[]{:S(2)}) collective-permute-start(bf16[16,4096]{1,0:T(8,128)(2,1)S(1)} %pad_maximum_fusion.refs_0_), channel_id=1, source_target_pairs={{0,6},{2,4},{4,2},{6,0},{8,14},{10,12},{12,10},{14,8},{1,7},{3,5},... | collective-permute-start | bytes 393224 | tf_op jit(solution)/shard_map/ppermute | solution.py:272
  45.4 6.4 %collective-permute-start.6 = (bf16[16,4096]{1,0:T(8,128)(2,1)S(1)}, bf16[16,4096]{1,0:T(8,128)(2,1)S(1)}, u32[]{:S(2)}, u32[]{:S(2)}) collective-permute-start(bf16[16,4096]{1,0:T(8,128)(2,1)S(1)} %pad_maximum_fusion.refs_0_), channel_id=1, source_target_pairs={{0,2},{2,0},{4,6},{6,4},{8,10},{10,8},{12,14},{14,12},{1,5},{3,7},... | collective-permute-start | bytes 393224 | tf_op jit(solution)/shard_map/ppermute | solution.py:272
  46.1 5.8 %collective-permute-start.7 = (bf16[16,4096]{1,0:T(8,128)(2,1)S(1)}, bf16[16,4096]{1,0:T(8,128)(2,1)S(1)}, u32[]{:S(2)}, u32[]{:S(2)}) collective-permute-start(bf16[16,4096]{1,0:T(8,128)(2,1)S(1)} %pad_maximum_fusion.refs_0_), channel_id=1, source_target_pairs={{0,4},{2,6},{4,0},{6,2},{8,12},{10,14},{12,8},{14,10},{1,3},{3,1},... | collective-permute-start | bytes 393224 | tf_op jit(solution)/shard_map/ppermute | solution.py:272
  54.2 1.6 %collective-permute-start.8 = (f32[64,1024]{1,0:T(8,128)S(1)}, f32[64,1024]{1,0:T(8,128)S(1)}, u32[]{:S(2)}, u32[]{:S(2)}) collective-permute-start(f32[64,1024]{1,0:T(8,128)S(1)} %output.1), channel_id=1, source_target_pairs={{0,1},{1,0},{2,3},{3,2},{4,5},{5,4},{6,7},{7,6},{8,9},{9,8},{10,11... | collective-permute-start | bytes 786440 | tf_op jit(solution)/shard_map/ppermute | solution.py:347

commit v2 on v1

--- a/solution.py
+++ b/solution.py
@@ -20,8 +20,10 @@
 BF16 = jnp.bfloat16
 
 
-def one_hot(shape, order_axis, place, order, outer, rows_dev, rows):
-    inner = order.shape[0]
+def one_hot(shape, order_axis, plans, outer, rows_dev, rows):
+    inner = len(plans[0])
+    place = lax.axis_index("wide")
+    core = lax.axis_index("narrow")
     ranked = lax.broadcasted_iota(jnp.int32, shape, order_axis)
     row = lax.broadcasted_iota(jnp.int32, shape, 1 - order_axis)
     request = lax.rem(ranked, rows_dev)
@@ -31,34 +33,45 @@
     inner_step = step // outer
     offset = jnp.zeros(shape, jnp.int32)
     for index in range(inner):
-        offset = jnp.where(inner_step == index, order[index], offset)
+        own = jnp.where(core == 0, plans[0][index], plans[1][index])
+        offset = jnp.where(inner_step == index, own, offset)
     device = jnp.bitwise_xor(place, offset + inner * outer_step)
     source = token * rows + device * rows_dev + request
     return (row == source).astype(BF16)
 
 
 def project_kernel(
-    rows_dev, outer, place, order, first, second, gain, w_query, w_key, w_value, keep, *rest
+    rows_dev, outer, plans, first, second, gain, w_query, w_key, w_value, keep, *rest
 ):
-    sends, (chunks, scaled, sems) = rest[:-3], rest[-3:]
+    sends, (chunks, key_part, value_part, tokens, gains, scaled, sems) = rest[:-7], rest[-7:]
     rows, depth = first.shape
     count = chunks.shape[0]
     heads_width = w_query.shape[1]
     kv_width = w_key.shape[1]
 
-    def fetch(index):
-        return pltpu.make_async_copy(
-            w_query.at[:, pl.ds(index * CHUNK, CHUNK)], chunks.at[index], sems.at[index]
-        )
-
-    for index in range(count):
-        fetch(index).start()
+    copies = [
+        (first, tokens.at[:rows]),
+        (second, tokens.at[rows:]),
+        (gain, gains),
+        (w_key, key_part),
+        (w_value, value_part),
+    ] + [
+        (w_query.at[:, index * CHUNK : (index + 1) * CHUNK], chunks.at[index])
+        for index in range(count)
+    ]
+    copies = [
+        pltpu.make_async_copy(source, target, sems.at[index])
+        for index, (source, target) in enumerate(copies)
+    ]
+    for copy in copies:
+        copy.start()
+    for copy in copies[:3]:
+        copy.wait()
     block = keep.shape[0]
-    pick = one_hot((2 * rows, 2 * rows), 0, place[0], order, outer, rows_dev, rows)
-    stacked = jnp.concatenate([first[...], second[...]], axis=0)
-    ordered = jnp.dot(pick, stacked, preferred_element_type=F32)
+    pick = one_hot((2 * rows, 2 * rows), 0, plans, outer, rows_dev, rows)
+    ordered = jnp.dot(pick, tokens[...], preferred_element_type=F32)
     squares = jnp.sum(ordered * ordered, axis=1, keepdims=True)
-    scaled[...] = (ordered * gain[...].astype(F32)).astype(BF16)
+    scaled[...] = (ordered * gains[...].astype(F32)[None, :]).astype(BF16)
 
     def put(start, width, value):
         keep[:, start : start + width] = value[:block]
@@ -74,14 +87,15 @@
     for index, send in enumerate(sends):
         begin = (index + 1) * block
         send[:, end : end + LANES] = coded[begin : begin + block].astype(BF16)
-    put(heads_width, kv_width, jnp.dot(scaled[...], w_key[...], preferred_element_type=F32))
-    put(
-        heads_width + kv_width,
-        kv_width,
-        jnp.dot(scaled[...], w_value[...], preferred_element_type=F32),
-    )
+    for index, part in enumerate((key_part, value_part)):
+        copies[3 + index].wait()
+        put(
+            heads_width + index * kv_width,
+            kv_width,
+            jnp.dot(scaled[...], part[...], preferred_element_type=F32),
+        )
     for index in range(count):
-        fetch(index).wait()
+        copies[5 + index].wait()
         put(
             index * CHUNK,
             CHUNK,
@@ -205,11 +219,11 @@
         attended[:, index * width : (index + 1) * width] = results[index].astype(BF16)
 
 
-def output_kernel(rows_dev, outer, place, order, *refs):
+def output_kernel(rows_dev, outer, plans, *refs):
     gathered, (w_output, out) = refs[:-2], refs[-2:]
     count = out.shape[0]
     stacked = jnp.concatenate([part[...] for part in gathered], axis=0)
-    back = one_hot((count, count), 1, place[0], order, outer, rows_dev, count // 2)
+    back = one_hot((count, count), 1, plans, outer, rows_dev, count // 2)
     attended = jnp.dot(back, stacked, preferred_element_type=F32).astype(BF16)
     out[...] = jnp.dot(attended, w_output[...], preferred_element_type=F32)
 
@@ -257,12 +271,6 @@
 
     plans = ([0, 1, 3, 2], [0, 2, 3, 1]) if inner == 4 else (list(range(inner)),) * 2
     gather_plans = ([0, 3, 1, 2], [0, 3, 2, 1]) if inner == 4 else plans
-    core = lax.axis_index("narrow")
-    place = lax.axis_index("wide").reshape(1).astype(jnp.int32)
-
-    def order_of(plan):
-        return jnp.where(core == 0, jnp.array(plan[0], jnp.int32), jnp.array(plan[1], jnp.int32))
-
     def exchange(value, steps):
         pairs = [
             (place_from * cores + c, (place_from ^ steps[min(c, 1)]) * cores + c)
@@ -271,21 +279,24 @@
         ]
         return lax.ppermute(value, ("wide", "narrow"), pairs)
 
-    order = order_of(plans)
+    def placed(space, *values):
+        return [pltpu.with_memory_space_constraint(value, space) for value in values]
+
     chunks = w_query.shape[1] // CHUNK
     keep, *sends = pl.pallas_call(
-        functools.partial(project_kernel, rows_dev, outer),
+        functools.partial(project_kernel, rows_dev, outer, plans),
         out_shape=[jax.ShapeDtypeStruct((block, columns), F32)]
         + [jax.ShapeDtypeStruct((block, columns), BF16)] * (inner - 1),
-        in_specs=[whole(pltpu.SMEM)] * 2
-        + [whole()] * 3
-        + [whole(pltpu.HBM)]
-        + [whole()] * 2,
+        in_specs=[whole(pltpu.HBM)] * 6,
         out_specs=[whole()] * inner,
         scratch_shapes=[
             pltpu.VMEM((chunks, depth, CHUNK), BF16),
+            pltpu.VMEM(w_key.shape, BF16),
+            pltpu.VMEM(w_value.shape, BF16),
             pltpu.VMEM((2 * rows, depth), BF16),
-            pltpu.SemaphoreType.DMA((chunks,)),
+            pltpu.VMEM((depth,), BF16),
+            pltpu.VMEM((2 * rows, depth), BF16),
+            pltpu.SemaphoreType.DMA((chunks + 5,)),
         ],
         compiler_params=pltpu.CompilerParams(vmem_limit_bytes=24 * MIB),
         cost_estimate=pl.CostEstimate(
@@ -294,7 +305,7 @@
             transcendentals=0,
         ),
         name="project",
-    )(place, order, first_input, second_input, norm_gain[None, :], w_query, w_key, w_value)
+    )(*placed(pltpu.HBM, first_input, second_input, norm_gain, w_query, w_key, w_value))
 
     received = [
         exchange(send, (plans[0][index + 1], plans[1][index + 1]))
@@ -327,7 +338,7 @@
         ],
         compiler_params=pltpu.CompilerParams(vmem_limit_bytes=32 * MIB),
         name="attend",
-    )(lengths, mine, *received, cosine, sine, key_cache, value_cache)
+    )(lengths, mine, *received, cosine, sine, *placed(pltpu.VMEM, key_cache, value_cache))
 
     near = jnp.concatenate(
         [attended] + [exchange(attended, (inner * step,) * 2) for step in range(1, outer)], axis=0
@@ -337,13 +348,13 @@
         for index in range(1, inner)
     ]
     part = pl.pallas_call(
-        functools.partial(output_kernel, rows_dev, outer),
+        functools.partial(output_kernel, rows_dev, outer, gather_plans),
         out_shape=jax.ShapeDtypeStruct((2 * rows, w_output.shape[1]), F32),
-        in_specs=[whole(pltpu.SMEM)] * 2 + [whole()] * (inner + 1),
+        in_specs=[whole()] * (inner + 1),
         out_specs=whole(),
         compiler_params=pltpu.CompilerParams(vmem_limit_bytes=24 * MIB),
         name="output",
-    )(place, order_of(gather_plans), *gathered, w_output)
+    )(*gathered, *placed(pltpu.VMEM, w_output))
     total = part + lax.ppermute(part, "narrow", [(c, c ^ 1) for c in range(cores)])
     return (
         (first_input.astype(F32) + total[:rows]).astype(BF16),

time: 57.1 us -> 45.6 us (0.80)
  local copies, waits for them, and re-layouts: 10.1 us -> 0.04 us
  other arithmetic: 1.66 us -> 1 us
    unnamed x30 -> x16, local copies, waits for them, and re-layouts: 9.36 us -> 0.04 us
    broadcast_in_dim x1 -> x0, local copies, waits for them, and re-layouts: 0.69 us -> none  [on_device(): norm_gain[None, :]]
    pallas_call x2, Pallas kernels: 6.84 us -> 6.15 us  [the longest x1 4.4 us: on_device(): pl.pallas_call(functools.partial(project_kernel, rows_dev, outer, plans),...]
    select_n x2 -> x0, other arithmetic: 0.66 us -> none  [order_of(): jnp.where(core == 0, jnp.array(plan[0], jnp.int32), jnp.array(plan[1], jn...]
  transfers between devices with their start and end apart: 9 -> 9, of which waited for: 8 -> 8; matrix products, arithmetic and copies ran while one was open for 0% -> 1% of each run, Pallas kernels for 0% -> 0%
where the time goes in v2:
time: 45.6 us; the launch traced here: 45.4 us
  waiting for transfers between devices  20.9 us (46%)
  starting transfers between devices  12.2 us (27%)
  Pallas kernels  10.4 us (23%)
  other arithmetic  1 us (2%)
  between operations  0.76 us (2%)
    ppermute x8, waiting for transfers between devices, exchange(): return lax.ppermute(value, ('wide', 'narrow'), pairs)  19.4 us
    ppermute x8, starting transfers between devices, exchange(): return lax.ppermute(value, ('wide', 'narrow'), pairs)  12.1 us
    pallas_call x1, Pallas kernels, on_device(): pl.pallas_call(functools.partial(project_kernel, rows_dev, outer, plans),...  4.4 us
    pallas_call x1, Pallas kernels, on_device(): pl.pallas_call(functools.partial(attend_kernel, outer - 1, devices * dept...  4.18 us
    pallas_call x1, Pallas kernels, on_device(): pl.pallas_call(functools.partial(output_kernel, rows_dev, outer, gather_p...  1.75 us
    ppermute x1, waiting for transfers between devices, on_device(): lax.ppermute(part, 'narrow', [(c, c ^ 1) for c in range(cores)])  1.52 us
  transfers between devices with their start and end apart: 9, of which 8 were waited for; matrix products, arithmetic and copies ran while one was open for 1% of the time, Pallas kernels for 0%

profile of v2, /device:TPU:0, one launch (start us, length us, event | category | flops | bytes accessed | tf_op | source)
XLA Modules:
  0.0 45.4 jit_solution(12184419008620363889)
XLA Ops:
  0.7 4.4 %project.1 = (f32[16,4736]{1,0:T(8,128)S(1)}, bf16[16,4736]{1,0:T(8,128)(2,1)S(1)}, bf16[16,4736]{1,0:T(8,128)(2,1)S(1)}, bf16[16,4736]{1,0:T(8,128)(2,1)S(1)}) custom-call(bf16[32,1024]{1,0:T(8,128)(2,1)} %first.1, bf16[32,1024]{1,0:T(8,128)(2,1)} %second.1, bf16[1024]{0:T(1024)(128)(2,1)} %gain.1, bf16[1024,4096]{1,0:T(8,128)(2,1)} %w_query.1, ...), custom_call_target="tpu_custom_call" | custom-call | flops 620756992 | bytes 9699328 | tf_op jit(solution)/shard_map/project/pallas_call | solution.py:286
  5.1 3.0 %collective-permute-start = (bf16[16,4736]{1,0:T(8,128)(2,1)S(1)}, bf16[16,4736]{1,0:T(8,128)(2,1)S(1)}, u32[]{:S(2)}, u32[]{:S(2)}) collective-permute-start(bf16[16,4736]{1,0:T(8,128)(2,1)S(1)} %get-tuple-element.9), channel_id=1, source_target_pairs={{0,2},{2,0},{4,6},{6,4},{8,10},{10,8},{12,14},{14,12},{1,5},{3,7},... | collective-permute-start | bytes 454664 | tf_op jit(solution)/shard_map/ppermute | solution.py:280
  8.1 1.5 %collective-permute-start.1 = (bf16[16,4736]{1,0:T(8,128)(2,1)S(1)}, bf16[16,4736]{1,0:T(8,128)(2,1)S(1)}, u32[]{:S(2)}, u32[]{:S(2)}) collective-permute-start(bf16[16,4736]{1,0:T(8,128)(2,1)S(1)} %get-tuple-element.10), channel_id=1, source_target_pairs={{0,6},{2,4},{4,2},{6,0},{8,14},{10,12},{12,10},{14,8},{1,7},{3,5},... | collective-permute-start | bytes 454664 | tf_op jit(solution)/shard_map/ppermute | solution.py:280
  9.7 0.1 add_convert_fusion
  9.8 0.1 fusion.2
  9.9 5.6 %collective-permute-done.refs_0_ = bf16[16,4736]{1,0:T(8,128)(2,1)S(1)} collective-permute-done((bf16[16,4736]{1,0:T(8,128)(2,1)S(1)}, bf16[16,4736]{1,0:T(8,128)(2,1)S(1)}, u32[]{:S(2)}, u32[]{:S(2)}) %collective-permute-start) | collective-permute-done | bytes 151584 | tf_op jit(solution)/shard_map/ppermute | solution.py:280
  15.5 0.6 %collective-permute-done.2.refs_2_ = bf16[16,4736]{1,0:T(8,128)(2,1)S(1)} collective-permute-done((bf16[16,4736]{1,0:T(8,128)(2,1)S(1)}, bf16[16,4736]{1,0:T(8,128)(2,1)S(1)}, u32[]{:S(2)}, u32[]{:S(2)}) %collective-permute-start.2) | collective-permute-done | bytes 151584 | tf_op jit(solution)/shard_map/ppermute | solution.py:280
  16.2 0.1 combine.1
  16.3 2.7 %collective-permute-start.3 = (bf16[8,4736]{1,0:T(8,128)(2,1)S(1)}, bf16[8,4736]{1,0:T(8,128)(2,1)S(1)}, u32[]{:S(2)}, u32[]{:S(2)}) collective-permute-start(bf16[8,4736]{1,0:T(8,128)(2,1)S(1)} %get-tuple-element.13), channel_id=1, source_target_pairs={{0,8},{2,10},{4,12},{6,14},{8,0},{10,2},{12,4},{14,6},{1,9},{3,11}... | collective-permute-start | bytes 227336 | tf_op jit(solution)/shard_map/ppermute | solution.py:280
  19.0 0.1 pad_maximum_fusion.1
  19.0 4.3 %collective-permute-done.3.refs_0_ = bf16[8,4736]{1,0:T(8,128)(2,1)S(1)} collective-permute-done((bf16[8,4736]{1,0:T(8,128)(2,1)S(1)}, bf16[8,4736]{1,0:T(8,128)(2,1)S(1)}, u32[]{:S(2)}, u32[]{:S(2)}) %collective-permute-start.3) | collective-permute-done | bytes 75808 | tf_op jit(solution)/shard_map/ppermute | solution.py:280
  23.4 4.2 %attend.1 = bf16[8,4096]{1,0:T(8,128)(2,1)S(1)} custom-call(s32[4]{0:T(128)S(1)} %copy-done.2, f32[8,4736]{1,0:T(8,128)S(1)} %get-tuple-element.12.mine, bf16[8,4736]{1,0:T(8,128)(2,1)S(1)} %collective-permute-done.3.refs_0_, f32[8,128]{1,0:T(8,128)S(1)} %get-tuple-element.19.refs_1_, f32[8,128]{1,0:T(8,128)S(1)} %get-tuple-element.20.refs_2_, ...), custom_call_target="tpu_custom_call" | custom-call | tf_op jit(solution)/shard_map/attend/pallas_call | solution.py:328
  27.6 1.3 %collective-permute-start.4 = (bf16[8,4096]{1,0:T(8,128)(2,1)S(1)}, bf16[8,4096]{1,0:T(8,128)(2,1)S(1)}, u32[]{:S(2)}, u32[]{:S(2)}) collective-permute-start(bf16[8,4096]{1,0:T(8,128)(2,1)S(1)} %attend.1), channel_id=1, source_target_pairs={{0,8},{2,10},{4,12},{6,14},{8,0},{10,2},{12,4},{14,6},{1,9},{3,11}... | collective-permute-start | bytes 196616 | tf_op jit(solution)/shard_map/ppermute | solution.py:280
  28.9 5.0 %collective-permute-done.4 = bf16[8,4096]{1,0:T(8,128)(2,1)S(1)} collective-permute-done((bf16[8,4096]{1,0:T(8,128)(2,1)S(1)}, bf16[8,4096]{1,0:T(8,128)(2,1)S(1)}, u32[]{:S(2)}, u32[]{:S(2)}) %collective-permute-start.4) | collective-permute-done | bytes 65568 | tf_op jit(solution)/shard_map/ppermute | solution.py:280
  33.8 1.0 %collective-permute-start.5 = (bf16[16,4096]{1,0:T(8,128)(2,1)S(1)}, bf16[16,4096]{1,0:T(8,128)(2,1)S(1)}, u32[]{:S(2)}, u32[]{:S(2)}) collective-permute-start(bf16[16,4096]{1,0:T(8,128)(2,1)S(1)} %pad_maximum_fusion.refs_0_), channel_id=1, source_target_pairs={{0,6},{2,4},{4,2},{6,0},{8,14},{10,12},{12,10},{14,8},{1,7},{3,5},... | collective-permute-start | bytes 393224 | tf_op jit(solution)/shard_map/ppermute | solution.py:280
  34.8 0.7 %collective-permute-start.6 = (bf16[16,4096]{1,0:T(8,128)(2,1)S(1)}, bf16[16,4096]{1,0:T(8,128)(2,1)S(1)}, u32[]{:S(2)}, u32[]{:S(2)}) collective-permute-start(bf16[16,4096]{1,0:T(8,128)(2,1)S(1)} %pad_maximum_fusion.refs_0_), channel_id=1, source_target_pairs={{0,2},{2,0},{4,6},{6,4},{8,10},{10,8},{12,14},{14,12},{1,5},{3,7},... | collective-permute-start | bytes 393224 | tf_op jit(solution)/shard_map/ppermute | solution.py:280
  35.5 1.8 %collective-permute-start.7 = (bf16[16,4096]{1,0:T(8,128)(2,1)S(1)}, bf16[16,4096]{1,0:T(8,128)(2,1)S(1)}, u32[]{:S(2)}, u32[]{:S(2)}) collective-permute-start(bf16[16,4096]{1,0:T(8,128)(2,1)S(1)} %pad_maximum_fusion.refs_0_), channel_id=1, source_target_pairs={{0,4},{2,6},{4,0},{6,2},{8,12},{10,14},{12,8},{14,10},{1,3},{3,1},... | collective-permute-start | bytes 393224 | tf_op jit(solution)/shard_map/ppermute | solution.py:280
  37.4 2.5 %collective-permute-done.5.refs_1_ = bf16[16,4096]{1,0:T(8,128)(2,1)S(1)} collective-permute-done((bf16[16,4096]{1,0:T(8,128)(2,1)S(1)}, bf16[16,4096]{1,0:T(8,128)(2,1)S(1)}, u32[]{:S(2)}, u32[]{:S(2)}) %collective-permute-start.5) | collective-permute-done | bytes 131104 | tf_op jit(solution)/shard_map/ppermute | solution.py:280
  39.9 1.3 %collective-permute-done.6.refs_2_ = bf16[16,4096]{1,0:T(8,128)(2,1)S(1)} collective-permute-done((bf16[16,4096]{1,0:T(8,128)(2,1)S(1)}, bf16[16,4096]{1,0:T(8,128)(2,1)S(1)}, u32[]{:S(2)}, u32[]{:S(2)}) %collective-permute-start.6) | collective-permute-done | bytes 131104 | tf_op jit(solution)/shard_map/ppermute | solution.py:280
  41.2 0.1 collective-permute-done.7.refs_3_
  41.3 1.8 %output.1 = f32[64,1024]{1,0:T(8,128)S(1)} custom-call(bf16[16,4096]{1,0:T(8,128)(2,1)S(1)} %pad_maximum_fusion.refs_0_, bf16[16,4096]{1,0:T(8,128)(2,1)S(1)} %collective-permute-done.5.refs_1_, bf16[16,4096]{1,0:T(8,128)(2,1)S(1)} %collective-permute-done.6.refs_2_, bf16[16,4096]{1,0:T(8,128)(2,1)S(1)} %collective-permute-done.7.refs_3_, ...), custom_call_target="tpu_custom_call" | custom-call | tf_op jit(solution)/shard_map/output/pallas_call | solution.py:350
  43.1 0.1 collective-permute-start.8
  43.1 1.5 %collective-permute-done.8 = f32[64,1024]{1,0:T(8,128)S(1)} collective-permute-done((f32[64,1024]{1,0:T(8,128)S(1)}, f32[64,1024]{1,0:T(8,128)S(1)}, u32[]{:S(2)}, u32[]{:S(2)}) %collective-permute-start.8) | collective-permute-done | bytes 262176 | tf_op jit(solution)/shard_map/ppermute | solution.py:358
  44.7 0.7 %fusion = (bf16[32,1024]{1,0:T(8,128)(2,1)}, bf16[32,1024]{1,0:T(8,128)(2,1)}) fusion(f32[64,1024]{1,0:T(8,128)S(1)} %add.13, bf16[32,1024]{1,0:T(8,128)(2,1)S(1)} %copy-done.4, bf16[32,1024]{1,0:T(8,128)(2,1)S(1)} %copy-done.3), kind=kLoop, calls=%fused_computation.1 | loop fusion | flops 196608 | bytes 524288 | tf_op jit(solution)/shard_map/convert_element_type | solution.py:361
  (23 shorter events, 0.2 us)
Async XLA Ops:
  0.6 9.1 %copy-start.5 = (s32[4]{0:T(128)S(1)}, s32[4]{0:T(128)}, u32[]{:S(2)}) copy-start(s32[4]{0:T(128)} %param.21) | copy-start | bytes 52
  0.6 22.7 %copy-start = (bf16[4,2,2048,128]{3,2,1,0:T(8,128)(2,1)S(1)}, bf16[4,2,2048,128]{3,2,1,0:T(8,128)(2,1)}, u32[]{:S(2)}) copy-start(bf16[4,2,2048,128]{3,2,1,0:T(8,128)(2,1)} %refs_3_.1) | copy-start | bytes 12582916
  0.7 22.7 %copy-start.1 = (bf16[4,2,2048,128]{3,2,1,0:T(8,128)(2,1)S(1)}, bf16[4,2,2048,128]{3,2,1,0:T(8,128)(2,1)}, u32[]{:S(2)}) copy-start(bf16[4,2,2048,128]{3,2,1,0:T(8,128)(2,1)} %refs_4_.2) | copy-start | bytes 12582916
  0.7 22.7 %copy-start.2 = (s32[4]{0:T(128)S(1)}, s32[4]{0:T(128)}, u32[]{:S(2)}) copy-start(s32[4]{0:T(128)} %lengths.1) | copy-start | bytes 52
  0.7 40.6 %slice-start = ((s8[8388608]{0:T(1024)(128)(4,1)}), s8[4194304]{0:T(1024)(128)(4,1)S(1)}, s32[]{:S(2)}) async-start(s8[8388608]{0:T(1024)(128)(4,1)} %bitcast), calls=%async_computation | async-start | bytes 8388608
  5.1 10.4 %collective-permute-start = (bf16[16,4736]{1,0:T(8,128)(2,1)S(1)}, bf16[16,4736]{1,0:T(8,128)(2,1)S(1)}, u32[]{:S(2)}, u32[]{:S(2)}) collective-permute-start(bf16[16,4736]{1,0:T(8,128)(2,1)S(1)} %get-tuple-element.9), channel_id=1, source_target_pairs={{0,2},{2,0},{4,6},{6,4},{8,10},{10,8},{12,14},{14,12},{1,5},{3,7},... | collective-permute-start | bytes 454664 | tf_op jit(solution)/shard_map/ppermute | solution.py:280
  8.1 7.4 %collective-permute-start.1 = (bf16[16,4736]{1,0:T(8,128)(2,1)S(1)}, bf16[16,4736]{1,0:T(8,128)(2,1)S(1)}, u32[]{:S(2)}, u32[]{:S(2)}) collective-permute-start(bf16[16,4736]{1,0:T(8,128)(2,1)S(1)} %get-tuple-element.10), channel_id=1, source_target_pairs={{0,6},{2,4},{4,2},{6,0},{8,14},{10,12},{12,10},{14,8},{1,7},{3,5},... | collective-permute-start | bytes 454664 | tf_op jit(solution)/shard_map/ppermute | solution.py:280
  9.6 6.5 %collective-permute-start.2 = (bf16[16,4736]{1,0:T(8,128)(2,1)S(1)}, bf16[16,4736]{1,0:T(8,128)(2,1)S(1)}, u32[]{:S(2)}, u32[]{:S(2)}) collective-permute-start(bf16[16,4736]{1,0:T(8,128)(2,1)S(1)} %get-tuple-element.11), channel_id=1, source_target_pairs={{0,4},{2,6},{4,0},{6,2},{8,12},{10,14},{12,8},{14,10},{1,3},{3,1},... | collective-permute-start | bytes 454664 | tf_op jit(solution)/shard_map/ppermute | solution.py:280
  16.2 25.1 %slice-start.1 = ((s8[8388608]{0:T(1024)(128)(4,1)}), s8[4194304]{0:T(1024)(128)(4,1)S(1)}, s32[]{:S(2)}) async-start(s8[8388608]{0:T(1024)(128)(4,1)} %bitcast), calls=%async_computation.1 | async-start | bytes 8388608
  16.3 7.1 %collective-permute-start.3 = (bf16[8,4736]{1,0:T(8,128)(2,1)S(1)}, bf16[8,4736]{1,0:T(8,128)(2,1)S(1)}, u32[]{:S(2)}, u32[]{:S(2)}) collective-permute-start(bf16[8,4736]{1,0:T(8,128)(2,1)S(1)} %get-tuple-element.13), channel_id=1, source_target_pairs={{0,8},{2,10},{4,12},{6,14},{8,0},{10,2},{12,4},{14,6},{1,9},{3,11}... | collective-permute-start | bytes 227336 | tf_op jit(solution)/shard_map/ppermute | solution.py:280
  23.4 21.3 %copy-start.3 = (bf16[32,1024]{1,0:T(8,128)(2,1)S(1)}, bf16[32,1024]{1,0:T(8,128)(2,1)}, u32[]{:S(2)}) copy-start(bf16[32,1024]{1,0:T(8,128)(2,1)} %first.1) | copy-start | bytes 196612
  23.4 21.3 %copy-start.4 = (bf16[32,1024]{1,0:T(8,128)(2,1)S(1)}, bf16[32,1024]{1,0:T(8,128)(2,1)}, u32[]{:S(2)}) copy-start(bf16[32,1024]{1,0:T(8,128)(2,1)} %second.1) | copy-start | bytes 196612
  27.6 6.2 %collective-permute-start.4 = (bf16[8,4096]{1,0:T(8,128)(2,1)S(1)}, bf16[8,4096]{1,0:T(8,128)(2,1)S(1)}, u32[]{:S(2)}, u32[]{:S(2)}) collective-permute-start(bf16[8,4096]{1,0:T(8,128)(2,1)S(1)} %attend.1), channel_id=1, source_target_pairs={{0,8},{2,10},{4,12},{6,14},{8,0},{10,2},{12,4},{14,6},{1,9},{3,11}... | collective-permute-start | bytes 196616 | tf_op jit(solution)/shard_map/ppermute | solution.py:280
  33.8 6.0 %collective-permute-start.5 = (bf16[16,4096]{1,0:T(8,128)(2,1)S(1)}, bf16[16,4096]{1,0:T(8,128)(2,1)S(1)}, u32[]{:S(2)}, u32[]{:S(2)}) collective-permute-start(bf16[16,4096]{1,0:T(8,128)(2,1)S(1)} %pad_maximum_fusion.refs_0_), channel_id=1, source_target_pairs={{0,6},{2,4},{4,2},{6,0},{8,14},{10,12},{12,10},{14,8},{1,7},{3,5},... | collective-permute-start | bytes 393224 | tf_op jit(solution)/shard_map/ppermute | solution.py:280
  34.8 6.3 %collective-permute-start.6 = (bf16[16,4096]{1,0:T(8,128)(2,1)S(1)}, bf16[16,4096]{1,0:T(8,128)(2,1)S(1)}, u32[]{:S(2)}, u32[]{:S(2)}) collective-permute-start(bf16[16,4096]{1,0:T(8,128)(2,1)S(1)} %pad_maximum_fusion.refs_0_), channel_id=1, source_target_pairs={{0,2},{2,0},{4,6},{6,4},{8,10},{10,8},{12,14},{14,12},{1,5},{3,7},... | collective-permute-start | bytes 393224 | tf_op jit(solution)/shard_map/ppermute | solution.py:280
  35.5 5.8 %collective-permute-start.7 = (bf16[16,4096]{1,0:T(8,128)(2,1)S(1)}, bf16[16,4096]{1,0:T(8,128)(2,1)S(1)}, u32[]{:S(2)}, u32[]{:S(2)}) collective-permute-start(bf16[16,4096]{1,0:T(8,128)(2,1)S(1)} %pad_maximum_fusion.refs_0_), channel_id=1, source_target_pairs={{0,4},{2,6},{4,0},{6,2},{8,12},{10,14},{12,8},{14,10},{1,3},{3,1},... | collective-permute-start | bytes 393224 | tf_op jit(solution)/shard_map/ppermute | solution.py:280
  43.1 1.6 %collective-permute-start.8 = (f32[64,1024]{1,0:T(8,128)S(1)}, f32[64,1024]{1,0:T(8,128)S(1)}, u32[]{:S(2)}, u32[]{:S(2)}) collective-permute-start(f32[64,1024]{1,0:T(8,128)S(1)} %output.1), channel_id=1, source_target_pairs={{0,1},{1,0},{2,3},{3,2},{4,5},{5,4},{6,7},{7,6},{8,9},{9,8},{10,11... | collective-permute-start | bytes 786440 | tf_op jit(solution)/shard_map/ppermute | solution.py:358

commit v3 on v2

v3 whole, which is shorter than its diff:
```python
import functools
import math

import jax
import jax.numpy as jnp
from jax import lax
from jax.experimental import pallas as pl
from jax.experimental.pallas import tpu as pltpu
from jax.sharding import PartitionSpec as P

EPSILON = 1e-05
THETA = 500000.0
NEGATIVE = -1e30
LANES = 128
CHUNK = 512
MIB = 1 << 20

F32 = jnp.float32
BF16 = jnp.bfloat16


def one_hot(shape, order_axis, plans, outer, rows_dev, rows):
    inner = len(plans[0])
    place = lax.axis_index("wide")
    core = lax.axis_index("narrow")
    ranked = lax.broadcasted_iota(jnp.int32, shape, order_axis)
    row = lax.broadcasted_iota(jnp.int32, shape, 1 - order_axis)
    request = lax.rem(ranked, rows_dev)
    token = lax.rem(ranked // rows_dev, 2)
    step = ranked // (2 * rows_dev)
    outer_step = lax.rem(step, outer)
    inner_step = step // outer
    offset = jnp.zeros(shape, jnp.int32)
    for index in range(inner):
        own = jnp.where(core == 0, plans[0][index], plans[1][index])
        offset = jnp.where(inner_step == index, own, offset)
    device = jnp.bitwise_xor(place, offset + inner * outer_step)
    source = token * rows + device * rows_dev + request
    return (row == source).astype(BF16)


def project_kernel(
    rows_dev, outer, plans, first, second, gain, w_query, w_key, w_value, *rest
):
    outs, (chunks, key_part, value_part, tokens, gains, scaled, sems) = rest[:-7], rest[-7:]
    nears, fars = outs[: len(plans[0])], outs[len(plans[0]) :]
    rows, depth = first.shape
    count = chunks.shape[0]
    heads_width = w_query.shape[1]
    kv_width = w_key.shape[1]

    copies = [
        (first, tokens.at[:rows]),
        (second, tokens.at[rows:]),
        (gain, gains),
        (w_key, key_part),
        (w_value, value_part),
    ] + [
        (w_query.at[:, index * CHUNK : (index + 1) * CHUNK], chunks.at[index])
        for index in range(count)
    ]
    copies = [
        pltpu.make_async_copy(source, target, sems.at[index])
        for index, (source, target) in enumerate(copies)
    ]
    for copy in copies:
        copy.start()
    for copy in copies[:3]:
        copy.wait()
    both = 2 * rows_dev
    block = outer * both
    pick = one_hot((2 * rows, 2 * rows), 0, plans, outer, rows_dev, rows)
    ordered = jnp.dot(pick, tokens[...], preferred_element_type=F32)
    squares = jnp.sum(ordered * ordered, axis=1, keepdims=True)
    scaled[...] = (ordered * gains[...].astype(F32)[None, :]).astype(BF16)

    def put(start, width, value, coded):
        for index, (near, far) in enumerate(zip(nears, fars)):
            begin = index * block
            part = coded if index > 0 else value
            near[:, start : start + width] = part[begin : begin + both].astype(near.dtype)
            far[:, start : start + width] = part[begin + both : begin + block].astype(far.dtype)

    end = heads_width + 2 * kv_width
    put(end, LANES, jnp.broadcast_to(squares, (2 * rows, LANES)), encoded(squares))
    for index, part in enumerate((key_part, value_part)):
        copies[3 + index].wait()
        put(
            heads_width + index * kv_width,
            kv_width,
            *[jnp.dot(scaled[...], part[...], preferred_element_type=F32)] * 2,
        )
    for index in range(count):
        copies[5 + index].wait()
        put(
            index * CHUNK,
            CHUNK,
            *[jnp.dot(scaled[...], chunks[index], preferred_element_type=F32)] * 2,
        )


def encoded(value):
    high = value.astype(BF16).astype(F32)
    lane = lax.broadcasted_iota(jnp.int32, (value.shape[0], LANES), 1)
    return jnp.where(lax.rem(lane, 2) == 0, high, value - high)


def decoded(tail):
    wide = tail.astype(F32)
    return wide + pltpu.roll(wide, 1, 1)


def combine_kernel(parts, keep, *refs):
    received, sends = refs[:parts], refs[parts:]
    width = keep.shape[1] - LANES
    both = sends[0].shape[0]
    total = keep[:, :width]
    tail = keep[:, width:]
    for part in received:
        total = total + part[:, :width].astype(F32)
        tail = tail + decoded(part[:, width:])
    coded = encoded(tail)
    for index, send in enumerate(sends):
        begin = index * both
        send[:, :width] = total[begin : begin + both].astype(BF16)
        send[:, width:] = coded[begin : begin + both].astype(BF16)


def attend_kernel(parts, model_width, lengths, mine, *refs):
    received = refs[:parts]
    (
        cosine,
        sine,
        key_cache,
        value_cache,
        attended,
        queries,
        new_keys,
        new_values,
        results,
        scores,
    ) = refs[parts:]
    rows_dev, kv_heads, _, width = key_cache.shape
    heads = queries.shape[0]
    group = heads // kv_heads
    both = mine.shape[0]
    end = mine.shape[1] - LANES
    tail = mine[:, end:]
    for part in received:
        tail = tail + decoded(part[:, end:])
    scale = lax.rsqrt(tail / model_width + EPSILON)

    def head(index):
        columns = slice(index * width, (index + 1) * width)
        value = mine[:, columns]
        for part in received:
            value = value + part[:, columns].astype(F32)
        return value * scale

    def rotate(value):
        return value * cosine[...] + pltpu.roll(value, width // 2, 1) * sine[...]

    for index in range(heads):
        queries[index] = rotate(head(index))
    blank = jnp.zeros((both, width), F32)
    for index in range(kv_heads):
        new_keys[index] = jnp.concatenate([rotate(head(heads + index)), blank], axis=0).astype(BF16)
        new_values[index] = jnp.concatenate(
            [head(heads + kv_heads + index), blank], axis=0
        ).astype(BF16)

    factor = 1.0 / math.sqrt(width)
    contract = (((1,), (1,)), ((), ()))

    pairs = [(row, index) for row in range(rows_dev) for index in range(kv_heads)]
    tops = []
    fresh = []
    for number, (row, index) in enumerate(pairs):
        pick = slice(index * group, (index + 1) * group)
        query = jnp.concatenate(
            [queries[pick, row, :], queries[pick, rows_dev + row, :]], axis=0
        ).astype(BF16)
        new = lax.dot_general(query, new_keys[index], contract, preferred_element_type=F32) * factor
        slot = lax.broadcasted_iota(jnp.int32, new.shape, 1)
        token = lax.broadcasted_iota(jnp.int32, new.shape, 0) // group
        seen = (lax.rem(slot, rows_dev) == row) & (slot // rows_dev <= token) & (slot < both)
        new = jnp.where(seen, new, NEGATIVE)
        cached = (
            lax.dot_general(query, key_cache[row, index], contract, preferred_element_type=F32)
            * factor
        )
        live = lax.broadcasted_iota(jnp.int32, cached.shape, 1) < lengths[row]
        cached = jnp.where(live, cached, NEGATIVE)
        scores[number] = cached
        tops.append(
            jnp.maximum(
                jnp.max(cached, axis=1, keepdims=True), jnp.max(new, axis=1, keepdims=True)
            )
        )
        fresh.append(new)
    for number, (row, index) in enumerate(pairs):
        pick = slice(index * group, (index + 1) * group)
        weight = jnp.exp(scores[number] - tops[number])
        new = jnp.exp(fresh[number] - tops[number])
        total = jnp.sum(weight, axis=1, keepdims=True) + jnp.sum(new, axis=1, keepdims=True)
        mixed = jnp.dot(
            weight.astype(BF16), value_cache[row, index], preferred_element_type=F32
        ) + jnp.dot(new.astype(BF16), new_values[index], preferred_element_type=F32)
        mixed = mixed / total
        results[pick, row, :] = mixed[:group]
        results[pick, rows_dev + row, :] = mixed[group:]

    for index in range(heads):
        attended[:, index * width : (index + 1) * width] = results[index].astype(BF16)


def output_kernel(rows_dev, outer, plans, gathered, w_output, out):
    count = out.shape[0]
    back = one_hot((count, count), 1, plans, outer, rows_dev, count // 2)
    attended = jnp.dot(back, gathered[...], preferred_element_type=F32).astype(BF16)
    out[...] = jnp.dot(attended, w_output[...], preferred_element_type=F32)


def whole(space=pltpu.VMEM):
    return pl.BlockSpec(memory_space=space)


def rotary(positions, width):
    half = width // 2
    inverse = jnp.exp(jnp.arange(half, dtype=F32) * (-2.0 * math.log(THETA) / width))
    where_at = jnp.concatenate([positions, positions + 1]).astype(F32)
    angle = where_at[:, None] * inverse
    cosine = jnp.cos(angle)
    sine = jnp.sin(angle)
    return (
        jnp.concatenate([cosine, cosine], axis=1),
        jnp.concatenate([-sine, sine], axis=1),
    )


def on_device(
    first_input,
    second_input,
    norm_gain,
    w_query,
    w_key,
    w_value,
    w_output,
    key_cache,
    value_cache,
    lengths,
    positions,
):
    devices = lax.axis_size("wide")
    cores = lax.axis_size("narrow")
    rows_dev, kv_heads, slots, width = key_cache.shape
    rows, depth = first_input.shape
    inner = math.gcd(devices, 4)
    outer = devices // inner
    both = 2 * rows_dev
    block = outer * both
    heads = w_query.shape[1] // width
    columns = w_query.shape[1] + 2 * w_key.shape[1] + LANES

    plans = ([0, 1, 2, 3], [0, 2, 1, 3]) if inner == 4 else (list(range(inner)),) * 2
    gather_plans = ([0, 1, 3, 2], [0, 2, 3, 1]) if inner == 4 else plans
    def exchange(value, steps):
        pairs = [
            (place_from * cores + c, (place_from ^ steps[min(c, 1)]) * cores + c)
            for c in range(cores)
            for place_from in range(devices)
        ]
        return lax.ppermute(value, ("wide", "narrow"), pairs)

    def placed(space, *values):
        return [pltpu.with_memory_space_constraint(value, space) for value in values]

    chunks = w_query.shape[1] // CHUNK
    types = [F32] + [BF16] * (inner - 1)
    near_far = pl.pallas_call(
        functools.partial(project_kernel, rows_dev, outer, plans),
        out_shape=[jax.ShapeDtypeStruct((both, columns), kind) for kind in types]
        + [jax.ShapeDtypeStruct((block - both, columns), kind) for kind in types],
        in_specs=[whole(pltpu.HBM)] * 6,
        out_specs=[whole()] * (2 * inner),
        scratch_shapes=[
            pltpu.VMEM((chunks, depth, CHUNK), BF16),
            pltpu.VMEM(w_key.shape, BF16),
            pltpu.VMEM(w_value.shape, BF16),
            pltpu.VMEM((2 * rows, depth), BF16),
            pltpu.VMEM((depth,), BF16),
            pltpu.VMEM((2 * rows, depth), BF16),
            pltpu.SemaphoreType.DMA((chunks + 5,)),
        ],
        compiler_params=pltpu.CompilerParams(vmem_limit_bytes=24 * MIB),
        cost_estimate=pl.CostEstimate(
            flops=4 * rows * depth * columns,
            bytes_accessed=2 * depth * columns,
            transcendentals=0,
        ),
        name="project",
    )(*placed(pltpu.HBM, first_input, second_input, norm_gain, w_query, w_key, w_value))

    def spread(values, steps):
        return [
            exchange(value, (steps[0][index + 1], steps[1][index + 1]))
            for index, value in enumerate(values)
        ]

    far = spread(near_far[inner + 1 :], plans)
    near = spread(near_far[1:inner], plans)
    sends = pl.pallas_call(
        functools.partial(combine_kernel, inner - 1),
        out_shape=[jax.ShapeDtypeStruct((both, columns), BF16)] * (outer - 1),
        in_specs=[whole()] * inner,
        out_specs=[whole()] * (outer - 1),
        compiler_params=pltpu.CompilerParams(vmem_limit_bytes=16 * MIB),
        name="combine",
    )(near_far[inner], *far)
    received = near + [
        exchange(send, (inner * (index + 1),) * 2) for index, send in enumerate(sends)
    ]

    cosine, sine = rotary(positions, width)
    attended = pl.pallas_call(
        functools.partial(attend_kernel, len(received), devices * depth),
        out_shape=jax.ShapeDtypeStruct((both, heads * width), BF16),
        in_specs=[whole(pltpu.SMEM)] + [whole()] * (len(received) + 5),
        out_specs=whole(),
        scratch_shapes=[
            pltpu.VMEM((heads, both, width), F32),
            pltpu.VMEM((kv_heads, 2 * both, width), BF16),
            pltpu.VMEM((kv_heads, 2 * both, width), BF16),
            pltpu.VMEM((heads, both, width), F32),
            pltpu.VMEM((rows_dev * kv_heads, 2 * heads // kv_heads, slots), F32),
        ],
        compiler_params=pltpu.CompilerParams(vmem_limit_bytes=32 * MIB),
        name="attend",
    )(lengths, near_far[0], *received, cosine, sine, *placed(pltpu.VMEM, key_cache, value_cache))

    far = [exchange(attended, (inner * step,) * 2) for step in range(1, outer)]
    far = jnp.concatenate(far, axis=0)
    own_blocks = spread([attended] * (inner - 1), gather_plans)
    far_blocks = spread([far] * (inner - 1), gather_plans)
    gathered = jnp.concatenate(
        [attended, far]
        + [block for blocks in zip(own_blocks, far_blocks) for block in blocks],
        axis=0,
    )
    part = pl.pallas_call(
        functools.partial(output_kernel, rows_dev, outer, gather_plans),
        out_shape=jax.ShapeDtypeStruct((2 * rows, w_output.shape[1]), F32),
        in_specs=[whole()] * 2,
        out_specs=whole(),
        compiler_params=pltpu.CompilerParams(vmem_limit_bytes=24 * MIB),
        name="output",
    )(gathered, *placed(pltpu.VMEM, w_output))
    total = part + lax.ppermute(part, "narrow", [(c, c ^ 1) for c in range(cores)])
    return (
        (first_input.astype(F32) + total[:rows]).astype(BF16),
        (second_input.astype(F32) + total[rows:]).astype(BF16),
    )


def solution(mesh):
    return jax.shard_map(
        on_device,
        mesh=mesh,
        in_specs=(
            P("groups", "wide"),
            P("groups", "wide"),
            P("wide"),
            P("wide", "narrow"),
            P("wide", "narrow"),
            P("wide", "narrow"),
            P("narrow", "wide"),
            P(("groups", "wide"), "narrow", None, None),
            P(("groups", "wide"), "narrow", None, None),
            P(("groups", "wide")),
            P(("groups", "wide")),
        ),
        out_specs=(P("groups", "wide"), P("groups", "wide")),
        check_vma=False,
    )
```

time: 45.6 us -> 41.9 us (0.919)
  waiting for transfers between devices: 20.9 us -> 8.5 us
  starting transfers between devices: 12.2 us -> 22.2 us
  Pallas kernels: 10.4 us -> 9.09 us
    ppermute x8 -> x14, waiting for transfers between devices: 19.4 us -> 6.98 us  [exchange(): return lax.ppermute(value, ('wide', 'narrow'), pairs)]
    ppermute x8 -> x14, starting transfers between devices: 12.1 us -> 22.2 us  [exchange(): return lax.ppermute(value, ('wide', 'narrow'), pairs)]
    pallas_call x2, Pallas kernels: 4.28 us -> 2.94 us  [the longest x1 2.85 us: on_device(): pl.pallas_call(functools.partial(attend_kernel, len(received), devices *...]
  transfers between devices with their start and end apart: 9 -> 15, of which waited for: 8 -> 7; matrix products, arithmetic and copies ran while one was open for 1% -> 1% of each run, Pallas kernels for 0% -> 0%
where the time goes in v3:
time: 41.9 us; the launch traced here: 41.7 us
  starting transfers between devices  22.2 us (53%)
  Pallas kernels  9.09 us (22%)
  waiting for transfers between devices  8.5 us (20%)
  other arithmetic  0.99 us (2%)
  between operations  0.82 us (2%)
    ppermute x14, starting transfers between devices, exchange(): return lax.ppermute(value, ('wide', 'narrow'), pairs)  22.2 us
    ppermute x14, waiting for transfers between devices, exchange(): return lax.ppermute(value, ('wide', 'narrow'), pairs)  6.98 us
    pallas_call x1, Pallas kernels, on_device(): pl.pallas_call(functools.partial(project_kernel, rows_dev, outer, plans),...  4.4 us
    pallas_call x1, Pallas kernels, on_device(): pl.pallas_call(functools.partial(attend_kernel, len(received), devices *...  2.85 us
    pallas_call x1, Pallas kernels, on_device(): pl.pallas_call(functools.partial(output_kernel, rows_dev, outer, gather_p...  1.75 us
    ppermute x1, waiting for transfers between devices, on_device(): lax.ppermute(part, 'narrow', [(c, c ^ 1) for c in range(cores)])  1.52 us
  transfers between devices with their start and end apart: 15, of which 7 were waited for; matrix products, arithmetic and copies ran while one was open for 1% of the time, Pallas kernels for 0%

profile of v3, /device:TPU:0, one launch (start us, length us, event | category | flops | bytes accessed | tf_op | source)
XLA Modules:
  0.0 41.7 jit_solution(7244386327843566957)
XLA Ops:
  0.7 4.4 %project.1 = (f32[8,4736]{1,0:T(8,128)S(1)}, bf16[8,4736]{1,0:T(8,128)(2,1)S(1)}, bf16[8,4736]{1,0:T(8,128)(2,1)S(1)}, bf16[8,4736]{1,0:T(8,128)(2,1)S(1)}, f32[...) custom-call(bf16[32,1024]{1,0:T(8,128)(2,1)} %first.1, ...), custom_call_target="tpu_custom_call" | custom-call | flops 620756992 | bytes 9699328 | tf_op jit(solution)/shard_map/project/pallas_call | solution.py:280
  5.1 3.0 %collective-permute-start.3 = (bf16[8,4736]{1,0:T(8,128)(2,1)S(1)}, bf16[8,4736]{1,0:T(8,128)(2,1)S(1)}, u32[]{:S(2)}, u32[]{:S(2)}) collective-permute-start(bf16[8,4736]{1,0:T(8,128)(2,1)S(1)} %get-tuple-element.15), channel_id=1, source_target_pairs={{0,2},{2,0},{4,6},{6,4},{8,10},{10,8},{12,14},{14,12},{1,5},{3,7},... | collective-permute-start | bytes 227336 | tf_op jit(solution)/shard_map/ppermute | solution.py:273
  8.1 1.6 %collective-permute-start.4 = (bf16[8,4736]{1,0:T(8,128)(2,1)S(1)}, bf16[8,4736]{1,0:T(8,128)(2,1)S(1)}, u32[]{:S(2)}, u32[]{:S(2)}) collective-permute-start(bf16[8,4736]{1,0:T(8,128)(2,1)S(1)} %get-tuple-element.16), channel_id=1, source_target_pairs={{0,4},{2,6},{4,0},{6,2},{8,12},{10,14},{12,8},{14,10},{1,3},{3,1},... | collective-permute-start | bytes 227336 | tf_op jit(solution)/shard_map/ppermute | solution.py:273
  9.7 1.9 %collective-permute-start = (bf16[8,4736]{1,0:T(8,128)(2,1)S(1)}, bf16[8,4736]{1,0:T(8,128)(2,1)S(1)}, u32[]{:S(2)}, u32[]{:S(2)}) collective-permute-start(bf16[8,4736]{1,0:T(8,128)(2,1)S(1)} %get-tuple-element.11), channel_id=1, source_target_pairs={{0,2},{2,0},{4,6},{6,4},{8,10},{10,8},{12,14},{14,12},{1,5},{3,7},... | collective-permute-start | bytes 227336 | tf_op jit(solution)/shard_map/ppermute | solution.py:273
  11.6 1.6 %collective-permute-start.1 = (bf16[8,4736]{1,0:T(8,128)(2,1)S(1)}, bf16[8,4736]{1,0:T(8,128)(2,1)S(1)}, u32[]{:S(2)}, u32[]{:S(2)}) collective-permute-start(bf16[8,4736]{1,0:T(8,128)(2,1)S(1)} %get-tuple-element.12), channel_id=1, source_target_pairs={{0,4},{2,6},{4,0},{6,2},{8,12},{10,14},{12,8},{14,10},{1,3},{3,1},... | collective-permute-start | bytes 227336 | tf_op jit(solution)/shard_map/ppermute | solution.py:273
  13.3 0.1 fusion.2
  13.4 0.9 %collective-permute-start.2 = (bf16[8,4736]{1,0:T(8,128)(2,1)S(1)}, bf16[8,4736]{1,0:T(8,128)(2,1)S(1)}, u32[]{:S(2)}, u32[]{:S(2)}) collective-permute-start(bf16[8,4736]{1,0:T(8,128)(2,1)S(1)} %get-tuple-element.13), channel_id=1, source_target_pairs={{0,6},{2,4},{4,2},{6,0},{8,14},{10,12},{12,10},{14,8},{1,7},{3,5},... | collective-permute-start | bytes 227336 | tf_op jit(solution)/shard_map/ppermute | solution.py:273
  14.3 0.8 %collective-permute-done.5.refs_2_ = bf16[8,4736]{1,0:T(8,128)(2,1)S(1)} collective-permute-done((bf16[8,4736]{1,0:T(8,128)(2,1)S(1)}, bf16[8,4736]{1,0:T(8,128)(2,1)S(1)}, u32[]{:S(2)}, u32[]{:S(2)}) %collective-permute-start.5) | collective-permute-done | bytes 75808 | tf_op jit(solution)/shard_map/ppermute | solution.py:273
  15.1 0.1 combine.1
  15.2 2.6 %collective-permute-start.6 = (bf16[8,4736]{1,0:T(8,128)(2,1)S(1)}, bf16[8,4736]{1,0:T(8,128)(2,1)S(1)}, u32[]{:S(2)}, u32[]{:S(2)}) collective-permute-start(bf16[8,4736]{1,0:T(8,128)(2,1)S(1)} %combine.1), channel_id=1, source_target_pairs={{0,8},{2,10},{4,12},{6,14},{8,0},{10,2},{12,4},{14,6},{1,9},{3,11}... | collective-permute-start | bytes 227336 | tf_op jit(solution)/shard_map/ppermute | solution.py:273
  17.9 1.0 %collective-permute-done.2.refs_2_ = bf16[8,4736]{1,0:T(8,128)(2,1)S(1)} collective-permute-done((bf16[8,4736]{1,0:T(8,128)(2,1)S(1)}, bf16[8,4736]{1,0:T(8,128)(2,1)S(1)}, u32[]{:S(2)}, u32[]{:S(2)}) %collective-permute-start.2) | collective-permute-done | bytes 75808 | tf_op jit(solution)/shard_map/ppermute | solution.py:273
  18.9 1.6 %collective-permute-done.6.refs_3_ = bf16[8,4736]{1,0:T(8,128)(2,1)S(1)} collective-permute-done((bf16[8,4736]{1,0:T(8,128)(2,1)S(1)}, bf16[8,4736]{1,0:T(8,128)(2,1)S(1)}, u32[]{:S(2)}, u32[]{:S(2)}) %collective-permute-start.6) | collective-permute-done | bytes 75808 | tf_op jit(solution)/shard_map/ppermute | solution.py:273
  20.5 2.8 %attend.1 = bf16[8,4096]{1,0:T(8,128)(2,1)S(1)} custom-call(s32[4]{0:T(128)S(1)} %copy-done.2, f32[8,4736]{1,0:T(8,128)S(1)} %get-tuple-element.10.mine, bf16[8,4736]{1,0:T(8,128)(2,1)S(1)} %collective-permute-done.refs_0_, bf16[8,4736]{1,0:T(8,128)(2,1)S(1)} %collective-permute-done.1.refs_1_, bf16[8,4736]{1,0:T(8,128)(2,1)S(1)} %collective-permute-done.2.refs_2_, ...), custom_call_target="tpu_custom_call" | custom-call | tf_op jit(solution)/shard_map/attend/pallas_call | solution.py:325
  23.4 2.7 %collective-permute-start.7 = (bf16[8,4096]{1,0:T(8,128)(2,1)S(1)}, bf16[8,4096]{1,0:T(8,128)(2,1)S(1)}, u32[]{:S(2)}, u32[]{:S(2)}) collective-permute-start(bf16[8,4096]{1,0:T(8,128)(2,1)S(1)} %attend.1), channel_id=1, source_target_pairs={{0,8},{2,10},{4,12},{6,14},{8,0},{10,2},{12,4},{14,6},{1,9},{3,11}... | collective-permute-start | bytes 196616 | tf_op jit(solution)/shard_map/ppermute | solution.py:273
  26.1 1.3 %collective-permute-start.8 = (bf16[8,4096]{1,0:T(8,128)(2,1)S(1)}, bf16[8,4096]{1,0:T(8,128)(2,1)S(1)}, u32[]{:S(2)}, u32[]{:S(2)}) collective-permute-start(bf16[8,4096]{1,0:T(8,128)(2,1)S(1)} %attend.1), channel_id=1, source_target_pairs={{0,2},{2,0},{4,6},{6,4},{8,10},{10,8},{12,14},{14,12},{1,5},{3,7},... | collective-permute-start | bytes 196616 | tf_op jit(solution)/shard_map/ppermute | solution.py:273
  27.5 2.3 %collective-permute-start.10 = (bf16[8,4096]{1,0:T(8,128)(2,1)S(1)}, bf16[8,4096]{1,0:T(8,128)(2,1)S(1)}, u32[]{:S(2)}, u32[]{:S(2)}) collective-permute-start(bf16[8,4096]{1,0:T(8,128)(2,1)S(1)} %attend.1), channel_id=1, source_target_pairs={{0,6},{2,4},{4,2},{6,0},{8,14},{10,12},{12,10},{14,8},{1,7},{3,5},... | collective-permute-start | bytes 196616 | tf_op jit(solution)/shard_map/ppermute | solution.py:273
  29.8 1.4 %collective-permute-start.9 = (bf16[8,4096]{1,0:T(8,128)(2,1)S(1)}, bf16[8,4096]{1,0:T(8,128)(2,1)S(1)}, u32[]{:S(2)}, u32[]{:S(2)}) collective-permute-start(bf16[8,4096]{1,0:T(8,128)(2,1)S(1)} %collective-permute-done.7), channel_id=1, source_target_pairs={{0,2},{2,0},{4,6},{6,4},{8,10},{10,8},{12,14},{14,12},{1,5},{3,7},... | collective-permute-start | bytes 196616 | tf_op jit(solution)/shard_map/ppermute | solution.py:273
  31.1 2.1 %collective-permute-start.11 = (bf16[8,4096]{1,0:T(8,128)(2,1)S(1)}, bf16[8,4096]{1,0:T(8,128)(2,1)S(1)}, u32[]{:S(2)}, u32[]{:S(2)}) collective-permute-start(bf16[8,4096]{1,0:T(8,128)(2,1)S(1)} %collective-permute-done.7), channel_id=1, source_target_pairs={{0,6},{2,4},{4,2},{6,0},{8,14},{10,12},{12,10},{14,8},{1,7},{3,5},... | collective-permute-start | bytes 196616 | tf_op jit(solution)/shard_map/ppermute | solution.py:273
  33.3 0.7 %collective-permute-start.13 = (bf16[8,4096]{1,0:T(8,128)(2,1)S(1)}, bf16[8,4096]{1,0:T(8,128)(2,1)S(1)}, u32[]{:S(2)}, u32[]{:S(2)}) collective-permute-start(bf16[8,4096]{1,0:T(8,128)(2,1)S(1)} %collective-permute-done.7), channel_id=1, source_target_pairs={{0,4},{2,6},{4,0},{6,2},{8,12},{10,14},{12,8},{14,10},{1,3},{3,1},... | collective-permute-start | bytes 196616 | tf_op jit(solution)/shard_map/ppermute | solution.py:273
  34.1 2.2 %collective-permute-done.11 = bf16[8,4096]{1,0:T(8,128)(2,1)S(1)} collective-permute-done((bf16[8,4096]{1,0:T(8,128)(2,1)S(1)}, bf16[8,4096]{1,0:T(8,128)(2,1)S(1)}, u32[]{:S(2)}, u32[]{:S(2)}) %collective-permute-start.11) | collective-permute-done | bytes 65568 | tf_op jit(solution)/shard_map/ppermute | solution.py:273
  36.3 1.3 %collective-permute-done.13 = bf16[8,4096]{1,0:T(8,128)(2,1)S(1)} collective-permute-done((bf16[8,4096]{1,0:T(8,128)(2,1)S(1)}, bf16[8,4096]{1,0:T(8,128)(2,1)S(1)}, u32[]{:S(2)}, u32[]{:S(2)}) %collective-permute-start.13) | collective-permute-done | bytes 65568 | tf_op jit(solution)/shard_map/ppermute | solution.py:273
  37.6 1.8 %output.1 = f32[64,1024]{1,0:T(8,128)S(1)} custom-call(bf16[64,4096]{1,0:T(8,128)(2,1)S(1)} %constant_dynamic-update-slice_fusion.gathered, bf16[4096,1024]{1,0:T(8,128)(2,1)S(1)} %bitcast.1), custom_call_target="tpu_custom_call" | custom-call | tf_op jit(solution)/shard_map/output/pallas_call | solution.py:350
  39.5 1.5 %collective-permute-done.14 = f32[64,1024]{1,0:T(8,128)S(1)} collective-permute-done((f32[64,1024]{1,0:T(8,128)S(1)}, f32[64,1024]{1,0:T(8,128)S(1)}, u32[]{:S(2)}, u32[]{:S(2)}) %collective-permute-start.14) | collective-permute-done | bytes 262176 | tf_op jit(solution)/shard_map/ppermute | solution.py:358
  41.0 0.7 %fusion = (bf16[32,1024]{1,0:T(8,128)(2,1)}, bf16[32,1024]{1,0:T(8,128)(2,1)}) fusion(f32[64,1024]{1,0:T(8,128)S(1)} %add.13, bf16[32,1024]{1,0:T(8,128)(2,1)S(1)} %copy-done.4, bf16[32,1024]{1,0:T(8,128)(2,1)S(1)} %copy-done.3), kind=kLoop, calls=%fused_computation.1 | loop fusion | flops 196608 | bytes 524288 | tf_op jit(solution)/shard_map/convert_element_type | solution.py:361
  (42 shorter events, 0.5 us)
Async XLA Ops:
  0.6 12.6 %copy-start.5 = (s32[4]{0:T(128)S(1)}, s32[4]{0:T(128)}, u32[]{:S(2)}) copy-start(s32[4]{0:T(128)} %param.21) | copy-start | bytes 52
  0.6 19.8 %copy-start = (bf16[4,2,2048,128]{3,2,1,0:T(8,128)(2,1)S(1)}, bf16[4,2,2048,128]{3,2,1,0:T(8,128)(2,1)}, u32[]{:S(2)}) copy-start(bf16[4,2,2048,128]{3,2,1,0:T(8,128)(2,1)} %refs_6_.1) | copy-start | bytes 12582916
  0.7 19.8 %copy-start.1 = (bf16[4,2,2048,128]{3,2,1,0:T(8,128)(2,1)S(1)}, bf16[4,2,2048,128]{3,2,1,0:T(8,128)(2,1)}, u32[]{:S(2)}) copy-start(bf16[4,2,2048,128]{3,2,1,0:T(8,128)(2,1)} %refs_7_.1) | copy-start | bytes 12582916
  0.7 19.8 %copy-start.2 = (s32[4]{0:T(128)S(1)}, s32[4]{0:T(128)}, u32[]{:S(2)}) copy-start(s32[4]{0:T(128)} %lengths.1) | copy-start | bytes 52
  0.7 36.9 %slice-start = ((s8[8388608]{0:T(1024)(128)(4,1)}), s8[4194304]{0:T(1024)(128)(4,1)S(1)}, s32[]{:S(2)}) async-start(s8[8388608]{0:T(1024)(128)(4,1)} %bitcast), calls=%async_computation | async-start | bytes 8388608
  5.1 8.3 %collective-permute-start.3 = (bf16[8,4736]{1,0:T(8,128)(2,1)S(1)}, bf16[8,4736]{1,0:T(8,128)(2,1)S(1)}, u32[]{:S(2)}, u32[]{:S(2)}) collective-permute-start(bf16[8,4736]{1,0:T(8,128)(2,1)S(1)} %get-tuple-element.15), channel_id=1, source_target_pairs={{0,2},{2,0},{4,6},{6,4},{8,10},{10,8},{12,14},{14,12},{1,5},{3,7},... | collective-permute-start | bytes 227336 | tf_op jit(solution)/shard_map/ppermute | solution.py:273
  8.1 6.2 %collective-permute-start.4 = (bf16[8,4736]{1,0:T(8,128)(2,1)S(1)}, bf16[8,4736]{1,0:T(8,128)(2,1)S(1)}, u32[]{:S(2)}, u32[]{:S(2)}) collective-permute-start(bf16[8,4736]{1,0:T(8,128)(2,1)S(1)} %get-tuple-element.16), channel_id=1, source_target_pairs={{0,4},{2,6},{4,0},{6,2},{8,12},{10,14},{12,8},{14,10},{1,3},{3,1},... | collective-permute-start | bytes 227336 | tf_op jit(solution)/shard_map/ppermute | solution.py:273
  9.7 5.4 %collective-permute-start.5 = (bf16[8,4736]{1,0:T(8,128)(2,1)S(1)}, bf16[8,4736]{1,0:T(8,128)(2,1)S(1)}, u32[]{:S(2)}, u32[]{:S(2)}) collective-permute-start(bf16[8,4736]{1,0:T(8,128)(2,1)S(1)} %get-tuple-element.17), channel_id=1, source_target_pairs={{0,6},{2,4},{4,2},{6,0},{8,14},{10,12},{12,10},{14,8},{1,7},{3,5},... | collective-permute-start | bytes 227336 | tf_op jit(solution)/shard_map/ppermute | solution.py:273
  9.7 8.2 %collective-permute-start = (bf16[8,4736]{1,0:T(8,128)(2,1)S(1)}, bf16[8,4736]{1,0:T(8,128)(2,1)S(1)}, u32[]{:S(2)}, u32[]{:S(2)}) collective-permute-start(bf16[8,4736]{1,0:T(8,128)(2,1)S(1)} %get-tuple-element.11), channel_id=1, source_target_pairs={{0,2},{2,0},{4,6},{6,4},{8,10},{10,8},{12,14},{14,12},{1,5},{3,7},... | collective-permute-start | bytes 227336 | tf_op jit(solution)/shard_map/ppermute | solution.py:273
  11.6 6.3 %collective-permute-start.1 = (bf16[8,4736]{1,0:T(8,128)(2,1)S(1)}, bf16[8,4736]{1,0:T(8,128)(2,1)S(1)}, u32[]{:S(2)}, u32[]{:S(2)}) collective-permute-start(bf16[8,4736]{1,0:T(8,128)(2,1)S(1)} %get-tuple-element.12), channel_id=1, source_target_pairs={{0,4},{2,6},{4,0},{6,2},{8,12},{10,14},{12,8},{14,10},{1,3},{3,1},... | collective-permute-start | bytes 227336 | tf_op jit(solution)/shard_map/ppermute | solution.py:273
  13.4 5.5 %collective-permute-start.2 = (bf16[8,4736]{1,0:T(8,128)(2,1)S(1)}, bf16[8,4736]{1,0:T(8,128)(2,1)S(1)}, u32[]{:S(2)}, u32[]{:S(2)}) collective-permute-start(bf16[8,4736]{1,0:T(8,128)(2,1)S(1)} %get-tuple-element.13), channel_id=1, source_target_pairs={{0,6},{2,4},{4,2},{6,0},{8,14},{10,12},{12,10},{14,8},{1,7},{3,5},... | collective-permute-start | bytes 227336 | tf_op jit(solution)/shard_map/ppermute | solution.py:273
  15.1 22.5 %slice-start.1 = ((s8[8388608]{0:T(1024)(128)(4,1)}), s8[4194304]{0:T(1024)(128)(4,1)S(1)}, s32[]{:S(2)}) async-start(s8[8388608]{0:T(1024)(128)(4,1)} %bitcast), calls=%async_computation.1 | async-start | bytes 8388608
  15.2 5.3 %collective-permute-start.6 = (bf16[8,4736]{1,0:T(8,128)(2,1)S(1)}, bf16[8,4736]{1,0:T(8,128)(2,1)S(1)}, u32[]{:S(2)}, u32[]{:S(2)}) collective-permute-start(bf16[8,4736]{1,0:T(8,128)(2,1)S(1)} %combine.1), channel_id=1, source_target_pairs={{0,8},{2,10},{4,12},{6,14},{8,0},{10,2},{12,4},{14,6},{1,9},{3,11}... | collective-permute-start | bytes 227336 | tf_op jit(solution)/shard_map/ppermute | solution.py:273
  20.5 20.5 %copy-start.3 = (bf16[32,1024]{1,0:T(8,128)(2,1)S(1)}, bf16[32,1024]{1,0:T(8,128)(2,1)}, u32[]{:S(2)}) copy-start(bf16[32,1024]{1,0:T(8,128)(2,1)} %first.1) | copy-start | bytes 196612
  20.5 20.5 %copy-start.4 = (bf16[32,1024]{1,0:T(8,128)(2,1)S(1)}, bf16[32,1024]{1,0:T(8,128)(2,1)}, u32[]{:S(2)}) copy-start(bf16[32,1024]{1,0:T(8,128)(2,1)} %second.1) | copy-start | bytes 196612
  23.4 6.4 %collective-permute-start.7 = (bf16[8,4096]{1,0:T(8,128)(2,1)S(1)}, bf16[8,4096]{1,0:T(8,128)(2,1)S(1)}, u32[]{:S(2)}, u32[]{:S(2)}) collective-permute-start(bf16[8,4096]{1,0:T(8,128)(2,1)S(1)} %attend.1), channel_id=1, source_target_pairs={{0,8},{2,10},{4,12},{6,14},{8,0},{10,2},{12,4},{14,6},{1,9},{3,11}... | collective-permute-start | bytes 196616 | tf_op jit(solution)/shard_map/ppermute | solution.py:273
  26.1 7.1 %collective-permute-start.8 = (bf16[8,4096]{1,0:T(8,128)(2,1)S(1)}, bf16[8,4096]{1,0:T(8,128)(2,1)S(1)}, u32[]{:S(2)}, u32[]{:S(2)}) collective-permute-start(bf16[8,4096]{1,0:T(8,128)(2,1)S(1)} %attend.1), channel_id=1, source_target_pairs={{0,2},{2,0},{4,6},{6,4},{8,10},{10,8},{12,14},{14,12},{1,5},{3,7},... | collective-permute-start | bytes 196616 | tf_op jit(solution)/shard_map/ppermute | solution.py:273
  27.5 6.6 %collective-permute-start.10 = (bf16[8,4096]{1,0:T(8,128)(2,1)S(1)}, bf16[8,4096]{1,0:T(8,128)(2,1)S(1)}, u32[]{:S(2)}, u32[]{:S(2)}) collective-permute-start(bf16[8,4096]{1,0:T(8,128)(2,1)S(1)} %attend.1), channel_id=1, source_target_pairs={{0,6},{2,4},{4,2},{6,0},{8,14},{10,12},{12,10},{14,8},{1,7},{3,5},... | collective-permute-start | bytes 196616 | tf_op jit(solution)/shard_map/ppermute | solution.py:273
  29.8 6.5 %collective-permute-start.12 = (bf16[8,4096]{1,0:T(8,128)(2,1)S(1)}, bf16[8,4096]{1,0:T(8,128)(2,1)S(1)}, u32[]{:S(2)}, u32[]{:S(2)}) collective-permute-start(bf16[8,4096]{1,0:T(8,128)(2,1)S(1)} %attend.1), channel_id=1, source_target_pairs={{0,4},{2,6},{4,0},{6,2},{8,12},{10,14},{12,8},{14,10},{1,3},{3,1},... | collective-permute-start | bytes 196616 | tf_op jit(solution)/shard_map/ppermute | solution.py:273
  29.8 4.3 %collective-permute-start.9 = (bf16[8,4096]{1,0:T(8,128)(2,1)S(1)}, bf16[8,4096]{1,0:T(8,128)(2,1)S(1)}, u32[]{:S(2)}, u32[]{:S(2)}) collective-permute-start(bf16[8,4096]{1,0:T(8,128)(2,1)S(1)} %collective-permute-done.7), channel_id=1, source_target_pairs={{0,2},{2,0},{4,6},{6,4},{8,10},{10,8},{12,14},{14,12},{1,5},{3,7},... | collective-permute-start | bytes 196616 | tf_op jit(solution)/shard_map/ppermute | solution.py:273
  31.1 5.2 %collective-permute-start.11 = (bf16[8,4096]{1,0:T(8,128)(2,1)S(1)}, bf16[8,4096]{1,0:T(8,128)(2,1)S(1)}, u32[]{:S(2)}, u32[]{:S(2)}) collective-permute-start(bf16[8,4096]{1,0:T(8,128)(2,1)S(1)} %collective-permute-done.7), channel_id=1, source_target_pairs={{0,6},{2,4},{4,2},{6,0},{8,14},{10,12},{12,10},{14,8},{1,7},{3,5},... | collective-permute-start | bytes 196616 | tf_op jit(solution)/shard_map/ppermute | solution.py:273
  33.3 4.3 %collective-permute-start.13 = (bf16[8,4096]{1,0:T(8,128)(2,1)S(1)}, bf16[8,4096]{1,0:T(8,128)(2,1)S(1)}, u32[]{:S(2)}, u32[]{:S(2)}) collective-permute-start(bf16[8,4096]{1,0:T(8,128)(2,1)S(1)} %collective-permute-done.7), channel_id=1, source_target_pairs={{0,4},{2,6},{4,0},{6,2},{8,12},{10,14},{12,8},{14,10},{1,3},{3,1},... | collective-permute-start | bytes 196616 | tf_op jit(solution)/shard_map/ppermute | solution.py:273
  39.4 1.6 %collective-permute-start.14 = (f32[64,1024]{1,0:T(8,128)S(1)}, f32[64,1024]{1,0:T(8,128)S(1)}, u32[]{:S(2)}, u32[]{:S(2)}) collective-permute-start(f32[64,1024]{1,0:T(8,128)S(1)} %output.1), channel_id=1, source_target_pairs={{0,1},{1,0},{2,3},{3,2},{4,5},{5,4},{6,7},{7,6},{8,9},{9,8},{10,11... | collective-permute-start | bytes 786440 | tf_op jit(solution)/shard_map/ppermute | solution.py:358

commit v4 on v3

--- a/solution.py
+++ b/solution.py
@@ -262,8 +262,8 @@
     heads = w_query.shape[1] // width
     columns = w_query.shape[1] + 2 * w_key.shape[1] + LANES
 
-    plans = ([0, 1, 2, 3], [0, 2, 1, 3]) if inner == 4 else (list(range(inner)),) * 2
-    gather_plans = ([0, 1, 3, 2], [0, 2, 3, 1]) if inner == 4 else plans
+    plans = ([0, 3, 1, 2], [0, 3, 1, 2]) if inner == 4 else (list(range(inner)),) * 2
+    gather_plans = ([0, 1, 2, 3], [0, 2, 1, 3]) if inner == 4 else plans
     def exchange(value, steps):
         pairs = [
             (place_from * cores + c, (place_from ^ steps[min(c, 1)]) * cores + c)
@@ -340,11 +340,12 @@
 
     far = [exchange(attended, (inner * step,) * 2) for step in range(1, outer)]
     far = jnp.concatenate(far, axis=0)
-    own_blocks = spread([attended] * (inner - 1), gather_plans)
-    far_blocks = spread([far] * (inner - 1), gather_plans)
+    own_blocks = spread([attended] * (inner - 2), gather_plans)
+    far_blocks = spread([far] * (inner - 2), gather_plans)
+    near = jnp.concatenate([attended, far], axis=0)
+    last = exchange(near, (gather_plans[0][-1], gather_plans[1][-1]))
     gathered = jnp.concatenate(
-        [attended, far]
-        + [block for blocks in zip(own_blocks, far_blocks) for block in blocks],
+        [near] + [block for blocks in zip(own_blocks, far_blocks) for block in blocks] + [last],
         axis=0,
     )
     part = pl.pallas_call(

time: 41.9 us -> 40 us (0.955)
  starting transfers between devices: 22.2 us -> 20.9 us
  waiting for transfers between devices: 8.5 us -> 7.91 us
    ppermute x14 -> x13, starting transfers between devices: 22.2 us -> 20.9 us  [exchange(): return lax.ppermute(value, ('wide', 'narrow'), pairs)]
    ppermute x14 -> x13, waiting for transfers between devices: 6.98 us -> 6.38 us  [exchange(): return lax.ppermute(value, ('wide', 'narrow'), pairs)]
  transfers between devices with their start and end apart: 15 -> 14, of which waited for: 7 -> 6; matrix products, arithmetic and copies ran while one was open for 1% -> 1% of each run, Pallas kernels for 0% -> 0%
where the time goes in v4:
time: 40 us; the launch traced here: 39.8 us
  starting transfers between devices  20.9 us (52%)
  Pallas kernels  9.08 us (23%)
  waiting for transfers between devices  7.91 us (20%)
  other arithmetic  1 us (2%)
  between operations  0.84 us (2%)
    ppermute x13, starting transfers between devices, exchange(): return lax.ppermute(value, ('wide', 'narrow'), pairs)  20.9 us
    ppermute x13, waiting for transfers between devices, exchange(): return lax.ppermute(value, ('wide', 'narrow'), pairs)  6.38 us
    pallas_call x1, Pallas kernels, on_device(): pl.pallas_call(functools.partial(project_kernel, rows_dev, outer, plans),...  4.4 us
    pallas_call x1, Pallas kernels, on_device(): pl.pallas_call(functools.partial(attend_kernel, len(received), devices *...  2.84 us
    pallas_call x1, Pallas kernels, on_device(): pl.pallas_call(functools.partial(output_kernel, rows_dev, outer, gather_p...  1.74 us
    ppermute x1, waiting for transfers between devices, on_device(): lax.ppermute(part, 'narrow', [(c, c ^ 1) for c in range(cores)])  1.52 us
  transfers between devices with their start and end apart: 14, of which 6 were waited for; matrix products, arithmetic and copies ran while one was open for 1% of the time, Pallas kernels for 0%

profile of v4, /device:TPU:0, one launch (start us, length us, event | category | flops | bytes accessed | tf_op | source)
XLA Modules:
  0.0 39.8 jit_solution(14593097781638888089)
XLA Ops:
  0.7 4.4 %project.1 = (f32[8,4736]{1,0:T(8,128)S(1)}, bf16[8,4736]{1,0:T(8,128)(2,1)S(1)}, bf16[8,4736]{1,0:T(8,128)(2,1)S(1)}, bf16[8,4736]{1,0:T(8,128)(2,1)S(1)}, f32[...) custom-call(bf16[32,1024]{1,0:T(8,128)(2,1)} %first.1, ...), custom_call_target="tpu_custom_call" | custom-call | flops 620756992 | bytes 9699328 | tf_op jit(solution)/shard_map/project/pallas_call | solution.py:280
  5.1 4.0 %collective-permute-start.3 = (bf16[8,4736]{1,0:T(8,128)(2,1)S(1)}, bf16[8,4736]{1,0:T(8,128)(2,1)S(1)}, u32[]{:S(2)}, u32[]{:S(2)}) collective-permute-start(bf16[8,4736]{1,0:T(8,128)(2,1)S(1)} %get-tuple-element.15), channel_id=1, source_target_pairs={{0,6},{2,4},{4,2},{6,0},{8,14},{10,12},{12,10},{14,8},{1,7},{3,5},... | collective-permute-start | bytes 227336 | tf_op jit(solution)/shard_map/ppermute | solution.py:273
  9.1 0.5 %collective-permute-start.4 = (bf16[8,4736]{1,0:T(8,128)(2,1)S(1)}, bf16[8,4736]{1,0:T(8,128)(2,1)S(1)}, u32[]{:S(2)}, u32[]{:S(2)}) collective-permute-start(bf16[8,4736]{1,0:T(8,128)(2,1)S(1)} %get-tuple-element.16), channel_id=1, source_target_pairs={{0,2},{2,0},{4,6},{6,4},{8,10},{10,8},{12,14},{14,12},{1,3},{3,1},... | collective-permute-start | bytes 227336 | tf_op jit(solution)/shard_map/ppermute | solution.py:273
  9.6 0.1 collective-permute-start.5
  9.8 2.8 %collective-permute-start = (bf16[8,4736]{1,0:T(8,128)(2,1)S(1)}, bf16[8,4736]{1,0:T(8,128)(2,1)S(1)}, u32[]{:S(2)}, u32[]{:S(2)}) collective-permute-start(bf16[8,4736]{1,0:T(8,128)(2,1)S(1)} %get-tuple-element.11), channel_id=1, source_target_pairs={{0,6},{2,4},{4,2},{6,0},{8,14},{10,12},{12,10},{14,8},{1,7},{3,5},... | collective-permute-start | bytes 227336 | tf_op jit(solution)/shard_map/ppermute | solution.py:273
  12.6 0.5 %collective-permute-start.1 = (bf16[8,4736]{1,0:T(8,128)(2,1)S(1)}, bf16[8,4736]{1,0:T(8,128)(2,1)S(1)}, u32[]{:S(2)}, u32[]{:S(2)}) collective-permute-start(bf16[8,4736]{1,0:T(8,128)(2,1)S(1)} %get-tuple-element.12), channel_id=1, source_target_pairs={{0,2},{2,0},{4,6},{6,4},{8,10},{10,8},{12,14},{14,12},{1,3},{3,1},... | collective-permute-start | bytes 227336 | tf_op jit(solution)/shard_map/ppermute | solution.py:273
  13.2 0.1 fusion.2
  13.4 0.6 %collective-permute-start.2 = (bf16[8,4736]{1,0:T(8,128)(2,1)S(1)}, bf16[8,4736]{1,0:T(8,128)(2,1)S(1)}, u32[]{:S(2)}, u32[]{:S(2)}) collective-permute-start(bf16[8,4736]{1,0:T(8,128)(2,1)S(1)} %get-tuple-element.13), channel_id=1, source_target_pairs={{0,4},{2,6},{4,0},{6,2},{8,12},{10,14},{12,8},{14,10},{1,5},{3,7},... | collective-permute-start | bytes 227336 | tf_op jit(solution)/shard_map/ppermute | solution.py:273
  14.0 0.4 %collective-permute-done.4.refs_1_ = bf16[8,4736]{1,0:T(8,128)(2,1)S(1)} collective-permute-done((bf16[8,4736]{1,0:T(8,128)(2,1)S(1)}, bf16[8,4736]{1,0:T(8,128)(2,1)S(1)}, u32[]{:S(2)}, u32[]{:S(2)}) %collective-permute-start.4) | collective-permute-done | bytes 75808 | tf_op jit(solution)/shard_map/ppermute | solution.py:273
  14.5 2.6 %collective-permute-start.6 = (bf16[8,4736]{1,0:T(8,128)(2,1)S(1)}, bf16[8,4736]{1,0:T(8,128)(2,1)S(1)}, u32[]{:S(2)}, u32[]{:S(2)}) collective-permute-start(bf16[8,4736]{1,0:T(8,128)(2,1)S(1)} %combine.1), channel_id=1, source_target_pairs={{0,8},{2,10},{4,12},{6,14},{8,0},{10,2},{12,4},{14,6},{1,9},{3,11}... | collective-permute-start | bytes 227336 | tf_op jit(solution)/shard_map/ppermute | solution.py:273
  17.2 0.9 %collective-permute-done.2.refs_2_ = bf16[8,4736]{1,0:T(8,128)(2,1)S(1)} collective-permute-done((bf16[8,4736]{1,0:T(8,128)(2,1)S(1)}, bf16[8,4736]{1,0:T(8,128)(2,1)S(1)}, u32[]{:S(2)}, u32[]{:S(2)}) %collective-permute-start.2) | collective-permute-done | bytes 75808 | tf_op jit(solution)/shard_map/ppermute | solution.py:273
  18.1 1.7 %collective-permute-done.6.refs_3_ = bf16[8,4736]{1,0:T(8,128)(2,1)S(1)} collective-permute-done((bf16[8,4736]{1,0:T(8,128)(2,1)S(1)}, bf16[8,4736]{1,0:T(8,128)(2,1)S(1)}, u32[]{:S(2)}, u32[]{:S(2)}) %collective-permute-start.6) | collective-permute-done | bytes 75808 | tf_op jit(solution)/shard_map/ppermute | solution.py:273
  19.9 2.8 %attend.1 = bf16[8,4096]{1,0:T(8,128)(2,1)S(1)} custom-call(s32[4]{0:T(128)S(1)} %copy-done.2, f32[8,4736]{1,0:T(8,128)S(1)} %get-tuple-element.10.mine, bf16[8,4736]{1,0:T(8,128)(2,1)S(1)} %collective-permute-done.refs_0_, bf16[8,4736]{1,0:T(8,128)(2,1)S(1)} %collective-permute-done.1.refs_1_, bf16[8,4736]{1,0:T(8,128)(2,1)S(1)} %collective-permute-done.2.refs_2_, ...), custom_call_target="tpu_custom_call" | custom-call | tf_op jit(solution)/shard_map/attend/pallas_call | solution.py:325
  22.7 2.7 %collective-permute-start.7 = (bf16[8,4096]{1,0:T(8,128)(2,1)S(1)}, bf16[8,4096]{1,0:T(8,128)(2,1)S(1)}, u32[]{:S(2)}, u32[]{:S(2)}) collective-permute-start(bf16[8,4096]{1,0:T(8,128)(2,1)S(1)} %attend.1), channel_id=1, source_target_pairs={{0,8},{2,10},{4,12},{6,14},{8,0},{10,2},{12,4},{14,6},{1,9},{3,11}... | collective-permute-start | bytes 196616 | tf_op jit(solution)/shard_map/ppermute | solution.py:273
  25.4 1.6 %collective-permute-start.8 = (bf16[8,4096]{1,0:T(8,128)(2,1)S(1)}, bf16[8,4096]{1,0:T(8,128)(2,1)S(1)}, u32[]{:S(2)}, u32[]{:S(2)}) collective-permute-start(bf16[8,4096]{1,0:T(8,128)(2,1)S(1)} %attend.1), channel_id=1, source_target_pairs={{0,2},{2,0},{4,6},{6,4},{8,10},{10,8},{12,14},{14,12},{1,5},{3,7},... | collective-permute-start | bytes 196616 | tf_op jit(solution)/shard_map/ppermute | solution.py:273
  27.0 1.7 %collective-permute-start.10 = (bf16[8,4096]{1,0:T(8,128)(2,1)S(1)}, bf16[8,4096]{1,0:T(8,128)(2,1)S(1)}, u32[]{:S(2)}, u32[]{:S(2)}) collective-permute-start(bf16[8,4096]{1,0:T(8,128)(2,1)S(1)} %attend.1), channel_id=1, source_target_pairs={{0,4},{2,6},{4,0},{6,2},{8,12},{10,14},{12,8},{14,10},{1,3},{3,1},... | collective-permute-start | bytes 196616 | tf_op jit(solution)/shard_map/ppermute | solution.py:273
  28.8 1.8 %collective-permute-start.12 = (bf16[16,4096]{1,0:T(8,128)(2,1)S(1)}, bf16[16,4096]{1,0:T(8,128)(2,1)S(1)}, u32[]{:S(2)}, u32[]{:S(2)}) collective-permute-start(bf16[16,4096]{1,0:T(8,128)(2,1)S(1)} %pad_maximum_fusion), channel_id=1, source_target_pairs={{0,6},{2,4},{4,2},{6,0},{8,14},{10,12},{12,10},{14,8},{1,7},{3,5},... | collective-permute-start | bytes 393224 | tf_op jit(solution)/shard_map/ppermute | solution.py:273
  30.6 0.8 %collective-permute-start.9 = (bf16[8,4096]{1,0:T(8,128)(2,1)S(1)}, bf16[8,4096]{1,0:T(8,128)(2,1)S(1)}, u32[]{:S(2)}, u32[]{:S(2)}) collective-permute-start(bf16[8,4096]{1,0:T(8,128)(2,1)S(1)} %collective-permute-done.7), channel_id=1, source_target_pairs={{0,2},{2,0},{4,6},{6,4},{8,10},{10,8},{12,14},{14,12},{1,5},{3,7},... | collective-permute-start | bytes 196616 | tf_op jit(solution)/shard_map/ppermute | solution.py:273
  31.4 0.9 %collective-permute-start.11 = (bf16[8,4096]{1,0:T(8,128)(2,1)S(1)}, bf16[8,4096]{1,0:T(8,128)(2,1)S(1)}, u32[]{:S(2)}, u32[]{:S(2)}) collective-permute-start(bf16[8,4096]{1,0:T(8,128)(2,1)S(1)} %collective-permute-done.7), channel_id=1, source_target_pairs={{0,4},{2,6},{4,0},{6,2},{8,12},{10,14},{12,8},{14,10},{1,3},{3,1},... | collective-permute-start | bytes 196616 | tf_op jit(solution)/shard_map/ppermute | solution.py:273
  32.3 3.1 %collective-permute-done.9 = bf16[8,4096]{1,0:T(8,128)(2,1)S(1)} collective-permute-done((bf16[8,4096]{1,0:T(8,128)(2,1)S(1)}, bf16[8,4096]{1,0:T(8,128)(2,1)S(1)}, u32[]{:S(2)}, u32[]{:S(2)}) %collective-permute-start.9) | collective-permute-done | bytes 65568 | tf_op jit(solution)/shard_map/ppermute | solution.py:273
  35.4 0.3 collective-permute-done.11
  35.8 1.7 %output.1 = f32[64,1024]{1,0:T(8,128)S(1)} custom-call(bf16[64,4096]{1,0:T(8,128)(2,1)S(1)} %constant_dynamic-update-slice_fusion.gathered, bf16[4096,1024]{1,0:T(8,128)(2,1)S(1)} %bitcast.1), custom_call_target="tpu_custom_call" | custom-call | tf_op jit(solution)/shard_map/output/pallas_call | solution.py:351
  37.6 1.5 %collective-permute-done.13 = f32[64,1024]{1,0:T(8,128)S(1)} collective-permute-done((f32[64,1024]{1,0:T(8,128)S(1)}, f32[64,1024]{1,0:T(8,128)S(1)}, u32[]{:S(2)}, u32[]{:S(2)}) %collective-permute-start.13) | collective-permute-done | bytes 262176 | tf_op jit(solution)/shard_map/ppermute | solution.py:359
  39.2 0.7 %fusion = (bf16[32,1024]{1,0:T(8,128)(2,1)}, bf16[32,1024]{1,0:T(8,128)(2,1)}) fusion(f32[64,1024]{1,0:T(8,128)S(1)} %add.13, bf16[32,1024]{1,0:T(8,128)(2,1)S(1)} %copy-done.4, bf16[32,1024]{1,0:T(8,128)(2,1)S(1)} %copy-done.3), kind=kLoop, calls=%fused_computation.1 | loop fusion | flops 196608 | bytes 524288 | tf_op jit(solution)/shard_map/convert_element_type | solution.py:362
  (40 shorter events, 0.5 us)
Async XLA Ops:
  0.6 12.5 %copy-start.5 = (s32[4]{0:T(128)S(1)}, s32[4]{0:T(128)}, u32[]{:S(2)}) copy-start(s32[4]{0:T(128)} %param.21) | copy-start | bytes 52
  0.6 19.2 %copy-start = (bf16[4,2,2048,128]{3,2,1,0:T(8,128)(2,1)S(1)}, bf16[4,2,2048,128]{3,2,1,0:T(8,128)(2,1)}, u32[]{:S(2)}) copy-start(bf16[4,2,2048,128]{3,2,1,0:T(8,128)(2,1)} %refs_6_.1) | copy-start | bytes 12582916
  0.7 19.2 %copy-start.1 = (bf16[4,2,2048,128]{3,2,1,0:T(8,128)(2,1)S(1)}, bf16[4,2,2048,128]{3,2,1,0:T(8,128)(2,1)}, u32[]{:S(2)}) copy-start(bf16[4,2,2048,128]{3,2,1,0:T(8,128)(2,1)} %refs_7_.1) | copy-start | bytes 12582916
  0.7 19.2 %copy-start.2 = (s32[4]{0:T(128)S(1)}, s32[4]{0:T(128)}, u32[]{:S(2)}) copy-start(s32[4]{0:T(128)} %lengths.1) | copy-start | bytes 52
  0.7 35.1 %slice-start = ((s8[8388608]{0:T(1024)(128)(4,1)}), s8[4194304]{0:T(1024)(128)(4,1)S(1)}, s32[]{:S(2)}) async-start(s8[8388608]{0:T(1024)(128)(4,1)} %bitcast), calls=%async_computation | async-start | bytes 8388608
  5.1 8.3 %collective-permute-start.3 = (bf16[8,4736]{1,0:T(8,128)(2,1)S(1)}, bf16[8,4736]{1,0:T(8,128)(2,1)S(1)}, u32[]{:S(2)}, u32[]{:S(2)}) collective-permute-start(bf16[8,4736]{1,0:T(8,128)(2,1)S(1)} %get-tuple-element.15), channel_id=1, source_target_pairs={{0,6},{2,4},{4,2},{6,0},{8,14},{10,12},{12,10},{14,8},{1,7},{3,5},... | collective-permute-start | bytes 227336 | tf_op jit(solution)/shard_map/ppermute | solution.py:273
  9.1 5.3 %collective-permute-start.4 = (bf16[8,4736]{1,0:T(8,128)(2,1)S(1)}, bf16[8,4736]{1,0:T(8,128)(2,1)S(1)}, u32[]{:S(2)}, u32[]{:S(2)}) collective-permute-start(bf16[8,4736]{1,0:T(8,128)(2,1)S(1)} %get-tuple-element.16), channel_id=1, source_target_pairs={{0,2},{2,0},{4,6},{6,4},{8,10},{10,8},{12,14},{14,12},{1,3},{3,1},... | collective-permute-start | bytes 227336 | tf_op jit(solution)/shard_map/ppermute | solution.py:273
  9.6 4.8 %collective-permute-start.5 = (bf16[8,4736]{1,0:T(8,128)(2,1)S(1)}, bf16[8,4736]{1,0:T(8,128)(2,1)S(1)}, u32[]{:S(2)}, u32[]{:S(2)}) collective-permute-start(bf16[8,4736]{1,0:T(8,128)(2,1)S(1)} %get-tuple-element.17), channel_id=1, source_target_pairs={{0,4},{2,6},{4,0},{6,2},{8,12},{10,14},{12,8},{14,10},{1,5},{3,7},... | collective-permute-start | bytes 227336 | tf_op jit(solution)/shard_map/ppermute | solution.py:273
  9.8 7.4 %collective-permute-start = (bf16[8,4736]{1,0:T(8,128)(2,1)S(1)}, bf16[8,4736]{1,0:T(8,128)(2,1)S(1)}, u32[]{:S(2)}, u32[]{:S(2)}) collective-permute-start(bf16[8,4736]{1,0:T(8,128)(2,1)S(1)} %get-tuple-element.11), channel_id=1, source_target_pairs={{0,6},{2,4},{4,2},{6,0},{8,14},{10,12},{12,10},{14,8},{1,7},{3,5},... | collective-permute-start | bytes 227336 | tf_op jit(solution)/shard_map/ppermute | solution.py:273
  12.6 4.6 %collective-permute-start.1 = (bf16[8,4736]{1,0:T(8,128)(2,1)S(1)}, bf16[8,4736]{1,0:T(8,128)(2,1)S(1)}, u32[]{:S(2)}, u32[]{:S(2)}) collective-permute-start(bf16[8,4736]{1,0:T(8,128)(2,1)S(1)} %get-tuple-element.12), channel_id=1, source_target_pairs={{0,2},{2,0},{4,6},{6,4},{8,10},{10,8},{12,14},{14,12},{1,3},{3,1},... | collective-permute-start | bytes 227336 | tf_op jit(solution)/shard_map/ppermute | solution.py:273
  13.4 4.7 %collective-permute-start.2 = (bf16[8,4736]{1,0:T(8,128)(2,1)S(1)}, bf16[8,4736]{1,0:T(8,128)(2,1)S(1)}, u32[]{:S(2)}, u32[]{:S(2)}) collective-permute-start(bf16[8,4736]{1,0:T(8,128)(2,1)S(1)} %get-tuple-element.13), channel_id=1, source_target_pairs={{0,4},{2,6},{4,0},{6,2},{8,12},{10,14},{12,8},{14,10},{1,5},{3,7},... | collective-permute-start | bytes 227336 | tf_op jit(solution)/shard_map/ppermute | solution.py:273
  14.5 5.3 %collective-permute-start.6 = (bf16[8,4736]{1,0:T(8,128)(2,1)S(1)}, bf16[8,4736]{1,0:T(8,128)(2,1)S(1)}, u32[]{:S(2)}, u32[]{:S(2)}) collective-permute-start(bf16[8,4736]{1,0:T(8,128)(2,1)S(1)} %combine.1), channel_id=1, source_target_pairs={{0,8},{2,10},{4,12},{6,14},{8,0},{10,2},{12,4},{14,6},{1,9},{3,11}... | collective-permute-start | bytes 227336 | tf_op jit(solution)/shard_map/ppermute | solution.py:273
  19.8 15.9 %slice-start.1 = ((s8[8388608]{0:T(1024)(128)(4,1)}), s8[4194304]{0:T(1024)(128)(4,1)S(1)}, s32[]{:S(2)}) async-start(s8[8388608]{0:T(1024)(128)(4,1)} %bitcast), calls=%async_computation.1 | async-start | bytes 8388608
  19.8 19.3 %copy-start.3 = (bf16[32,1024]{1,0:T(8,128)(2,1)S(1)}, bf16[32,1024]{1,0:T(8,128)(2,1)}, u32[]{:S(2)}) copy-start(bf16[32,1024]{1,0:T(8,128)(2,1)} %first.1) | copy-start | bytes 196612
  19.9 19.3 %copy-start.4 = (bf16[32,1024]{1,0:T(8,128)(2,1)S(1)}, bf16[32,1024]{1,0:T(8,128)(2,1)}, u32[]{:S(2)}) copy-start(bf16[32,1024]{1,0:T(8,128)(2,1)} %second.1) | copy-start | bytes 196612
  22.7 6.0 %collective-permute-start.7 = (bf16[8,4096]{1,0:T(8,128)(2,1)S(1)}, bf16[8,4096]{1,0:T(8,128)(2,1)S(1)}, u32[]{:S(2)}, u32[]{:S(2)}) collective-permute-start(bf16[8,4096]{1,0:T(8,128)(2,1)S(1)} %attend.1), channel_id=1, source_target_pairs={{0,8},{2,10},{4,12},{6,14},{8,0},{10,2},{12,4},{14,6},{1,9},{3,11}... | collective-permute-start | bytes 196616 | tf_op jit(solution)/shard_map/ppermute | solution.py:273
  25.4 6.9 %collective-permute-start.8 = (bf16[8,4096]{1,0:T(8,128)(2,1)S(1)}, bf16[8,4096]{1,0:T(8,128)(2,1)S(1)}, u32[]{:S(2)}, u32[]{:S(2)}) collective-permute-start(bf16[8,4096]{1,0:T(8,128)(2,1)S(1)} %attend.1), channel_id=1, source_target_pairs={{0,2},{2,0},{4,6},{6,4},{8,10},{10,8},{12,14},{14,12},{1,5},{3,7},... | collective-permute-start | bytes 196616 | tf_op jit(solution)/shard_map/ppermute | solution.py:273
  27.0 8.4 %collective-permute-start.10 = (bf16[8,4096]{1,0:T(8,128)(2,1)S(1)}, bf16[8,4096]{1,0:T(8,128)(2,1)S(1)}, u32[]{:S(2)}, u32[]{:S(2)}) collective-permute-start(bf16[8,4096]{1,0:T(8,128)(2,1)S(1)} %attend.1), channel_id=1, source_target_pairs={{0,4},{2,6},{4,0},{6,2},{8,12},{10,14},{12,8},{14,10},{1,3},{3,1},... | collective-permute-start | bytes 196616 | tf_op jit(solution)/shard_map/ppermute | solution.py:273
  28.8 7.0 %collective-permute-start.12 = (bf16[16,4096]{1,0:T(8,128)(2,1)S(1)}, bf16[16,4096]{1,0:T(8,128)(2,1)S(1)}, u32[]{:S(2)}, u32[]{:S(2)}) collective-permute-start(bf16[16,4096]{1,0:T(8,128)(2,1)S(1)} %pad_maximum_fusion), channel_id=1, source_target_pairs={{0,6},{2,4},{4,2},{6,0},{8,14},{10,12},{12,10},{14,8},{1,7},{3,5},... | collective-permute-start | bytes 393224 | tf_op jit(solution)/shard_map/ppermute | solution.py:273
  30.6 4.8 %collective-permute-start.9 = (bf16[8,4096]{1,0:T(8,128)(2,1)S(1)}, bf16[8,4096]{1,0:T(8,128)(2,1)S(1)}, u32[]{:S(2)}, u32[]{:S(2)}) collective-permute-start(bf16[8,4096]{1,0:T(8,128)(2,1)S(1)} %collective-permute-done.7), channel_id=1, source_target_pairs={{0,2},{2,0},{4,6},{6,4},{8,10},{10,8},{12,14},{14,12},{1,5},{3,7},... | collective-permute-start | bytes 196616 | tf_op jit(solution)/shard_map/ppermute | solution.py:273
  31.4 4.3 %collective-permute-start.11 = (bf16[8,4096]{1,0:T(8,128)(2,1)S(1)}, bf16[8,4096]{1,0:T(8,128)(2,1)S(1)}, u32[]{:S(2)}, u32[]{:S(2)}) collective-permute-start(bf16[8,4096]{1,0:T(8,128)(2,1)S(1)} %collective-permute-done.7), channel_id=1, source_target_pairs={{0,4},{2,6},{4,0},{6,2},{8,12},{10,14},{12,8},{14,10},{1,3},{3,1},... | collective-permute-start | bytes 196616 | tf_op jit(solution)/shard_map/ppermute | solution.py:273
  37.5 1.6 %collective-permute-start.13 = (f32[64,1024]{1,0:T(8,128)S(1)}, f32[64,1024]{1,0:T(8,128)S(1)}, u32[]{:S(2)}, u32[]{:S(2)}) collective-permute-start(f32[64,1024]{1,0:T(8,128)S(1)} %output.1), channel_id=1, source_target_pairs={{0,1},{1,0},{2,3},{3,2},{4,5},{5,4},{6,7},{7,6},{8,9},{9,8},{10,11... | collective-permute-start | bytes 786440 | tf_op jit(solution)/shard_map/ppermute | solution.py:359

commit v5 on v4

--- a/solution.py
+++ b/solution.py
@@ -126,7 +126,7 @@
         send[:, width:] = coded[begin : begin + both].astype(BF16)
 
 
-def attend_kernel(parts, model_width, lengths, mine, *refs):
+def attend_kernel(parts, model_width, bias, mine, *refs):
     received = refs[:parts]
     (
         cosine,
@@ -169,7 +169,7 @@
             [head(heads + kv_heads + index), blank], axis=0
         ).astype(BF16)
 
-    factor = 1.0 / math.sqrt(width)
+    factor = math.log2(math.e) / math.sqrt(width)
     contract = (((1,), (1,)), ((), ()))
 
     pairs = [(row, index) for row in range(rows_dev) for index in range(kv_heads)]
@@ -180,17 +180,15 @@
         query = jnp.concatenate(
             [queries[pick, row, :], queries[pick, rows_dev + row, :]], axis=0
         ).astype(BF16)
-        new = lax.dot_general(query, new_keys[index], contract, preferred_element_type=F32) * factor
+        new = lax.dot_general(query, new_keys[index], contract, preferred_element_type=F32)
         slot = lax.broadcasted_iota(jnp.int32, new.shape, 1)
         token = lax.broadcasted_iota(jnp.int32, new.shape, 0) // group
         seen = (lax.rem(slot, rows_dev) == row) & (slot // rows_dev <= token) & (slot < both)
         new = jnp.where(seen, new, NEGATIVE)
-        cached = (
-            lax.dot_general(query, key_cache[row, index], contract, preferred_element_type=F32)
-            * factor
+        cached = lax.dot_general(
+            query, key_cache[row, index], contract, preferred_element_type=F32
         )
-        live = lax.broadcasted_iota(jnp.int32, cached.shape, 1) < lengths[row]
-        cached = jnp.where(live, cached, NEGATIVE)
+        cached = cached + bias[row : row + 1, :]
         scores[number] = cached
         tops.append(
             jnp.maximum(
@@ -200,8 +198,8 @@
         fresh.append(new)
     for number, (row, index) in enumerate(pairs):
         pick = slice(index * group, (index + 1) * group)
-        weight = jnp.exp(scores[number] - tops[number])
-        new = jnp.exp(fresh[number] - tops[number])
+        weight = jnp.exp2((scores[number] - tops[number]) * factor)
+        new = jnp.exp2((fresh[number] - tops[number]) * factor)
         total = jnp.sum(weight, axis=1, keepdims=True) + jnp.sum(new, axis=1, keepdims=True)
         mixed = jnp.dot(
             weight.astype(BF16), value_cache[row, index], preferred_element_type=F32
@@ -322,10 +320,12 @@
     ]
 
     cosine, sine = rotary(positions, width)
+    slot = lax.broadcasted_iota(jnp.int32, (rows_dev, slots), 1)
+    bias = jnp.where(slot < lengths[:, None], 0.0, NEGATIVE)
     attended = pl.pallas_call(
         functools.partial(attend_kernel, len(received), devices * depth),
         out_shape=jax.ShapeDtypeStruct((both, heads * width), BF16),
-        in_specs=[whole(pltpu.SMEM)] + [whole()] * (len(received) + 5),
+        in_specs=[whole()] * (len(received) + 6),
         out_specs=whole(),
         scratch_shapes=[
             pltpu.VMEM((heads, both, width), F32),
@@ -336,7 +336,7 @@
         ],
         compiler_params=pltpu.CompilerParams(vmem_limit_bytes=32 * MIB),
         name="attend",
-    )(lengths, near_far[0], *received, cosine, sine, *placed(pltpu.VMEM, key_cache, value_cache))
+    )(bias, near_far[0], *received, cosine, sine, *placed(pltpu.VMEM, key_cache, value_cache))
 
     far = [exchange(attended, (inner * step,) * 2) for step in range(1, outer)]
     far = jnp.concatenate(far, axis=0)

time: 40 us -> 39.6 us (0.990)
  no operation moved by 1% of the time
where the time goes in v5:
time: 39.6 us; the launch traced here: 39.5 us
  starting transfers between devices  20.9 us (53%)
  Pallas kernels  8.72 us (22%)
  waiting for transfers between devices  7.83 us (20%)
  other arithmetic  1.07 us (3%)
  between operations  0.83 us (2%)
    ppermute x13, starting transfers between devices, exchange(): return lax.ppermute(value, ('wide', 'narrow'), pairs)  20.9 us
    ppermute x13, waiting for transfers between devices, exchange(): return lax.ppermute(value, ('wide', 'narrow'), pairs)  6.31 us
    pallas_call x1, Pallas kernels, on_device(): pl.pallas_call(functools.partial(project_kernel, rows_dev, outer, plans),...  4.4 us
    pallas_call x1, Pallas kernels, on_device(): pl.pallas_call(functools.partial(attend_kernel, len(received), devices *...  2.46 us
    pallas_call x1, Pallas kernels, on_device(): pl.pallas_call(functools.partial(output_kernel, rows_dev, outer, gather_p...  1.76 us
    ppermute x1, waiting for transfers between devices, on_device(): lax.ppermute(part, 'narrow', [(c, c ^ 1) for c in range(cores)])  1.52 us
  transfers between devices with their start and end apart: 14, of which 6 were waited for; matrix products, arithmetic and copies ran while one was open for 1% of the time, Pallas kernels for 0%

profile of v5, /device:TPU:0, one launch (start us, length us, event | category | flops | bytes accessed | tf_op | source)
XLA Modules:
  0.0 39.5 jit_solution(10043686587215774573)
XLA Ops:
  0.7 4.4 %project.1 = (f32[8,4736]{1,0:T(8,128)S(1)}, bf16[8,4736]{1,0:T(8,128)(2,1)S(1)}, bf16[8,4736]{1,0:T(8,128)(2,1)S(1)}, bf16[8,4736]{1,0:T(8,128)(2,1)S(1)}, f32[...) custom-call(bf16[32,1024]{1,0:T(8,128)(2,1)} %first.1, ...), custom_call_target="tpu_custom_call" | custom-call | flops 620756992 | bytes 9699328 | tf_op jit(solution)/shard_map/project/pallas_call | solution.py:278
  5.1 4.0 %collective-permute-start.3 = (bf16[8,4736]{1,0:T(8,128)(2,1)S(1)}, bf16[8,4736]{1,0:T(8,128)(2,1)S(1)}, u32[]{:S(2)}, u32[]{:S(2)}) collective-permute-start(bf16[8,4736]{1,0:T(8,128)(2,1)S(1)} %get-tuple-element.15), channel_id=1, source_target_pairs={{0,6},{2,4},{4,2},{6,0},{8,14},{10,12},{12,10},{14,8},{1,7},{3,5},... | collective-permute-start | bytes 227336 | tf_op jit(solution)/shard_map/ppermute | solution.py:271
  9.1 0.5 %collective-permute-start.4 = (bf16[8,4736]{1,0:T(8,128)(2,1)S(1)}, bf16[8,4736]{1,0:T(8,128)(2,1)S(1)}, u32[]{:S(2)}, u32[]{:S(2)}) collective-permute-start(bf16[8,4736]{1,0:T(8,128)(2,1)S(1)} %get-tuple-element.16), channel_id=1, source_target_pairs={{0,2},{2,0},{4,6},{6,4},{8,10},{10,8},{12,14},{14,12},{1,3},{3,1},... | collective-permute-start | bytes 227336 | tf_op jit(solution)/shard_map/ppermute | solution.py:271
  9.6 0.1 collective-permute-start.5
  9.8 2.8 %collective-permute-start = (bf16[8,4736]{1,0:T(8,128)(2,1)S(1)}, bf16[8,4736]{1,0:T(8,128)(2,1)S(1)}, u32[]{:S(2)}, u32[]{:S(2)}) collective-permute-start(bf16[8,4736]{1,0:T(8,128)(2,1)S(1)} %get-tuple-element.11), channel_id=1, source_target_pairs={{0,6},{2,4},{4,2},{6,0},{8,14},{10,12},{12,10},{14,8},{1,7},{3,5},... | collective-permute-start | bytes 227336 | tf_op jit(solution)/shard_map/ppermute | solution.py:271
  12.6 0.5 %collective-permute-start.1 = (bf16[8,4736]{1,0:T(8,128)(2,1)S(1)}, bf16[8,4736]{1,0:T(8,128)(2,1)S(1)}, u32[]{:S(2)}, u32[]{:S(2)}) collective-permute-start(bf16[8,4736]{1,0:T(8,128)(2,1)S(1)} %get-tuple-element.12), channel_id=1, source_target_pairs={{0,2},{2,0},{4,6},{6,4},{8,10},{10,8},{12,14},{14,12},{1,3},{3,1},... | collective-permute-start | bytes 227336 | tf_op jit(solution)/shard_map/ppermute | solution.py:271
  13.3 0.1 fusion.3
  13.4 0.6 %collective-permute-start.2 = (bf16[8,4736]{1,0:T(8,128)(2,1)S(1)}, bf16[8,4736]{1,0:T(8,128)(2,1)S(1)}, u32[]{:S(2)}, u32[]{:S(2)}) collective-permute-start(bf16[8,4736]{1,0:T(8,128)(2,1)S(1)} %get-tuple-element.13), channel_id=1, source_target_pairs={{0,4},{2,6},{4,0},{6,2},{8,12},{10,14},{12,8},{14,10},{1,5},{3,7},... | collective-permute-start | bytes 227336 | tf_op jit(solution)/shard_map/ppermute | solution.py:271
  14.0 0.4 %collective-permute-done.4.refs_1_ = bf16[8,4736]{1,0:T(8,128)(2,1)S(1)} collective-permute-done((bf16[8,4736]{1,0:T(8,128)(2,1)S(1)}, bf16[8,4736]{1,0:T(8,128)(2,1)S(1)}, u32[]{:S(2)}, u32[]{:S(2)}) %collective-permute-start.4) | collective-permute-done | bytes 75808 | tf_op jit(solution)/shard_map/ppermute | solution.py:271
  14.5 2.6 %collective-permute-start.6 = (bf16[8,4736]{1,0:T(8,128)(2,1)S(1)}, bf16[8,4736]{1,0:T(8,128)(2,1)S(1)}, u32[]{:S(2)}, u32[]{:S(2)}) collective-permute-start(bf16[8,4736]{1,0:T(8,128)(2,1)S(1)} %combine.1), channel_id=1, source_target_pairs={{0,8},{2,10},{4,12},{6,14},{8,0},{10,2},{12,4},{14,6},{1,9},{3,11}... | collective-permute-start | bytes 227336 | tf_op jit(solution)/shard_map/ppermute | solution.py:271
  17.2 0.9 %collective-permute-done.2.refs_2_ = bf16[8,4736]{1,0:T(8,128)(2,1)S(1)} collective-permute-done((bf16[8,4736]{1,0:T(8,128)(2,1)S(1)}, bf16[8,4736]{1,0:T(8,128)(2,1)S(1)}, u32[]{:S(2)}, u32[]{:S(2)}) %collective-permute-start.2) | collective-permute-done | bytes 75808 | tf_op jit(solution)/shard_map/ppermute | solution.py:271
  18.1 1.7 %collective-permute-done.6.refs_3_ = bf16[8,4736]{1,0:T(8,128)(2,1)S(1)} collective-permute-done((bf16[8,4736]{1,0:T(8,128)(2,1)S(1)}, bf16[8,4736]{1,0:T(8,128)(2,1)S(1)}, u32[]{:S(2)}, u32[]{:S(2)}) %collective-permute-start.6) | collective-permute-done | bytes 75808 | tf_op jit(solution)/shard_map/ppermute | solution.py:271
  19.8 2.5 %attend.1 = bf16[8,4096]{1,0:T(8,128)(2,1)S(1)} custom-call(f32[4,2048]{1,0:T(4,128)S(1)} %fusion.2.bias, f32[8,4736]{1,0:T(8,128)S(1)} %get-tuple-element.10.mine, bf16[8,4736]{1,0:T(8,128)(2,1)S(1)} %collective-permute-done.refs_0_, bf16[8,4736]{1,0:T(8,128)(2,1)S(1)} %collective-permute-done.1.refs_1_, ...), custom_call_target="tpu_custom_call" | custom-call | tf_op jit(solution)/shard_map/attend/pallas_call | solution.py:325
  22.3 2.7 %collective-permute-start.7 = (bf16[8,4096]{1,0:T(8,128)(2,1)S(1)}, bf16[8,4096]{1,0:T(8,128)(2,1)S(1)}, u32[]{:S(2)}, u32[]{:S(2)}) collective-permute-start(bf16[8,4096]{1,0:T(8,128)(2,1)S(1)} %attend.1), channel_id=1, source_target_pairs={{0,8},{2,10},{4,12},{6,14},{8,0},{10,2},{12,4},{14,6},{1,9},{3,11}... | collective-permute-start | bytes 196616 | tf_op jit(solution)/shard_map/ppermute | solution.py:271
  25.0 1.5 %collective-permute-start.8 = (bf16[8,4096]{1,0:T(8,128)(2,1)S(1)}, bf16[8,4096]{1,0:T(8,128)(2,1)S(1)}, u32[]{:S(2)}, u32[]{:S(2)}) collective-permute-start(bf16[8,4096]{1,0:T(8,128)(2,1)S(1)} %attend.1), channel_id=1, source_target_pairs={{0,2},{2,0},{4,6},{6,4},{8,10},{10,8},{12,14},{14,12},{1,5},{3,7},... | collective-permute-start | bytes 196616 | tf_op jit(solution)/shard_map/ppermute | solution.py:271
  26.6 1.8 %collective-permute-start.10 = (bf16[8,4096]{1,0:T(8,128)(2,1)S(1)}, bf16[8,4096]{1,0:T(8,128)(2,1)S(1)}, u32[]{:S(2)}, u32[]{:S(2)}) collective-permute-start(bf16[8,4096]{1,0:T(8,128)(2,1)S(1)} %attend.1), channel_id=1, source_target_pairs={{0,4},{2,6},{4,0},{6,2},{8,12},{10,14},{12,8},{14,10},{1,3},{3,1},... | collective-permute-start | bytes 196616 | tf_op jit(solution)/shard_map/ppermute | solution.py:271
  28.4 1.8 %collective-permute-start.12 = (bf16[16,4096]{1,0:T(8,128)(2,1)S(1)}, bf16[16,4096]{1,0:T(8,128)(2,1)S(1)}, u32[]{:S(2)}, u32[]{:S(2)}) collective-permute-start(bf16[16,4096]{1,0:T(8,128)(2,1)S(1)} %pad_maximum_fusion), channel_id=1, source_target_pairs={{0,6},{2,4},{4,2},{6,0},{8,14},{10,12},{12,10},{14,8},{1,7},{3,5},... | collective-permute-start | bytes 393224 | tf_op jit(solution)/shard_map/ppermute | solution.py:271
  30.3 0.8 %collective-permute-start.9 = (bf16[8,4096]{1,0:T(8,128)(2,1)S(1)}, bf16[8,4096]{1,0:T(8,128)(2,1)S(1)}, u32[]{:S(2)}, u32[]{:S(2)}) collective-permute-start(bf16[8,4096]{1,0:T(8,128)(2,1)S(1)} %collective-permute-done.7), channel_id=1, source_target_pairs={{0,2},{2,0},{4,6},{6,4},{8,10},{10,8},{12,14},{14,12},{1,5},{3,7},... | collective-permute-start | bytes 196616 | tf_op jit(solution)/shard_map/ppermute | solution.py:271
  31.0 1.0 %collective-permute-start.11 = (bf16[8,4096]{1,0:T(8,128)(2,1)S(1)}, bf16[8,4096]{1,0:T(8,128)(2,1)S(1)}, u32[]{:S(2)}, u32[]{:S(2)}) collective-permute-start(bf16[8,4096]{1,0:T(8,128)(2,1)S(1)} %collective-permute-done.7), channel_id=1, source_target_pairs={{0,4},{2,6},{4,0},{6,2},{8,12},{10,14},{12,8},{14,10},{1,3},{3,1},... | collective-permute-start | bytes 196616 | tf_op jit(solution)/shard_map/ppermute | solution.py:271
  32.0 3.1 %collective-permute-done.9 = bf16[8,4096]{1,0:T(8,128)(2,1)S(1)} collective-permute-done((bf16[8,4096]{1,0:T(8,128)(2,1)S(1)}, bf16[8,4096]{1,0:T(8,128)(2,1)S(1)}, u32[]{:S(2)}, u32[]{:S(2)}) %collective-permute-start.9) | collective-permute-done | bytes 65568 | tf_op jit(solution)/shard_map/ppermute | solution.py:271
  35.1 0.2 collective-permute-done.11
  35.4 1.8 %output.1 = f32[64,1024]{1,0:T(8,128)S(1)} custom-call(bf16[64,4096]{1,0:T(8,128)(2,1)S(1)} %constant_dynamic-update-slice_fusion.gathered, bf16[4096,1024]{1,0:T(8,128)(2,1)S(1)} %bitcast.1), custom_call_target="tpu_custom_call" | custom-call | tf_op jit(solution)/shard_map/output/pallas_call | solution.py:351
  37.2 1.5 %collective-permute-done.13 = f32[64,1024]{1,0:T(8,128)S(1)} collective-permute-done((f32[64,1024]{1,0:T(8,128)S(1)}, f32[64,1024]{1,0:T(8,128)S(1)}, u32[]{:S(2)}, u32[]{:S(2)}) %collective-permute-start.13) | collective-permute-done | bytes 262176 | tf_op jit(solution)/shard_map/ppermute | solution.py:359
  38.8 0.7 %fusion = (bf16[32,1024]{1,0:T(8,128)(2,1)}, bf16[32,1024]{1,0:T(8,128)(2,1)}) fusion(f32[64,1024]{1,0:T(8,128)S(1)} %add.13, bf16[32,1024]{1,0:T(8,128)(2,1)S(1)} %copy-done.3, bf16[32,1024]{1,0:T(8,128)(2,1)S(1)} %copy-done.2), kind=kLoop, calls=%fused_computation.1 | loop fusion | flops 196608 | bytes 524288 | tf_op jit(solution)/shard_map/convert_element_type | solution.py:362
  (41 shorter events, 0.5 us)
Async XLA Ops:
  0.6 12.5 %copy-start.5 = (s32[4]{0:T(128)S(1)}, s32[4]{0:T(128)}, u32[]{:S(2)}) copy-start(s32[4]{0:T(128)} %param.21) | copy-start | bytes 52
  0.6 12.6 %copy-start.4 = (s32[4]{0:T(128)S(1)}, s32[4]{0:T(128)}, u32[]{:S(2)}) copy-start(s32[4]{0:T(128)} %param.20) | copy-start | bytes 52
  0.7 19.2 %copy-start = (bf16[4,2,2048,128]{3,2,1,0:T(8,128)(2,1)S(1)}, bf16[4,2,2048,128]{3,2,1,0:T(8,128)(2,1)}, u32[]{:S(2)}) copy-start(bf16[4,2,2048,128]{3,2,1,0:T(8,128)(2,1)} %refs_6_.1) | copy-start | bytes 12582916
  0.7 19.2 %copy-start.1 = (bf16[4,2,2048,128]{3,2,1,0:T(8,128)(2,1)S(1)}, bf16[4,2,2048,128]{3,2,1,0:T(8,128)(2,1)}, u32[]{:S(2)}) copy-start(bf16[4,2,2048,128]{3,2,1,0:T(8,128)(2,1)} %refs_7_.1) | copy-start | bytes 12582916
  0.7 34.7 %slice-start = ((s8[8388608]{0:T(1024)(128)(4,1)}), s8[4194304]{0:T(1024)(128)(4,1)S(1)}, s32[]{:S(2)}) async-start(s8[8388608]{0:T(1024)(128)(4,1)} %bitcast), calls=%async_computation | async-start | bytes 8388608
  5.1 8.3 %collective-permute-start.3 = (bf16[8,4736]{1,0:T(8,128)(2,1)S(1)}, bf16[8,4736]{1,0:T(8,128)(2,1)S(1)}, u32[]{:S(2)}, u32[]{:S(2)}) collective-permute-start(bf16[8,4736]{1,0:T(8,128)(2,1)S(1)} %get-tuple-element.15), channel_id=1, source_target_pairs={{0,6},{2,4},{4,2},{6,0},{8,14},{10,12},{12,10},{14,8},{1,7},{3,5},... | collective-permute-start | bytes 227336 | tf_op jit(solution)/shard_map/ppermute | solution.py:271
  9.1 5.3 %collective-permute-start.4 = (bf16[8,4736]{1,0:T(8,128)(2,1)S(1)}, bf16[8,4736]{1,0:T(8,128)(2,1)S(1)}, u32[]{:S(2)}, u32[]{:S(2)}) collective-permute-start(bf16[8,4736]{1,0:T(8,128)(2,1)S(1)} %get-tuple-element.16), channel_id=1, source_target_pairs={{0,2},{2,0},{4,6},{6,4},{8,10},{10,8},{12,14},{14,12},{1,3},{3,1},... | collective-permute-start | bytes 227336 | tf_op jit(solution)/shard_map/ppermute | solution.py:271
  9.6 4.8 %collective-permute-start.5 = (bf16[8,4736]{1,0:T(8,128)(2,1)S(1)}, bf16[8,4736]{1,0:T(8,128)(2,1)S(1)}, u32[]{:S(2)}, u32[]{:S(2)}) collective-permute-start(bf16[8,4736]{1,0:T(8,128)(2,1)S(1)} %get-tuple-element.17), channel_id=1, source_target_pairs={{0,4},{2,6},{4,0},{6,2},{8,12},{10,14},{12,8},{14,10},{1,5},{3,7},... | collective-permute-start | bytes 227336 | tf_op jit(solution)/shard_map/ppermute | solution.py:271
  9.8 7.4 %collective-permute-start = (bf16[8,4736]{1,0:T(8,128)(2,1)S(1)}, bf16[8,4736]{1,0:T(8,128)(2,1)S(1)}, u32[]{:S(2)}, u32[]{:S(2)}) collective-permute-start(bf16[8,4736]{1,0:T(8,128)(2,1)S(1)} %get-tuple-element.11), channel_id=1, source_target_pairs={{0,6},{2,4},{4,2},{6,0},{8,14},{10,12},{12,10},{14,8},{1,7},{3,5},... | collective-permute-start | bytes 227336 | tf_op jit(solution)/shard_map/ppermute | solution.py:271
  12.6 4.6 %collective-permute-start.1 = (bf16[8,4736]{1,0:T(8,128)(2,1)S(1)}, bf16[8,4736]{1,0:T(8,128)(2,1)S(1)}, u32[]{:S(2)}, u32[]{:S(2)}) collective-permute-start(bf16[8,4736]{1,0:T(8,128)(2,1)S(1)} %get-tuple-element.12), channel_id=1, source_target_pairs={{0,2},{2,0},{4,6},{6,4},{8,10},{10,8},{12,14},{14,12},{1,3},{3,1},... | collective-permute-start | bytes 227336 | tf_op jit(solution)/shard_map/ppermute | solution.py:271
  13.4 4.7 %collective-permute-start.2 = (bf16[8,4736]{1,0:T(8,128)(2,1)S(1)}, bf16[8,4736]{1,0:T(8,128)(2,1)S(1)}, u32[]{:S(2)}, u32[]{:S(2)}) collective-permute-start(bf16[8,4736]{1,0:T(8,128)(2,1)S(1)} %get-tuple-element.13), channel_id=1, source_target_pairs={{0,4},{2,6},{4,0},{6,2},{8,12},{10,14},{12,8},{14,10},{1,5},{3,7},... | collective-permute-start | bytes 227336 | tf_op jit(solution)/shard_map/ppermute | solution.py:271
  14.5 5.3 %collective-permute-start.6 = (bf16[8,4736]{1,0:T(8,128)(2,1)S(1)}, bf16[8,4736]{1,0:T(8,128)(2,1)S(1)}, u32[]{:S(2)}, u32[]{:S(2)}) collective-permute-start(bf16[8,4736]{1,0:T(8,128)(2,1)S(1)} %combine.1), channel_id=1, source_target_pairs={{0,8},{2,10},{4,12},{6,14},{8,0},{10,2},{12,4},{14,6},{1,9},{3,11}... | collective-permute-start | bytes 227336 | tf_op jit(solution)/shard_map/ppermute | solution.py:271
  19.8 15.5 %slice-start.1 = ((s8[8388608]{0:T(1024)(128)(4,1)}), s8[4194304]{0:T(1024)(128)(4,1)S(1)}, s32[]{:S(2)}) async-start(s8[8388608]{0:T(1024)(128)(4,1)} %bitcast), calls=%async_computation.1 | async-start | bytes 8388608
  19.8 18.9 %copy-start.2 = (bf16[32,1024]{1,0:T(8,128)(2,1)S(1)}, bf16[32,1024]{1,0:T(8,128)(2,1)}, u32[]{:S(2)}) copy-start(bf16[32,1024]{1,0:T(8,128)(2,1)} %first.1) | copy-start | bytes 196612
  19.8 18.9 %copy-start.3 = (bf16[32,1024]{1,0:T(8,128)(2,1)S(1)}, bf16[32,1024]{1,0:T(8,128)(2,1)}, u32[]{:S(2)}) copy-start(bf16[32,1024]{1,0:T(8,128)(2,1)} %second.1) | copy-start | bytes 196612
  22.3 6.1 %collective-permute-start.7 = (bf16[8,4096]{1,0:T(8,128)(2,1)S(1)}, bf16[8,4096]{1,0:T(8,128)(2,1)S(1)}, u32[]{:S(2)}, u32[]{:S(2)}) collective-permute-start(bf16[8,4096]{1,0:T(8,128)(2,1)S(1)} %attend.1), channel_id=1, source_target_pairs={{0,8},{2,10},{4,12},{6,14},{8,0},{10,2},{12,4},{14,6},{1,9},{3,11}... | collective-permute-start | bytes 196616 | tf_op jit(solution)/shard_map/ppermute | solution.py:271
  25.0 7.0 %collective-permute-start.8 = (bf16[8,4096]{1,0:T(8,128)(2,1)S(1)}, bf16[8,4096]{1,0:T(8,128)(2,1)S(1)}, u32[]{:S(2)}, u32[]{:S(2)}) collective-permute-start(bf16[8,4096]{1,0:T(8,128)(2,1)S(1)} %attend.1), channel_id=1, source_target_pairs={{0,2},{2,0},{4,6},{6,4},{8,10},{10,8},{12,14},{14,12},{1,5},{3,7},... | collective-permute-start | bytes 196616 | tf_op jit(solution)/shard_map/ppermute | solution.py:271
  26.6 8.5 %collective-permute-start.10 = (bf16[8,4096]{1,0:T(8,128)(2,1)S(1)}, bf16[8,4096]{1,0:T(8,128)(2,1)S(1)}, u32[]{:S(2)}, u32[]{:S(2)}) collective-permute-start(bf16[8,4096]{1,0:T(8,128)(2,1)S(1)} %attend.1), channel_id=1, source_target_pairs={{0,4},{2,6},{4,0},{6,2},{8,12},{10,14},{12,8},{14,10},{1,3},{3,1},... | collective-permute-start | bytes 196616 | tf_op jit(solution)/shard_map/ppermute | solution.py:271
  28.4 6.9 %collective-permute-start.12 = (bf16[16,4096]{1,0:T(8,128)(2,1)S(1)}, bf16[16,4096]{1,0:T(8,128)(2,1)S(1)}, u32[]{:S(2)}, u32[]{:S(2)}) collective-permute-start(bf16[16,4096]{1,0:T(8,128)(2,1)S(1)} %pad_maximum_fusion), channel_id=1, source_target_pairs={{0,6},{2,4},{4,2},{6,0},{8,14},{10,12},{12,10},{14,8},{1,7},{3,5},... | collective-permute-start | bytes 393224 | tf_op jit(solution)/shard_map/ppermute | solution.py:271
  30.3 4.8 %collective-permute-start.9 = (bf16[8,4096]{1,0:T(8,128)(2,1)S(1)}, bf16[8,4096]{1,0:T(8,128)(2,1)S(1)}, u32[]{:S(2)}, u32[]{:S(2)}) collective-permute-start(bf16[8,4096]{1,0:T(8,128)(2,1)S(1)} %collective-permute-done.7), channel_id=1, source_target_pairs={{0,2},{2,0},{4,6},{6,4},{8,10},{10,8},{12,14},{14,12},{1,5},{3,7},... | collective-permute-start | bytes 196616 | tf_op jit(solution)/shard_map/ppermute | solution.py:271
  31.0 4.3 %collective-permute-start.11 = (bf16[8,4096]{1,0:T(8,128)(2,1)S(1)}, bf16[8,4096]{1,0:T(8,128)(2,1)S(1)}, u32[]{:S(2)}, u32[]{:S(2)}) collective-permute-start(bf16[8,4096]{1,0:T(8,128)(2,1)S(1)} %collective-permute-done.7), channel_id=1, source_target_pairs={{0,4},{2,6},{4,0},{6,2},{8,12},{10,14},{12,8},{14,10},{1,3},{3,1},... | collective-permute-start | bytes 196616 | tf_op jit(solution)/shard_map/ppermute | solution.py:271
  37.1 1.6 %collective-permute-start.13 = (f32[64,1024]{1,0:T(8,128)S(1)}, f32[64,1024]{1,0:T(8,128)S(1)}, u32[]{:S(2)}, u32[]{:S(2)}) collective-permute-start(f32[64,1024]{1,0:T(8,128)S(1)} %output.1), channel_id=1, source_target_pairs={{0,1},{1,0},{2,3},{3,2},{4,5},{5,4},{6,7},{7,6},{8,9},{9,8},{10,11... | collective-permute-start | bytes 786440 | tf_op jit(solution)/shard_map/ppermute | solution.py:359

commit v6 on v5

--- a/solution.py
+++ b/solution.py
@@ -17,6 +17,9 @@
 
 F32 = jnp.float32
 BF16 = jnp.bfloat16
+LINK = jnp.float16
+LIFT = 16.0
+DROP = 0.125
 
 
 def one_hot(shape, order_axis, plans, outer, rows_dev, rows):
@@ -71,8 +74,8 @@
     block = outer * both
     pick = one_hot((2 * rows, 2 * rows), 0, plans, outer, rows_dev, rows)
     ordered = jnp.dot(pick, tokens[...], preferred_element_type=F32)
-    squares = jnp.sum(ordered * ordered, axis=1, keepdims=True)
-    scaled[...] = (ordered * gains[...].astype(F32)[None, :]).astype(BF16)
+    squares = jnp.sum(ordered * ordered, axis=1, keepdims=True) * DROP
+    scaled[...] = (ordered * gains[...].astype(F32)[None, :]).astype(BF16) * LIFT
 
     def put(start, width, value, coded):
         for index, (near, far) in enumerate(zip(nears, fars)):
@@ -122,8 +125,8 @@
     coded = encoded(tail)
     for index, send in enumerate(sends):
         begin = index * both
-        send[:, :width] = total[begin : begin + both].astype(BF16)
-        send[:, width:] = coded[begin : begin + both].astype(BF16)
+        send[:, :width] = total[begin : begin + both]
+        send[:, width:] = coded[begin : begin + both]
 
 
 def attend_kernel(parts, model_width, bias, mine, *refs):
@@ -148,7 +151,7 @@
     tail = mine[:, end:]
     for part in received:
         tail = tail + decoded(part[:, end:])
-    scale = lax.rsqrt(tail / model_width + EPSILON)
+    scale = lax.rsqrt(tail / (DROP * model_width) + EPSILON) / LIFT
 
     def head(index):
         columns = slice(index * width, (index + 1) * width)
@@ -172,41 +175,59 @@
     factor = math.log2(math.e) / math.sqrt(width)
     contract = (((1,), (1,)), ((), ()))
 
-    pairs = [(row, index) for row in range(rows_dev) for index in range(kv_heads)]
     tops = []
     fresh = []
-    for number, (row, index) in enumerate(pairs):
-        pick = slice(index * group, (index + 1) * group)
-        query = jnp.concatenate(
-            [queries[pick, row, :], queries[pick, rows_dev + row, :]], axis=0
-        ).astype(BF16)
-        new = lax.dot_general(query, new_keys[index], contract, preferred_element_type=F32)
+    for row in range(rows_dev):
+        own = []
+        for index in range(kv_heads):
+            pick = slice(index * group, (index + 1) * group)
+            own.append(
+                jnp.concatenate(
+                    [queries[pick, row, :], queries[pick, rows_dev + row, :]], axis=0
+                ).astype(BF16)
+            )
+        cached = jnp.concatenate(
+            [
+                lax.dot_general(own[index], key_cache[row, index], contract, preferred_element_type=F32)
+                for index in range(kv_heads)
+            ],
+            axis=0,
+        )
+        cached = cached + bias[row : row + 1, :]
+        scores[row] = cached
+        new = jnp.concatenate(
+            [
+                lax.dot_general(own[index], new_keys[index], contract, preferred_element_type=F32)
+                for index in range(kv_heads)
+            ],
+            axis=0,
+        )
         slot = lax.broadcasted_iota(jnp.int32, new.shape, 1)
-        token = lax.broadcasted_iota(jnp.int32, new.shape, 0) // group
+        token = lax.rem(lax.broadcasted_iota(jnp.int32, new.shape, 0) // group, 2)
         seen = (lax.rem(slot, rows_dev) == row) & (slot // rows_dev <= token) & (slot < both)
         new = jnp.where(seen, new, NEGATIVE)
-        cached = lax.dot_general(
-            query, key_cache[row, index], contract, preferred_element_type=F32
-        )
-        cached = cached + bias[row : row + 1, :]
-        scores[number] = cached
         tops.append(
             jnp.maximum(
                 jnp.max(cached, axis=1, keepdims=True), jnp.max(new, axis=1, keepdims=True)
             )
         )
         fresh.append(new)
-    for number, (row, index) in enumerate(pairs):
-        pick = slice(index * group, (index + 1) * group)
-        weight = jnp.exp2((scores[number] - tops[number]) * factor)
-        new = jnp.exp2((fresh[number] - tops[number]) * factor)
+    for row in range(rows_dev):
+        weight = jnp.exp2((scores[row] - tops[row]) * factor)
+        new = jnp.exp2((fresh[row] - tops[row]) * factor)
         total = jnp.sum(weight, axis=1, keepdims=True) + jnp.sum(new, axis=1, keepdims=True)
-        mixed = jnp.dot(
-            weight.astype(BF16), value_cache[row, index], preferred_element_type=F32
-        ) + jnp.dot(new.astype(BF16), new_values[index], preferred_element_type=F32)
-        mixed = mixed / total
-        results[pick, row, :] = mixed[:group]
-        results[pick, rows_dev + row, :] = mixed[group:]
+        weight = weight.astype(BF16)
+        new = new.astype(BF16)
+        values = jnp.concatenate([value_cache[row, index] for index in range(kv_heads)], axis=1)
+        mixed = jnp.dot(weight, values, preferred_element_type=F32)
+        for index in range(kv_heads):
+            pick = slice(index * group, (index + 1) * group)
+            span = slice(2 * index * group, 2 * (index + 1) * group)
+            part = mixed[span, index * width : (index + 1) * width]
+            part = part + jnp.dot(new[span], new_values[index], preferred_element_type=F32)
+            part = part / total[span]
+            results[pick, row, :] = part[:group]
+            results[pick, rows_dev + row, :] = part[group:]
 
     for index in range(heads):
         attended[:, index * width : (index + 1) * width] = results[index].astype(BF16)
@@ -274,7 +295,7 @@
         return [pltpu.with_memory_space_constraint(value, space) for value in values]
 
     chunks = w_query.shape[1] // CHUNK
-    types = [F32] + [BF16] * (inner - 1)
+    types = [F32] * inner
     near_far = pl.pallas_call(
         functools.partial(project_kernel, rows_dev, outer, plans),
         out_shape=[jax.ShapeDtypeStruct((both, columns), kind) for kind in types]
@@ -305,18 +326,22 @@
             for index, value in enumerate(values)
         ]
 
-    far = spread(near_far[inner + 1 :], plans)
-    near = spread(near_far[1:inner], plans)
+    def narrowed(values):
+        return [value.astype(LINK) for value in values]
+
+    far = [value.astype(F32) for value in spread(narrowed(near_far[inner + 1 :]), plans)]
+    near = [value.astype(F32) for value in spread(narrowed(near_far[1:inner]), plans)]
     sends = pl.pallas_call(
         functools.partial(combine_kernel, inner - 1),
-        out_shape=[jax.ShapeDtypeStruct((both, columns), BF16)] * (outer - 1),
+        out_shape=[jax.ShapeDtypeStruct((both, columns), F32)] * (outer - 1),
         in_specs=[whole()] * inner,
         out_specs=[whole()] * (outer - 1),
         compiler_params=pltpu.CompilerParams(vmem_limit_bytes=16 * MIB),
         name="combine",
     )(near_far[inner], *far)
     received = near + [
-        exchange(send, (inner * (index + 1),) * 2) for index, send in enumerate(sends)
+        exchange(send, (inner * (index + 1),) * 2).astype(F32)
+        for index, send in enumerate(narrowed(sends))
     ]
 
     cosine, sine = rotary(positions, width)
@@ -332,7 +357,7 @@
             pltpu.VMEM((kv_heads, 2 * both, width), BF16),
             pltpu.VMEM((kv_heads, 2 * both, width), BF16),
             pltpu.VMEM((heads, both, width), F32),
-            pltpu.VMEM((rows_dev * kv_heads, 2 * heads // kv_heads, slots), F32),
+            pltpu.VMEM((rows_dev, 2 * heads, slots), F32),
         ],
         compiler_params=pltpu.CompilerParams(vmem_limit_bytes=32 * MIB),
         name="attend",
@@ -356,7 +381,9 @@
         compiler_params=pltpu.CompilerParams(vmem_limit_bytes=24 * MIB),
         name="output",
     )(gathered, *placed(pltpu.VMEM, w_output))
-    total = part + lax.ppermute(part, "narrow", [(c, c ^ 1) for c in range(cores)])
+    part = (part * DROP).astype(LINK)
+    other = lax.ppermute(part, "narrow", [(c, cores - 1 - c) for c in range(cores)])
+    total = (part.astype(F32) + other.astype(F32)) / DROP
     return (
         (first_input.astype(F32) + total[:rows]).astype(BF16),
         (second_input.astype(F32) + total[rows:]).astype(BF16),

time: 39.6 us -> 39.6 us (level)
  no operation moved by 1% of the time
where the time goes in v6:
time: 39.6 us; the launch traced here: 39.4 us
  starting transfers between devices  20.9 us (53%)
  Pallas kernels  8.6 us (22%)
  waiting for transfers between devices  7.65 us (19%)
  other arithmetic  1.28 us (3%)
  between operations  0.95 us (2%)
    ppermute x13, starting transfers between devices, exchange(): return lax.ppermute(value, ('wide', 'narrow'), pairs)  20.8 us
    ppermute x13, waiting for transfers between devices, exchange(): return lax.ppermute(value, ('wide', 'narrow'), pairs)  6.32 us
    pallas_call x1, Pallas kernels, on_device(): pl.pallas_call(functools.partial(project_kernel, rows_dev, outer, plans),...  4.4 us
    pallas_call x1, Pallas kernels, on_device(): pl.pallas_call(functools.partial(attend_kernel, len(received), devices *...  2.36 us
    pallas_call x1, Pallas kernels, on_device(): pl.pallas_call(functools.partial(output_kernel, rows_dev, outer, gather_p...  1.76 us
    ppermute x1, waiting for transfers between devices, on_device(): lax.ppermute(part, 'narrow', [(c, cores - 1 - c) for c in range(cores)])  1.33 us
  transfers between devices with their start and end apart: 14, of which 6 were waited for; matrix products, arithmetic and copies ran while one was open for 1% of the time, Pallas kernels for 0%

profile of v6, /device:TPU:0, one launch (start us, length us, event | category | flops | bytes accessed | tf_op | source)
XLA Modules:
  0.0 39.4 jit_solution(10343328500567633701)
XLA Ops:
  0.7 4.4 %project.1 = (f32[8,4736]{1,0:T(8,128)S(1)}, f32[8,4736]{1,0:T(8,128)S(1)}, f32[8,4736]{1,0:T(8,128)S(1)}, f32[8,4736]{1,0:T(8,128)S(1)}, f32[8,4736]{1,0:T(8,12...) custom-call(bf16[32,1024]{1,0:T(8,128)(2,1)} %first.1, bf16[32,1024]{1,0:T(8,128)(2,1)} %second.1, ...), custom_call_target="tpu_custom_call" | custom-call | flops 620756992 | bytes 9699328 | tf_op jit(solution)/shard_map/project/pallas_call | solution.py:299
  5.1 4.0 %collective-permute-start.3 = (f16[8,4736]{1,0:T(8,128)(2,1)S(1)}, f16[8,4736]{1,0:T(8,128)(2,1)S(1)}, u32[]{:S(2)}, u32[]{:S(2)}) collective-permute-start(f16[8,4736]{1,0:T(8,128)(2,1)S(1)} %convert_element_type.77), channel_id=1, source_target_pairs={{0,6},{2,4},{4,2},{6,0},{8,14},{10,12},{12,10},{14,8},{1,7},{3,5},... | collective-permute-start | bytes 227336 | tf_op jit(solution)/shard_map/ppermute | solution.py:292
  9.2 0.6 %collective-permute-start.4 = (f16[8,4736]{1,0:T(8,128)(2,1)S(1)}, f16[8,4736]{1,0:T(8,128)(2,1)S(1)}, u32[]{:S(2)}, u32[]{:S(2)}) collective-permute-start(f16[8,4736]{1,0:T(8,128)(2,1)S(1)} %convert_element_type.79), channel_id=1, source_target_pairs={{0,2},{2,0},{4,6},{6,4},{8,10},{10,8},{12,14},{14,12},{1,3},{3,1},... | collective-permute-start | bytes 227336 | tf_op jit(solution)/shard_map/ppermute | solution.py:292
  9.8 0.1 collective-permute-start.5
  9.9 3.0 %collective-permute-start = (f16[8,4736]{1,0:T(8,128)(2,1)S(1)}, f16[8,4736]{1,0:T(8,128)(2,1)S(1)}, u32[]{:S(2)}, u32[]{:S(2)}) collective-permute-start(f16[8,4736]{1,0:T(8,128)(2,1)S(1)} %convert_element_type.71), channel_id=1, source_target_pairs={{0,6},{2,4},{4,2},{6,0},{8,14},{10,12},{12,10},{14,8},{1,7},{3,5},... | collective-permute-start | bytes 227336 | tf_op jit(solution)/shard_map/ppermute | solution.py:292
  12.9 0.6 %collective-permute-start.1 = (f16[8,4736]{1,0:T(8,128)(2,1)S(1)}, f16[8,4736]{1,0:T(8,128)(2,1)S(1)}, u32[]{:S(2)}, u32[]{:S(2)}) collective-permute-start(f16[8,4736]{1,0:T(8,128)(2,1)S(1)} %convert_element_type.73), channel_id=1, source_target_pairs={{0,2},{2,0},{4,6},{6,4},{8,10},{10,8},{12,14},{14,12},{1,3},{3,1},... | collective-permute-start | bytes 227336 | tf_op jit(solution)/shard_map/ppermute | solution.py:292
  13.6 0.1 fusion.3
  13.8 0.2 collective-permute-start.2
  14.0 0.5 %collective-permute-done.4 = f16[8,4736]{1,0:T(8,128)(2,1)S(1)} collective-permute-done((f16[8,4736]{1,0:T(8,128)(2,1)S(1)}, f16[8,4736]{1,0:T(8,128)(2,1)S(1)}, u32[]{:S(2)}, u32[]{:S(2)}) %collective-permute-start.4) | collective-permute-done | bytes 75808 | tf_op jit(solution)/shard_map/ppermute | solution.py:292
  14.5 0.1 combine.1
  14.6 2.7 %collective-permute-start.6 = (f16[8,4736]{1,0:T(8,128)(2,1)S(1)}, f16[8,4736]{1,0:T(8,128)(2,1)S(1)}, u32[]{:S(2)}, u32[]{:S(2)}) collective-permute-start(f16[8,4736]{1,0:T(8,128)(2,1)S(1)} %convert_element_type.83), channel_id=1, source_target_pairs={{0,8},{2,10},{4,12},{6,14},{8,0},{10,2},{12,4},{14,6},{1,9},{3,11}... | collective-permute-start | bytes 227336 | tf_op jit(solution)/shard_map/ppermute | solution.py:292
  17.4 0.8 %collective-permute-done.2 = f16[8,4736]{1,0:T(8,128)(2,1)S(1)} collective-permute-done((f16[8,4736]{1,0:T(8,128)(2,1)S(1)}, f16[8,4736]{1,0:T(8,128)(2,1)S(1)}, u32[]{:S(2)}, u32[]{:S(2)}) %collective-permute-start.2) | collective-permute-done | bytes 75808 | tf_op jit(solution)/shard_map/ppermute | solution.py:292
  18.2 1.9 %collective-permute-done.6 = f16[8,4736]{1,0:T(8,128)(2,1)S(1)} collective-permute-done((f16[8,4736]{1,0:T(8,128)(2,1)S(1)}, f16[8,4736]{1,0:T(8,128)(2,1)S(1)}, u32[]{:S(2)}, u32[]{:S(2)}) %collective-permute-start.6) | collective-permute-done | bytes 75808 | tf_op jit(solution)/shard_map/ppermute | solution.py:292
  20.2 2.4 %attend.1 = bf16[8,4096]{1,0:T(8,128)(2,1)S(1)} custom-call(f32[4,2048]{1,0:T(4,128)S(1)} %fusion.2.bias, f32[8,4736]{1,0:T(8,128)S(1)} %get-tuple-element.10.mine, f32[8,4736]{1,0:T(8,128)S(1)} %convert_element_type.72.refs_0_, f32[8,4736]{1,0:T(8,128)S(1)} %convert_element_type.74.refs_1_, f32[8,4736]{1,0:T(8,128)S(1)} %convert_element_type.76.refs_2_, ...), custom_call_target="tpu_custom_call" | custom-call | tf_op jit(solution)/shard_map/attend/pallas_call | solution.py:350
  22.6 2.6 %collective-permute-start.7 = (bf16[8,4096]{1,0:T(8,128)(2,1)S(1)}, bf16[8,4096]{1,0:T(8,128)(2,1)S(1)}, u32[]{:S(2)}, u32[]{:S(2)}) collective-permute-start(bf16[8,4096]{1,0:T(8,128)(2,1)S(1)} %attend.1), channel_id=1, source_target_pairs={{0,8},{2,10},{4,12},{6,14},{8,0},{10,2},{12,4},{14,6},{1,9},{3,11}... | collective-permute-start | bytes 196616 | tf_op jit(solution)/shard_map/ppermute | solution.py:292
  25.2 1.3 %collective-permute-start.8 = (bf16[8,4096]{1,0:T(8,128)(2,1)S(1)}, bf16[8,4096]{1,0:T(8,128)(2,1)S(1)}, u32[]{:S(2)}, u32[]{:S(2)}) collective-permute-start(bf16[8,4096]{1,0:T(8,128)(2,1)S(1)} %attend.1), channel_id=1, source_target_pairs={{0,2},{2,0},{4,6},{6,4},{8,10},{10,8},{12,14},{14,12},{1,5},{3,7},... | collective-permute-start | bytes 196616 | tf_op jit(solution)/shard_map/ppermute | solution.py:292
  26.5 2.2 %collective-permute-start.10 = (bf16[8,4096]{1,0:T(8,128)(2,1)S(1)}, bf16[8,4096]{1,0:T(8,128)(2,1)S(1)}, u32[]{:S(2)}, u32[]{:S(2)}) collective-permute-start(bf16[8,4096]{1,0:T(8,128)(2,1)S(1)} %attend.1), channel_id=1, source_target_pairs={{0,4},{2,6},{4,0},{6,2},{8,12},{10,14},{12,8},{14,10},{1,3},{3,1},... | collective-permute-start | bytes 196616 | tf_op jit(solution)/shard_map/ppermute | solution.py:292
  28.7 1.7 %collective-permute-start.12 = (bf16[16,4096]{1,0:T(8,128)(2,1)S(1)}, bf16[16,4096]{1,0:T(8,128)(2,1)S(1)}, u32[]{:S(2)}, u32[]{:S(2)}) collective-permute-start(bf16[16,4096]{1,0:T(8,128)(2,1)S(1)} %pad_maximum_fusion), channel_id=1, source_target_pairs={{0,6},{2,4},{4,2},{6,0},{8,14},{10,12},{12,10},{14,8},{1,7},{3,5},... | collective-permute-start | bytes 393224 | tf_op jit(solution)/shard_map/ppermute | solution.py:292
  30.5 0.6 %collective-permute-start.9 = (bf16[8,4096]{1,0:T(8,128)(2,1)S(1)}, bf16[8,4096]{1,0:T(8,128)(2,1)S(1)}, u32[]{:S(2)}, u32[]{:S(2)}) collective-permute-start(bf16[8,4096]{1,0:T(8,128)(2,1)S(1)} %collective-permute-done.7), channel_id=1, source_target_pairs={{0,2},{2,0},{4,6},{6,4},{8,10},{10,8},{12,14},{14,12},{1,5},{3,7},... | collective-permute-start | bytes 196616 | tf_op jit(solution)/shard_map/ppermute | solution.py:292
  31.1 1.2 %collective-permute-start.11 = (bf16[8,4096]{1,0:T(8,128)(2,1)S(1)}, bf16[8,4096]{1,0:T(8,128)(2,1)S(1)}, u32[]{:S(2)}, u32[]{:S(2)}) collective-permute-start(bf16[8,4096]{1,0:T(8,128)(2,1)S(1)} %collective-permute-done.7), channel_id=1, source_target_pairs={{0,4},{2,6},{4,0},{6,2},{8,12},{10,14},{12,8},{14,10},{1,3},{3,1},... | collective-permute-start | bytes 196616 | tf_op jit(solution)/shard_map/ppermute | solution.py:292
  32.3 3.1 %collective-permute-done.9 = bf16[8,4096]{1,0:T(8,128)(2,1)S(1)} collective-permute-done((bf16[8,4096]{1,0:T(8,128)(2,1)S(1)}, bf16[8,4096]{1,0:T(8,128)(2,1)S(1)}, u32[]{:S(2)}, u32[]{:S(2)}) %collective-permute-start.9) | collective-permute-done | bytes 65568 | tf_op jit(solution)/shard_map/ppermute | solution.py:292
  35.5 1.8 %output.1 = f32[64,1024]{1,0:T(8,128)S(1)} custom-call(bf16[64,4096]{1,0:T(8,128)(2,1)S(1)} %constant_dynamic-update-slice_fusion.gathered, bf16[4096,1024]{1,0:T(8,128)(2,1)S(1)} %bitcast.1), custom_call_target="tpu_custom_call" | custom-call | tf_op jit(solution)/shard_map/output/pallas_call | solution.py:376
  37.4 1.3 %collective-permute-done.13 = f16[64,1024]{1,0:T(8,128)(2,1)S(1)} collective-permute-done((f16[64,1024]{1,0:T(8,128)(2,1)S(1)}, f16[64,1024]{1,0:T(8,128)(2,1)S(1)}, u32[]{:S(2)}, u32[]{:S(2)}) %collective-permute-start.13) | collective-permute-done | bytes 131104 | tf_op jit(solution)/shard_map/ppermute | solution.py:385
  38.8 0.7 %fusion = (bf16[32,1024]{1,0:T(8,128)(2,1)}, bf16[32,1024]{1,0:T(8,128)(2,1)}) fusion(f32[64,1024]{1,0:T(8,128)S(1)} %add_multiply_fusion, bf16[32,1024]{1,0:T(8,128)(2,1)S(1)} %copy-done.3, bf16[32,1024]{1,0:T(8,128)(2,1)S(1)} %copy-done.2), kind=kLoop, calls=%fused_computation.3 | loop fusion | flops 196608 | bytes 524288 | tf_op jit(solution)/shard_map/convert_element_type | solution.py:389
  (56 shorter events, 0.7 us)
Async XLA Ops:
  0.6 12.8 %copy-start.5 = (s32[4]{0:T(128)S(1)}, s32[4]{0:T(128)}, u32[]{:S(2)}) copy-start(s32[4]{0:T(128)} %param.21) | copy-start | bytes 52
  0.6 12.9 %copy-start.4 = (s32[4]{0:T(128)S(1)}, s32[4]{0:T(128)}, u32[]{:S(2)}) copy-start(s32[4]{0:T(128)} %param.20) | copy-start | bytes 52
  0.7 19.5 %copy-start = (bf16[4,2,2048,128]{3,2,1,0:T(8,128)(2,1)S(1)}, bf16[4,2,2048,128]{3,2,1,0:T(8,128)(2,1)}, u32[]{:S(2)}) copy-start(bf16[4,2,2048,128]{3,2,1,0:T(8,128)(2,1)} %refs_6_.1) | copy-start | bytes 12582916
  0.7 19.5 %copy-start.1 = (bf16[4,2,2048,128]{3,2,1,0:T(8,128)(2,1)S(1)}, bf16[4,2,2048,128]{3,2,1,0:T(8,128)(2,1)}, u32[]{:S(2)}) copy-start(bf16[4,2,2048,128]{3,2,1,0:T(8,128)(2,1)} %refs_7_.1) | copy-start | bytes 12582916
  0.7 34.8 %slice-start = ((s8[8388608]{0:T(1024)(128)(4,1)}), s8[4194304]{0:T(1024)(128)(4,1)S(1)}, s32[]{:S(2)}) async-start(s8[8388608]{0:T(1024)(128)(4,1)} %bitcast), calls=%async_computation | async-start | bytes 8388608
  5.1 8.7 %collective-permute-start.3 = (f16[8,4736]{1,0:T(8,128)(2,1)S(1)}, f16[8,4736]{1,0:T(8,128)(2,1)S(1)}, u32[]{:S(2)}, u32[]{:S(2)}) collective-permute-start(f16[8,4736]{1,0:T(8,128)(2,1)S(1)} %convert_element_type.77), channel_id=1, source_target_pairs={{0,6},{2,4},{4,2},{6,0},{8,14},{10,12},{12,10},{14,8},{1,7},{3,5},... | collective-permute-start | bytes 227336 | tf_op jit(solution)/shard_map/ppermute | solution.py:292
  9.2 5.3 %collective-permute-start.4 = (f16[8,4736]{1,0:T(8,128)(2,1)S(1)}, f16[8,4736]{1,0:T(8,128)(2,1)S(1)}, u32[]{:S(2)}, u32[]{:S(2)}) collective-permute-start(f16[8,4736]{1,0:T(8,128)(2,1)S(1)} %convert_element_type.79), channel_id=1, source_target_pairs={{0,2},{2,0},{4,6},{6,4},{8,10},{10,8},{12,14},{14,12},{1,3},{3,1},... | collective-permute-start | bytes 227336 | tf_op jit(solution)/shard_map/ppermute | solution.py:292
  9.8 4.8 %collective-permute-start.5 = (f16[8,4736]{1,0:T(8,128)(2,1)S(1)}, f16[8,4736]{1,0:T(8,128)(2,1)S(1)}, u32[]{:S(2)}, u32[]{:S(2)}) collective-permute-start(f16[8,4736]{1,0:T(8,128)(2,1)S(1)} %convert_element_type.81), channel_id=1, source_target_pairs={{0,4},{2,6},{4,0},{6,2},{8,12},{10,14},{12,8},{14,10},{1,5},{3,7},... | collective-permute-start | bytes 227336 | tf_op jit(solution)/shard_map/ppermute | solution.py:292
  9.9 7.5 %collective-permute-start = (f16[8,4736]{1,0:T(8,128)(2,1)S(1)}, f16[8,4736]{1,0:T(8,128)(2,1)S(1)}, u32[]{:S(2)}, u32[]{:S(2)}) collective-permute-start(f16[8,4736]{1,0:T(8,128)(2,1)S(1)} %convert_element_type.71), channel_id=1, source_target_pairs={{0,6},{2,4},{4,2},{6,0},{8,14},{10,12},{12,10},{14,8},{1,7},{3,5},... | collective-permute-start | bytes 227336 | tf_op jit(solution)/shard_map/ppermute | solution.py:292
  12.9 4.5 %collective-permute-start.1 = (f16[8,4736]{1,0:T(8,128)(2,1)S(1)}, f16[8,4736]{1,0:T(8,128)(2,1)S(1)}, u32[]{:S(2)}, u32[]{:S(2)}) collective-permute-start(f16[8,4736]{1,0:T(8,128)(2,1)S(1)} %convert_element_type.73), channel_id=1, source_target_pairs={{0,2},{2,0},{4,6},{6,4},{8,10},{10,8},{12,14},{14,12},{1,3},{3,1},... | collective-permute-start | bytes 227336 | tf_op jit(solution)/shard_map/ppermute | solution.py:292
  13.8 4.4 %collective-permute-start.2 = (f16[8,4736]{1,0:T(8,128)(2,1)S(1)}, f16[8,4736]{1,0:T(8,128)(2,1)S(1)}, u32[]{:S(2)}, u32[]{:S(2)}) collective-permute-start(f16[8,4736]{1,0:T(8,128)(2,1)S(1)} %convert_element_type.75), channel_id=1, source_target_pairs={{0,4},{2,6},{4,0},{6,2},{8,12},{10,14},{12,8},{14,10},{1,5},{3,7},... | collective-permute-start | bytes 227336 | tf_op jit(solution)/shard_map/ppermute | solution.py:292
  14.5 20.9 %slice-start.1 = ((s8[8388608]{0:T(1024)(128)(4,1)}), s8[4194304]{0:T(1024)(128)(4,1)S(1)}, s32[]{:S(2)}) async-start(s8[8388608]{0:T(1024)(128)(4,1)} %bitcast), calls=%async_computation.1 | async-start | bytes 8388608
  14.6 5.5 %collective-permute-start.6 = (f16[8,4736]{1,0:T(8,128)(2,1)S(1)}, f16[8,4736]{1,0:T(8,128)(2,1)S(1)}, u32[]{:S(2)}, u32[]{:S(2)}) collective-permute-start(f16[8,4736]{1,0:T(8,128)(2,1)S(1)} %convert_element_type.83), channel_id=1, source_target_pairs={{0,8},{2,10},{4,12},{6,14},{8,0},{10,2},{12,4},{14,6},{1,9},{3,11}... | collective-permute-start | bytes 227336 | tf_op jit(solution)/shard_map/ppermute | solution.py:292
  20.2 18.6 %copy-start.2 = (bf16[32,1024]{1,0:T(8,128)(2,1)S(1)}, bf16[32,1024]{1,0:T(8,128)(2,1)}, u32[]{:S(2)}) copy-start(bf16[32,1024]{1,0:T(8,128)(2,1)} %first.1) | copy-start | bytes 196612
  20.2 18.6 %copy-start.3 = (bf16[32,1024]{1,0:T(8,128)(2,1)S(1)}, bf16[32,1024]{1,0:T(8,128)(2,1)}, u32[]{:S(2)}) copy-start(bf16[32,1024]{1,0:T(8,128)(2,1)} %second.1) | copy-start | bytes 196612
  22.6 6.1 %collective-permute-start.7 = (bf16[8,4096]{1,0:T(8,128)(2,1)S(1)}, bf16[8,4096]{1,0:T(8,128)(2,1)S(1)}, u32[]{:S(2)}, u32[]{:S(2)}) collective-permute-start(bf16[8,4096]{1,0:T(8,128)(2,1)S(1)} %attend.1), channel_id=1, source_target_pairs={{0,8},{2,10},{4,12},{6,14},{8,0},{10,2},{12,4},{14,6},{1,9},{3,11}... | collective-permute-start | bytes 196616 | tf_op jit(solution)/shard_map/ppermute | solution.py:292
  25.2 7.1 %collective-permute-start.8 = (bf16[8,4096]{1,0:T(8,128)(2,1)S(1)}, bf16[8,4096]{1,0:T(8,128)(2,1)S(1)}, u32[]{:S(2)}, u32[]{:S(2)}) collective-permute-start(bf16[8,4096]{1,0:T(8,128)(2,1)S(1)} %attend.1), channel_id=1, source_target_pairs={{0,2},{2,0},{4,6},{6,4},{8,10},{10,8},{12,14},{14,12},{1,5},{3,7},... | collective-permute-start | bytes 196616 | tf_op jit(solution)/shard_map/ppermute | solution.py:292
  26.5 8.9 %collective-permute-start.10 = (bf16[8,4096]{1,0:T(8,128)(2,1)S(1)}, bf16[8,4096]{1,0:T(8,128)(2,1)S(1)}, u32[]{:S(2)}, u32[]{:S(2)}) collective-permute-start(bf16[8,4096]{1,0:T(8,128)(2,1)S(1)} %attend.1), channel_id=1, source_target_pairs={{0,4},{2,6},{4,0},{6,2},{8,12},{10,14},{12,8},{14,10},{1,3},{3,1},... | collective-permute-start | bytes 196616 | tf_op jit(solution)/shard_map/ppermute | solution.py:292
  28.7 6.7 %collective-permute-start.12 = (bf16[16,4096]{1,0:T(8,128)(2,1)S(1)}, bf16[16,4096]{1,0:T(8,128)(2,1)S(1)}, u32[]{:S(2)}, u32[]{:S(2)}) collective-permute-start(bf16[16,4096]{1,0:T(8,128)(2,1)S(1)} %pad_maximum_fusion), channel_id=1, source_target_pairs={{0,6},{2,4},{4,2},{6,0},{8,14},{10,12},{12,10},{14,8},{1,7},{3,5},... | collective-permute-start | bytes 393224 | tf_op jit(solution)/shard_map/ppermute | solution.py:292
  30.5 4.9 %collective-permute-start.9 = (bf16[8,4096]{1,0:T(8,128)(2,1)S(1)}, bf16[8,4096]{1,0:T(8,128)(2,1)S(1)}, u32[]{:S(2)}, u32[]{:S(2)}) collective-permute-start(bf16[8,4096]{1,0:T(8,128)(2,1)S(1)} %collective-permute-done.7), channel_id=1, source_target_pairs={{0,2},{2,0},{4,6},{6,4},{8,10},{10,8},{12,14},{14,12},{1,5},{3,7},... | collective-permute-start | bytes 196616 | tf_op jit(solution)/shard_map/ppermute | solution.py:292
  31.1 4.3 %collective-permute-start.11 = (bf16[8,4096]{1,0:T(8,128)(2,1)S(1)}, bf16[8,4096]{1,0:T(8,128)(2,1)S(1)}, u32[]{:S(2)}, u32[]{:S(2)}) collective-permute-start(bf16[8,4096]{1,0:T(8,128)(2,1)S(1)} %collective-permute-done.7), channel_id=1, source_target_pairs={{0,4},{2,6},{4,0},{6,2},{8,12},{10,14},{12,8},{14,10},{1,3},{3,1},... | collective-permute-start | bytes 196616 | tf_op jit(solution)/shard_map/ppermute | solution.py:292
  37.3 1.4 %collective-permute-start.13 = (f16[64,1024]{1,0:T(8,128)(2,1)S(1)}, f16[64,1024]{1,0:T(8,128)(2,1)S(1)}, u32[]{:S(2)}, u32[]{:S(2)}) collective-permute-start(f16[64,1024]{1,0:T(8,128)(2,1)S(1)} %multiply_convert_fusion), channel_id=1, source_target_pairs={{0,1},{1,0},{2,3},{3,2},{4,5},{5,4},{6,7},{7,6},{8,9},{9,8},{10,11... | collective-permute-start | bytes 393224 | tf_op jit(solution)/shard_map/ppermute | solution.py:385

commit v7 on v6

--- a/solution.py
+++ b/solution.py
@@ -282,7 +282,7 @@
     columns = w_query.shape[1] + 2 * w_key.shape[1] + LANES
 
     plans = ([0, 3, 1, 2], [0, 3, 1, 2]) if inner == 4 else (list(range(inner)),) * 2
-    gather_plans = ([0, 1, 2, 3], [0, 2, 1, 3]) if inner == 4 else plans
+    gather_plans = ([0, 2, 1, 3], [0, 2, 1, 3]) if inner == 4 else plans
     def exchange(value, steps):
         pairs = [
             (place_from * cores + c, (place_from ^ steps[min(c, 1)]) * cores + c)

time: 39.6 us -> 39.5 us (level)
  transfers between devices with their start and end apart: 14 -> 14, of which waited for: 6 -> 7; matrix products, arithmetic and copies ran while one was open for 1% -> 1% of each run, Pallas kernels for 0% -> 0%
where the time goes in v7:
time: 39.5 us; the launch traced here: 39.4 us
  starting transfers between devices  20.9 us (53%)
  Pallas kernels  8.6 us (22%)
  waiting for transfers between devices  7.62 us (19%)
  other arithmetic  1.28 us (3%)
  between operations  0.93 us (2%)
    ppermute x13, starting transfers between devices, exchange(): return lax.ppermute(value, ('wide', 'narrow'), pairs)  20.8 us
    ppermute x13, waiting for transfers between devices, exchange(): return lax.ppermute(value, ('wide', 'narrow'), pairs)  6.29 us
    pallas_call x1, Pallas kernels, on_device(): pl.pallas_call(functools.partial(project_kernel, rows_dev, outer, plans),...  4.4 us
    pallas_call x1, Pallas kernels, on_device(): pl.pallas_call(functools.partial(attend_kernel, len(received), devices *...  2.36 us
    pallas_call x1, Pallas kernels, on_device(): pl.pallas_call(functools.partial(output_kernel, rows_dev, outer, gather_p...  1.76 us
    ppermute x1, waiting for transfers between devices, on_device(): lax.ppermute(part, 'narrow', [(c, cores - 1 - c) for c in range(cores)])  1.33 us
  transfers between devices with their start and end apart: 14, of which 7 were waited for; matrix products, arithmetic and copies ran while one was open for 1% of the time, Pallas kernels for 0%

profile of v7, /device:TPU:0, one launch (start us, length us, event | category | flops | bytes accessed | tf_op | source)
XLA Modules:
  0.0 39.4 jit_solution(5984781736444032494)
XLA Ops:
  0.7 4.4 %project.1 = (f32[8,4736]{1,0:T(8,128)S(1)}, f32[8,4736]{1,0:T(8,128)S(1)}, f32[8,4736]{1,0:T(8,128)S(1)}, f32[8,4736]{1,0:T(8,128)S(1)}, f32[8,4736]{1,0:T(8,12...) custom-call(bf16[32,1024]{1,0:T(8,128)(2,1)} %first.1, bf16[32,1024]{1,0:T(8,128)(2,1)} %second.1, ...), custom_call_target="tpu_custom_call" | custom-call | flops 620756992 | bytes 9699328 | tf_op jit(solution)/shard_map/project/pallas_call | solution.py:299
  5.1 4.0 %collective-permute-start.3 = (f16[8,4736]{1,0:T(8,128)(2,1)S(1)}, f16[8,4736]{1,0:T(8,128)(2,1)S(1)}, u32[]{:S(2)}, u32[]{:S(2)}) collective-permute-start(f16[8,4736]{1,0:T(8,128)(2,1)S(1)} %convert_element_type.77), channel_id=1, source_target_pairs={{0,6},{2,4},{4,2},{6,0},{8,14},{10,12},{12,10},{14,8},{1,7},{3,5},... | collective-permute-start | bytes 227336 | tf_op jit(solution)/shard_map/ppermute | solution.py:292
  9.2 0.6 %collective-permute-start.4 = (f16[8,4736]{1,0:T(8,128)(2,1)S(1)}, f16[8,4736]{1,0:T(8,128)(2,1)S(1)}, u32[]{:S(2)}, u32[]{:S(2)}) collective-permute-start(f16[8,4736]{1,0:T(8,128)(2,1)S(1)} %convert_element_type.79), channel_id=1, source_target_pairs={{0,2},{2,0},{4,6},{6,4},{8,10},{10,8},{12,14},{14,12},{1,3},{3,1},... | collective-permute-start | bytes 227336 | tf_op jit(solution)/shard_map/ppermute | solution.py:292
  9.8 0.1 collective-permute-start.5
  9.9 3.0 %collective-permute-start = (f16[8,4736]{1,0:T(8,128)(2,1)S(1)}, f16[8,4736]{1,0:T(8,128)(2,1)S(1)}, u32[]{:S(2)}, u32[]{:S(2)}) collective-permute-start(f16[8,4736]{1,0:T(8,128)(2,1)S(1)} %convert_element_type.71), channel_id=1, source_target_pairs={{0,6},{2,4},{4,2},{6,0},{8,14},{10,12},{12,10},{14,8},{1,7},{3,5},... | collective-permute-start | bytes 227336 | tf_op jit(solution)/shard_map/ppermute | solution.py:292
  12.9 0.6 %collective-permute-start.1 = (f16[8,4736]{1,0:T(8,128)(2,1)S(1)}, f16[8,4736]{1,0:T(8,128)(2,1)S(1)}, u32[]{:S(2)}, u32[]{:S(2)}) collective-permute-start(f16[8,4736]{1,0:T(8,128)(2,1)S(1)} %convert_element_type.73), channel_id=1, source_target_pairs={{0,2},{2,0},{4,6},{6,4},{8,10},{10,8},{12,14},{14,12},{1,3},{3,1},... | collective-permute-start | bytes 227336 | tf_op jit(solution)/shard_map/ppermute | solution.py:292
  13.6 0.1 fusion.3
  13.8 0.2 collective-permute-start.2
  14.0 0.5 %collective-permute-done.4 = f16[8,4736]{1,0:T(8,128)(2,1)S(1)} collective-permute-done((f16[8,4736]{1,0:T(8,128)(2,1)S(1)}, f16[8,4736]{1,0:T(8,128)(2,1)S(1)}, u32[]{:S(2)}, u32[]{:S(2)}) %collective-permute-start.4) | collective-permute-done | bytes 75808 | tf_op jit(solution)/shard_map/ppermute | solution.py:292
  14.6 2.7 %collective-permute-start.6 = (f16[8,4736]{1,0:T(8,128)(2,1)S(1)}, f16[8,4736]{1,0:T(8,128)(2,1)S(1)}, u32[]{:S(2)}, u32[]{:S(2)}) collective-permute-start(f16[8,4736]{1,0:T(8,128)(2,1)S(1)} %convert_element_type.83), channel_id=1, source_target_pairs={{0,8},{2,10},{4,12},{6,14},{8,0},{10,2},{12,4},{14,6},{1,9},{3,11}... | collective-permute-start | bytes 227336 | tf_op jit(solution)/shard_map/ppermute | solution.py:292
  17.4 0.8 %collective-permute-done.2 = f16[8,4736]{1,0:T(8,128)(2,1)S(1)} collective-permute-done((f16[8,4736]{1,0:T(8,128)(2,1)S(1)}, f16[8,4736]{1,0:T(8,128)(2,1)S(1)}, u32[]{:S(2)}, u32[]{:S(2)}) %collective-permute-start.2) | collective-permute-done | bytes 75808 | tf_op jit(solution)/shard_map/ppermute | solution.py:292
  18.2 1.9 %collective-permute-done.6 = f16[8,4736]{1,0:T(8,128)(2,1)S(1)} collective-permute-done((f16[8,4736]{1,0:T(8,128)(2,1)S(1)}, f16[8,4736]{1,0:T(8,128)(2,1)S(1)}, u32[]{:S(2)}, u32[]{:S(2)}) %collective-permute-start.6) | collective-permute-done | bytes 75808 | tf_op jit(solution)/shard_map/ppermute | solution.py:292
  20.2 2.4 %attend.1 = bf16[8,4096]{1,0:T(8,128)(2,1)S(1)} custom-call(f32[4,2048]{1,0:T(4,128)S(1)} %fusion.2.bias, f32[8,4736]{1,0:T(8,128)S(1)} %get-tuple-element.10.mine, f32[8,4736]{1,0:T(8,128)S(1)} %convert_element_type.72.refs_0_, f32[8,4736]{1,0:T(8,128)S(1)} %convert_element_type.74.refs_1_, f32[8,4736]{1,0:T(8,128)S(1)} %convert_element_type.76.refs_2_, ...), custom_call_target="tpu_custom_call" | custom-call | tf_op jit(solution)/shard_map/attend/pallas_call | solution.py:350
  22.6 2.6 %collective-permute-start.7 = (bf16[8,4096]{1,0:T(8,128)(2,1)S(1)}, bf16[8,4096]{1,0:T(8,128)(2,1)S(1)}, u32[]{:S(2)}, u32[]{:S(2)}) collective-permute-start(bf16[8,4096]{1,0:T(8,128)(2,1)S(1)} %attend.1), channel_id=1, source_target_pairs={{0,8},{2,10},{4,12},{6,14},{8,0},{10,2},{12,4},{14,6},{1,9},{3,11}... | collective-permute-start | bytes 196616 | tf_op jit(solution)/shard_map/ppermute | solution.py:292
  25.2 2.1 %collective-permute-start.8 = (bf16[8,4096]{1,0:T(8,128)(2,1)S(1)}, bf16[8,4096]{1,0:T(8,128)(2,1)S(1)}, u32[]{:S(2)}, u32[]{:S(2)}) collective-permute-start(bf16[8,4096]{1,0:T(8,128)(2,1)S(1)} %attend.1), channel_id=1, source_target_pairs={{0,4},{2,6},{4,0},{6,2},{8,12},{10,14},{12,8},{14,10},{1,5},{3,7},... | collective-permute-start | bytes 196616 | tf_op jit(solution)/shard_map/ppermute | solution.py:292
  27.3 1.4 %collective-permute-start.10 = (bf16[8,4096]{1,0:T(8,128)(2,1)S(1)}, bf16[8,4096]{1,0:T(8,128)(2,1)S(1)}, u32[]{:S(2)}, u32[]{:S(2)}) collective-permute-start(bf16[8,4096]{1,0:T(8,128)(2,1)S(1)} %attend.1), channel_id=1, source_target_pairs={{0,2},{2,0},{4,6},{6,4},{8,10},{10,8},{12,14},{14,12},{1,3},{3,1},... | collective-permute-start | bytes 196616 | tf_op jit(solution)/shard_map/ppermute | solution.py:292
  28.7 1.7 %collective-permute-start.12 = (bf16[16,4096]{1,0:T(8,128)(2,1)S(1)}, bf16[16,4096]{1,0:T(8,128)(2,1)S(1)}, u32[]{:S(2)}, u32[]{:S(2)}) collective-permute-start(bf16[16,4096]{1,0:T(8,128)(2,1)S(1)} %pad_maximum_fusion), channel_id=1, source_target_pairs={{0,6},{2,4},{4,2},{6,0},{8,14},{10,12},{12,10},{14,8},{1,7},{3,5},... | collective-permute-start | bytes 393224 | tf_op jit(solution)/shard_map/ppermute | solution.py:292
  30.5 0.4 %collective-permute-start.9 = (bf16[8,4096]{1,0:T(8,128)(2,1)S(1)}, bf16[8,4096]{1,0:T(8,128)(2,1)S(1)}, u32[]{:S(2)}, u32[]{:S(2)}) collective-permute-start(bf16[8,4096]{1,0:T(8,128)(2,1)S(1)} %collective-permute-done.7), channel_id=1, source_target_pairs={{0,4},{2,6},{4,0},{6,2},{8,12},{10,14},{12,8},{14,10},{1,5},{3,7},... | collective-permute-start | bytes 196616 | tf_op jit(solution)/shard_map/ppermute | solution.py:292
  30.9 1.4 %collective-permute-start.11 = (bf16[8,4096]{1,0:T(8,128)(2,1)S(1)}, bf16[8,4096]{1,0:T(8,128)(2,1)S(1)}, u32[]{:S(2)}, u32[]{:S(2)}) collective-permute-start(bf16[8,4096]{1,0:T(8,128)(2,1)S(1)} %collective-permute-done.7), channel_id=1, source_target_pairs={{0,2},{2,0},{4,6},{6,4},{8,10},{10,8},{12,14},{14,12},{1,3},{3,1},... | collective-permute-start | bytes 196616 | tf_op jit(solution)/shard_map/ppermute | solution.py:292
  32.3 2.4 %collective-permute-done.9 = bf16[8,4096]{1,0:T(8,128)(2,1)S(1)} collective-permute-done((bf16[8,4096]{1,0:T(8,128)(2,1)S(1)}, bf16[8,4096]{1,0:T(8,128)(2,1)S(1)}, u32[]{:S(2)}, u32[]{:S(2)}) %collective-permute-start.9) | collective-permute-done | bytes 65568 | tf_op jit(solution)/shard_map/ppermute | solution.py:292
  34.8 0.6 %collective-permute-done.11 = bf16[8,4096]{1,0:T(8,128)(2,1)S(1)} collective-permute-done((bf16[8,4096]{1,0:T(8,128)(2,1)S(1)}, bf16[8,4096]{1,0:T(8,128)(2,1)S(1)}, u32[]{:S(2)}, u32[]{:S(2)}) %collective-permute-start.11) | collective-permute-done | bytes 65568 | tf_op jit(solution)/shard_map/ppermute | solution.py:292
  35.4 1.8 %output.1 = f32[64,1024]{1,0:T(8,128)S(1)} custom-call(bf16[64,4096]{1,0:T(8,128)(2,1)S(1)} %constant_dynamic-update-slice_fusion.gathered, bf16[4096,1024]{1,0:T(8,128)(2,1)S(1)} %bitcast.1), custom_call_target="tpu_custom_call" | custom-call | tf_op jit(solution)/shard_map/output/pallas_call | solution.py:376
  37.3 1.3 %collective-permute-done.13 = f16[64,1024]{1,0:T(8,128)(2,1)S(1)} collective-permute-done((f16[64,1024]{1,0:T(8,128)(2,1)S(1)}, f16[64,1024]{1,0:T(8,128)(2,1)S(1)}, u32[]{:S(2)}, u32[]{:S(2)}) %collective-permute-start.13) | collective-permute-done | bytes 131104 | tf_op jit(solution)/shard_map/ppermute | solution.py:385
  38.7 0.7 %fusion = (bf16[32,1024]{1,0:T(8,128)(2,1)}, bf16[32,1024]{1,0:T(8,128)(2,1)}) fusion(f32[64,1024]{1,0:T(8,128)S(1)} %add_multiply_fusion, bf16[32,1024]{1,0:T(8,128)(2,1)S(1)} %copy-done.3, bf16[32,1024]{1,0:T(8,128)(2,1)S(1)} %copy-done.2), kind=kLoop, calls=%fused_computation.3 | loop fusion | flops 196608 | bytes 524288 | tf_op jit(solution)/shard_map/convert_element_type | solution.py:389
  (56 shorter events, 0.8 us)
Async XLA Ops:
  0.6 12.8 %copy-start.5 = (s32[4]{0:T(128)S(1)}, s32[4]{0:T(128)}, u32[]{:S(2)}) copy-start(s32[4]{0:T(128)} %param.21) | copy-start | bytes 52
  0.6 12.9 %copy-start.4 = (s32[4]{0:T(128)S(1)}, s32[4]{0:T(128)}, u32[]{:S(2)}) copy-start(s32[4]{0:T(128)} %param.20) | copy-start | bytes 52
  0.7 19.5 %copy-start = (bf16[4,2,2048,128]{3,2,1,0:T(8,128)(2,1)S(1)}, bf16[4,2,2048,128]{3,2,1,0:T(8,128)(2,1)}, u32[]{:S(2)}) copy-start(bf16[4,2,2048,128]{3,2,1,0:T(8,128)(2,1)} %refs_6_.1) | copy-start | bytes 12582916
  0.7 19.5 %copy-start.1 = (bf16[4,2,2048,128]{3,2,1,0:T(8,128)(2,1)S(1)}, bf16[4,2,2048,128]{3,2,1,0:T(8,128)(2,1)}, u32[]{:S(2)}) copy-start(bf16[4,2,2048,128]{3,2,1,0:T(8,128)(2,1)} %refs_7_.1) | copy-start | bytes 12582916
  0.7 34.7 %slice-start = ((s8[8388608]{0:T(1024)(128)(4,1)}), s8[4194304]{0:T(1024)(128)(4,1)S(1)}, s32[]{:S(2)}) async-start(s8[8388608]{0:T(1024)(128)(4,1)} %bitcast), calls=%async_computation | async-start | bytes 8388608
  5.1 8.7 %collective-permute-start.3 = (f16[8,4736]{1,0:T(8,128)(2,1)S(1)}, f16[8,4736]{1,0:T(8,128)(2,1)S(1)}, u32[]{:S(2)}, u32[]{:S(2)}) collective-permute-start(f16[8,4736]{1,0:T(8,128)(2,1)S(1)} %convert_element_type.77), channel_id=1, source_target_pairs={{0,6},{2,4},{4,2},{6,0},{8,14},{10,12},{12,10},{14,8},{1,7},{3,5},... | collective-permute-start | bytes 227336 | tf_op jit(solution)/shard_map/ppermute | solution.py:292
  9.2 5.3 %collective-permute-start.4 = (f16[8,4736]{1,0:T(8,128)(2,1)S(1)}, f16[8,4736]{1,0:T(8,128)(2,1)S(1)}, u32[]{:S(2)}, u32[]{:S(2)}) collective-permute-start(f16[8,4736]{1,0:T(8,128)(2,1)S(1)} %convert_element_type.79), channel_id=1, source_target_pairs={{0,2},{2,0},{4,6},{6,4},{8,10},{10,8},{12,14},{14,12},{1,3},{3,1},... | collective-permute-start | bytes 227336 | tf_op jit(solution)/shard_map/ppermute | solution.py:292
  9.8 4.8 %collective-permute-start.5 = (f16[8,4736]{1,0:T(8,128)(2,1)S(1)}, f16[8,4736]{1,0:T(8,128)(2,1)S(1)}, u32[]{:S(2)}, u32[]{:S(2)}) collective-permute-start(f16[8,4736]{1,0:T(8,128)(2,1)S(1)} %convert_element_type.81), channel_id=1, source_target_pairs={{0,4},{2,6},{4,0},{6,2},{8,12},{10,14},{12,8},{14,10},{1,5},{3,7},... | collective-permute-start | bytes 227336 | tf_op jit(solution)/shard_map/ppermute | solution.py:292
  9.9 7.5 %collective-permute-start = (f16[8,4736]{1,0:T(8,128)(2,1)S(1)}, f16[8,4736]{1,0:T(8,128)(2,1)S(1)}, u32[]{:S(2)}, u32[]{:S(2)}) collective-permute-start(f16[8,4736]{1,0:T(8,128)(2,1)S(1)} %convert_element_type.71), channel_id=1, source_target_pairs={{0,6},{2,4},{4,2},{6,0},{8,14},{10,12},{12,10},{14,8},{1,7},{3,5},... | collective-permute-start | bytes 227336 | tf_op jit(solution)/shard_map/ppermute | solution.py:292
  12.9 4.5 %collective-permute-start.1 = (f16[8,4736]{1,0:T(8,128)(2,1)S(1)}, f16[8,4736]{1,0:T(8,128)(2,1)S(1)}, u32[]{:S(2)}, u32[]{:S(2)}) collective-permute-start(f16[8,4736]{1,0:T(8,128)(2,1)S(1)} %convert_element_type.73), channel_id=1, source_target_pairs={{0,2},{2,0},{4,6},{6,4},{8,10},{10,8},{12,14},{14,12},{1,3},{3,1},... | collective-permute-start | bytes 227336 | tf_op jit(solution)/shard_map/ppermute | solution.py:292
  13.8 4.4 %collective-permute-start.2 = (f16[8,4736]{1,0:T(8,128)(2,1)S(1)}, f16[8,4736]{1,0:T(8,128)(2,1)S(1)}, u32[]{:S(2)}, u32[]{:S(2)}) collective-permute-start(f16[8,4736]{1,0:T(8,128)(2,1)S(1)} %convert_element_type.75), channel_id=1, source_target_pairs={{0,4},{2,6},{4,0},{6,2},{8,12},{10,14},{12,8},{14,10},{1,5},{3,7},... | collective-permute-start | bytes 227336 | tf_op jit(solution)/shard_map/ppermute | solution.py:292
  14.5 20.9 %slice-start.1 = ((s8[8388608]{0:T(1024)(128)(4,1)}), s8[4194304]{0:T(1024)(128)(4,1)S(1)}, s32[]{:S(2)}) async-start(s8[8388608]{0:T(1024)(128)(4,1)} %bitcast), calls=%async_computation.1 | async-start | bytes 8388608
  14.6 5.5 %collective-permute-start.6 = (f16[8,4736]{1,0:T(8,128)(2,1)S(1)}, f16[8,4736]{1,0:T(8,128)(2,1)S(1)}, u32[]{:S(2)}, u32[]{:S(2)}) collective-permute-start(f16[8,4736]{1,0:T(8,128)(2,1)S(1)} %convert_element_type.83), channel_id=1, source_target_pairs={{0,8},{2,10},{4,12},{6,14},{8,0},{10,2},{12,4},{14,6},{1,9},{3,11}... | collective-permute-start | bytes 227336 | tf_op jit(solution)/shard_map/ppermute | solution.py:292
  20.2 18.5 %copy-start.2 = (bf16[32,1024]{1,0:T(8,128)(2,1)S(1)}, bf16[32,1024]{1,0:T(8,128)(2,1)}, u32[]{:S(2)}) copy-start(bf16[32,1024]{1,0:T(8,128)(2,1)} %first.1) | copy-start | bytes 196612
  20.2 18.5 %copy-start.3 = (bf16[32,1024]{1,0:T(8,128)(2,1)S(1)}, bf16[32,1024]{1,0:T(8,128)(2,1)}, u32[]{:S(2)}) copy-start(bf16[32,1024]{1,0:T(8,128)(2,1)} %second.1) | copy-start | bytes 196612
  22.6 6.1 %collective-permute-start.7 = (bf16[8,4096]{1,0:T(8,128)(2,1)S(1)}, bf16[8,4096]{1,0:T(8,128)(2,1)S(1)}, u32[]{:S(2)}, u32[]{:S(2)}) collective-permute-start(bf16[8,4096]{1,0:T(8,128)(2,1)S(1)} %attend.1), channel_id=1, source_target_pairs={{0,8},{2,10},{4,12},{6,14},{8,0},{10,2},{12,4},{14,6},{1,9},{3,11}... | collective-permute-start | bytes 196616 | tf_op jit(solution)/shard_map/ppermute | solution.py:292
  25.2 7.1 %collective-permute-start.8 = (bf16[8,4096]{1,0:T(8,128)(2,1)S(1)}, bf16[8,4096]{1,0:T(8,128)(2,1)S(1)}, u32[]{:S(2)}, u32[]{:S(2)}) collective-permute-start(bf16[8,4096]{1,0:T(8,128)(2,1)S(1)} %attend.1), channel_id=1, source_target_pairs={{0,4},{2,6},{4,0},{6,2},{8,12},{10,14},{12,8},{14,10},{1,5},{3,7},... | collective-permute-start | bytes 196616 | tf_op jit(solution)/shard_map/ppermute | solution.py:292
  27.3 7.4 %collective-permute-start.10 = (bf16[8,4096]{1,0:T(8,128)(2,1)S(1)}, bf16[8,4096]{1,0:T(8,128)(2,1)S(1)}, u32[]{:S(2)}, u32[]{:S(2)}) collective-permute-start(bf16[8,4096]{1,0:T(8,128)(2,1)S(1)} %attend.1), channel_id=1, source_target_pairs={{0,2},{2,0},{4,6},{6,4},{8,10},{10,8},{12,14},{14,12},{1,3},{3,1},... | collective-permute-start | bytes 196616 | tf_op jit(solution)/shard_map/ppermute | solution.py:292
  28.7 6.6 %collective-permute-start.12 = (bf16[16,4096]{1,0:T(8,128)(2,1)S(1)}, bf16[16,4096]{1,0:T(8,128)(2,1)S(1)}, u32[]{:S(2)}, u32[]{:S(2)}) collective-permute-start(bf16[16,4096]{1,0:T(8,128)(2,1)S(1)} %pad_maximum_fusion), channel_id=1, source_target_pairs={{0,6},{2,4},{4,2},{6,0},{8,14},{10,12},{12,10},{14,8},{1,7},{3,5},... | collective-permute-start | bytes 393224 | tf_op jit(solution)/shard_map/ppermute | solution.py:292
  30.5 4.3 %collective-permute-start.9 = (bf16[8,4096]{1,0:T(8,128)(2,1)S(1)}, bf16[8,4096]{1,0:T(8,128)(2,1)S(1)}, u32[]{:S(2)}, u32[]{:S(2)}) collective-permute-start(bf16[8,4096]{1,0:T(8,128)(2,1)S(1)} %collective-permute-done.7), channel_id=1, source_target_pairs={{0,4},{2,6},{4,0},{6,2},{8,12},{10,14},{12,8},{14,10},{1,5},{3,7},... | collective-permute-start | bytes 196616 | tf_op jit(solution)/shard_map/ppermute | solution.py:292
  30.9 4.5 %collective-permute-start.11 = (bf16[8,4096]{1,0:T(8,128)(2,1)S(1)}, bf16[8,4096]{1,0:T(8,128)(2,1)S(1)}, u32[]{:S(2)}, u32[]{:S(2)}) collective-permute-start(bf16[8,4096]{1,0:T(8,128)(2,1)S(1)} %collective-permute-done.7), channel_id=1, source_target_pairs={{0,2},{2,0},{4,6},{6,4},{8,10},{10,8},{12,14},{14,12},{1,3},{3,1},... | collective-permute-start | bytes 196616 | tf_op jit(solution)/shard_map/ppermute | solution.py:292
  37.2 1.4 %collective-permute-start.13 = (f16[64,1024]{1,0:T(8,128)(2,1)S(1)}, f16[64,1024]{1,0:T(8,128)(2,1)S(1)}, u32[]{:S(2)}, u32[]{:S(2)}) collective-permute-start(f16[64,1024]{1,0:T(8,128)(2,1)S(1)} %multiply_convert_fusion), channel_id=1, source_target_pairs={{0,1},{1,0},{2,3},{3,2},{4,5},{5,4},{6,7},{7,6},{8,9},{9,8},{10,11... | collective-permute-start | bytes 393224 | tf_op jit(solution)/shard_map/ppermute | solution.py:385

commit v8 on v6

--- a/solution.py
+++ b/solution.py
@@ -142,6 +142,7 @@
         new_values,
         results,
         scores,
+        weights,
     ) = refs[parts:]
     rows_dev, kv_heads, _, width = key_cache.shape
     heads = queries.shape[0]
@@ -175,8 +176,7 @@
     factor = math.log2(math.e) / math.sqrt(width)
     contract = (((1,), (1,)), ((), ()))
 
-    tops = []
-    fresh = []
+    asked = []
     for row in range(rows_dev):
         own = []
         for index in range(kv_heads):
@@ -186,18 +186,14 @@
                     [queries[pick, row, :], queries[pick, rows_dev + row, :]], axis=0
                 ).astype(BF16)
             )
-        cached = jnp.concatenate(
-            [
-                lax.dot_general(own[index], key_cache[row, index], contract, preferred_element_type=F32)
-                for index in range(kv_heads)
-            ],
-            axis=0,
-        )
-        cached = cached + bias[row : row + 1, :]
-        scores[row] = cached
+        asked.append(own)
+    fresh = []
+    for row in range(rows_dev):
         new = jnp.concatenate(
             [
-                lax.dot_general(own[index], new_keys[index], contract, preferred_element_type=F32)
+                lax.dot_general(
+                    asked[row][index], new_keys[index], contract, preferred_element_type=F32
+                )
                 for index in range(kv_heads)
             ],
             axis=0,
@@ -205,19 +201,37 @@
         slot = lax.broadcasted_iota(jnp.int32, new.shape, 1)
         token = lax.rem(lax.broadcasted_iota(jnp.int32, new.shape, 0) // group, 2)
         seen = (lax.rem(slot, rows_dev) == row) & (slot // rows_dev <= token) & (slot < both)
-        new = jnp.where(seen, new, NEGATIVE)
-        tops.append(
-            jnp.maximum(
-                jnp.max(cached, axis=1, keepdims=True), jnp.max(new, axis=1, keepdims=True)
-            )
+        fresh.append(jnp.where(seen, new, NEGATIVE))
+    tops = []
+    for row in range(rows_dev):
+        cached = jnp.concatenate(
+            [
+                lax.dot_general(
+                    asked[row][index], key_cache[row, index], contract, preferred_element_type=F32
+                )
+                for index in range(kv_heads)
+            ],
+            axis=0,
         )
-        fresh.append(new)
+        cached = cached + bias[row : row + 1, :]
+        scores[row] = cached
+        tops.append(jnp.max(cached, axis=1, keepdims=True))
+    for row in range(rows_dev):
+        tops[row] = jnp.maximum(tops[row], jnp.max(fresh[row], axis=1, keepdims=True))
+    totals = []
+    news = []
     for row in range(rows_dev):
         weight = jnp.exp2((scores[row] - tops[row]) * factor)
         new = jnp.exp2((fresh[row] - tops[row]) * factor)
-        total = jnp.sum(weight, axis=1, keepdims=True) + jnp.sum(new, axis=1, keepdims=True)
-        weight = weight.astype(BF16)
-        new = new.astype(BF16)
+        totals.append(
+            jnp.sum(weight, axis=1, keepdims=True) + jnp.sum(new, axis=1, keepdims=True)
+        )
+        weights[row] = weight.astype(BF16)
+        news.append(new.astype(BF16))
+    for row in range(rows_dev):
+        new = news[row]
+        total = totals[row]
+        weight = weights[row]
         values = jnp.concatenate([value_cache[row, index] for index in range(kv_heads)], axis=1)
         mixed = jnp.dot(weight, values, preferred_element_type=F32)
         for index in range(kv_heads):
@@ -358,6 +372,7 @@
             pltpu.VMEM((kv_heads, 2 * both, width), BF16),
             pltpu.VMEM((heads, both, width), F32),
             pltpu.VMEM((rows_dev, 2 * heads, slots), F32),
+            pltpu.VMEM((rows_dev, 2 * heads, slots), BF16),
         ],
         compiler_params=pltpu.CompilerParams(vmem_limit_bytes=32 * MIB),
         name="attend",

time: 39.6 us -> 39.7 us (level)
  no operation moved by 1% of the time
where the time goes in v8:
time: 39.7 us; the launch traced here: 39.5 us
  starting transfers between devices  20.9 us (53%)
  Pallas kernels  8.67 us (22%)
  waiting for transfers between devices  7.65 us (19%)
  other arithmetic  1.28 us (3%)
  between operations  0.95 us (2%)
    ppermute x13, starting transfers between devices, exchange(): return lax.ppermute(value, ('wide', 'narrow'), pairs)  20.8 us
    ppermute x13, waiting for transfers between devices, exchange(): return lax.ppermute(value, ('wide', 'narrow'), pairs)  6.32 us
    pallas_call x1, Pallas kernels, on_device(): pl.pallas_call(functools.partial(project_kernel, rows_dev, outer, plans),...  4.4 us
    pallas_call x1, Pallas kernels, on_device(): pl.pallas_call(functools.partial(attend_kernel, len(received), devices *...  2.44 us
    pallas_call x1, Pallas kernels, on_device(): pl.pallas_call(functools.partial(output_kernel, rows_dev, outer, gather_p...  1.75 us
    ppermute x1, waiting for transfers between devices, on_device(): lax.ppermute(part, 'narrow', [(c, cores - 1 - c) for c in range(cores)])  1.33 us
  transfers between devices with their start and end apart: 14, of which 6 were waited for; matrix products, arithmetic and copies ran while one was open for 1% of the time, Pallas kernels for 0%

profile of v8, /device:TPU:0, one launch (start us, length us, event | category | flops | bytes accessed | tf_op | source)
XLA Modules:
  0.0 39.5 jit_solution(11253832999747404562)
XLA Ops:
  0.7 4.4 %project.1 = (f32[8,4736]{1,0:T(8,128)S(1)}, f32[8,4736]{1,0:T(8,128)S(1)}, f32[8,4736]{1,0:T(8,128)S(1)}, f32[8,4736]{1,0:T(8,128)S(1)}, f32[8,4736]{1,0:T(8,12...) custom-call(bf16[32,1024]{1,0:T(8,128)(2,1)} %first.1, bf16[32,1024]{1,0:T(8,128)(2,1)} %second.1, ...), custom_call_target="tpu_custom_call" | custom-call | flops 620756992 | bytes 9699328 | tf_op jit(solution)/shard_map/project/pallas_call | solution.py:313
  5.1 4.0 %collective-permute-start.3 = (f16[8,4736]{1,0:T(8,128)(2,1)S(1)}, f16[8,4736]{1,0:T(8,128)(2,1)S(1)}, u32[]{:S(2)}, u32[]{:S(2)}) collective-permute-start(f16[8,4736]{1,0:T(8,128)(2,1)S(1)} %convert_element_type.77), channel_id=1, source_target_pairs={{0,6},{2,4},{4,2},{6,0},{8,14},{10,12},{12,10},{14,8},{1,7},{3,5},... | collective-permute-start | bytes 227336 | tf_op jit(solution)/shard_map/ppermute | solution.py:306
  9.2 0.6 %collective-permute-start.4 = (f16[8,4736]{1,0:T(8,128)(2,1)S(1)}, f16[8,4736]{1,0:T(8,128)(2,1)S(1)}, u32[]{:S(2)}, u32[]{:S(2)}) collective-permute-start(f16[8,4736]{1,0:T(8,128)(2,1)S(1)} %convert_element_type.79), channel_id=1, source_target_pairs={{0,2},{2,0},{4,6},{6,4},{8,10},{10,8},{12,14},{14,12},{1,3},{3,1},... | collective-permute-start | bytes 227336 | tf_op jit(solution)/shard_map/ppermute | solution.py:306
  9.8 0.1 collective-permute-start.5
  9.9 3.0 %collective-permute-start = (f16[8,4736]{1,0:T(8,128)(2,1)S(1)}, f16[8,4736]{1,0:T(8,128)(2,1)S(1)}, u32[]{:S(2)}, u32[]{:S(2)}) collective-permute-start(f16[8,4736]{1,0:T(8,128)(2,1)S(1)} %convert_element_type.71), channel_id=1, source_target_pairs={{0,6},{2,4},{4,2},{6,0},{8,14},{10,12},{12,10},{14,8},{1,7},{3,5},... | collective-permute-start | bytes 227336 | tf_op jit(solution)/shard_map/ppermute | solution.py:306
  12.9 0.6 %collective-permute-start.1 = (f16[8,4736]{1,0:T(8,128)(2,1)S(1)}, f16[8,4736]{1,0:T(8,128)(2,1)S(1)}, u32[]{:S(2)}, u32[]{:S(2)}) collective-permute-start(f16[8,4736]{1,0:T(8,128)(2,1)S(1)} %convert_element_type.73), channel_id=1, source_target_pairs={{0,2},{2,0},{4,6},{6,4},{8,10},{10,8},{12,14},{14,12},{1,3},{3,1},... | collective-permute-start | bytes 227336 | tf_op jit(solution)/shard_map/ppermute | solution.py:306
  13.6 0.1 fusion.3
  13.8 0.2 collective-permute-start.2
  14.0 0.5 %collective-permute-done.4 = f16[8,4736]{1,0:T(8,128)(2,1)S(1)} collective-permute-done((f16[8,4736]{1,0:T(8,128)(2,1)S(1)}, f16[8,4736]{1,0:T(8,128)(2,1)S(1)}, u32[]{:S(2)}, u32[]{:S(2)}) %collective-permute-start.4) | collective-permute-done | bytes 75808 | tf_op jit(solution)/shard_map/ppermute | solution.py:306
  14.5 0.1 combine.1
  14.6 2.7 %collective-permute-start.6 = (f16[8,4736]{1,0:T(8,128)(2,1)S(1)}, f16[8,4736]{1,0:T(8,128)(2,1)S(1)}, u32[]{:S(2)}, u32[]{:S(2)}) collective-permute-start(f16[8,4736]{1,0:T(8,128)(2,1)S(1)} %convert_element_type.83), channel_id=1, source_target_pairs={{0,8},{2,10},{4,12},{6,14},{8,0},{10,2},{12,4},{14,6},{1,9},{3,11}... | collective-permute-start | bytes 227336 | tf_op jit(solution)/shard_map/ppermute | solution.py:306
  17.4 0.8 %collective-permute-done.2 = f16[8,4736]{1,0:T(8,128)(2,1)S(1)} collective-permute-done((f16[8,4736]{1,0:T(8,128)(2,1)S(1)}, f16[8,4736]{1,0:T(8,128)(2,1)S(1)}, u32[]{:S(2)}, u32[]{:S(2)}) %collective-permute-start.2) | collective-permute-done | bytes 75808 | tf_op jit(solution)/shard_map/ppermute | solution.py:306
  18.2 1.9 %collective-permute-done.6 = f16[8,4736]{1,0:T(8,128)(2,1)S(1)} collective-permute-done((f16[8,4736]{1,0:T(8,128)(2,1)S(1)}, f16[8,4736]{1,0:T(8,128)(2,1)S(1)}, u32[]{:S(2)}, u32[]{:S(2)}) %collective-permute-start.6) | collective-permute-done | bytes 75808 | tf_op jit(solution)/shard_map/ppermute | solution.py:306
  20.2 2.4 %attend.1 = bf16[8,4096]{1,0:T(8,128)(2,1)S(1)} custom-call(f32[4,2048]{1,0:T(4,128)S(1)} %fusion.2.bias, f32[8,4736]{1,0:T(8,128)S(1)} %get-tuple-element.10.mine, f32[8,4736]{1,0:T(8,128)S(1)} %convert_element_type.72.refs_0_, f32[8,4736]{1,0:T(8,128)S(1)} %convert_element_type.74.refs_1_, f32[8,4736]{1,0:T(8,128)S(1)} %convert_element_type.76.refs_2_, ...), custom_call_target="tpu_custom_call" | custom-call | tf_op jit(solution)/shard_map/attend/pallas_call | solution.py:364
  22.6 2.6 %collective-permute-start.7 = (bf16[8,4096]{1,0:T(8,128)(2,1)S(1)}, bf16[8,4096]{1,0:T(8,128)(2,1)S(1)}, u32[]{:S(2)}, u32[]{:S(2)}) collective-permute-start(bf16[8,4096]{1,0:T(8,128)(2,1)S(1)} %attend.1), channel_id=1, source_target_pairs={{0,8},{2,10},{4,12},{6,14},{8,0},{10,2},{12,4},{14,6},{1,9},{3,11}... | collective-permute-start | bytes 196616 | tf_op jit(solution)/shard_map/ppermute | solution.py:306
  25.3 1.3 %collective-permute-start.8 = (bf16[8,4096]{1,0:T(8,128)(2,1)S(1)}, bf16[8,4096]{1,0:T(8,128)(2,1)S(1)}, u32[]{:S(2)}, u32[]{:S(2)}) collective-permute-start(bf16[8,4096]{1,0:T(8,128)(2,1)S(1)} %attend.1), channel_id=1, source_target_pairs={{0,2},{2,0},{4,6},{6,4},{8,10},{10,8},{12,14},{14,12},{1,5},{3,7},... | collective-permute-start | bytes 196616 | tf_op jit(solution)/shard_map/ppermute | solution.py:306
  26.6 2.2 %collective-permute-start.10 = (bf16[8,4096]{1,0:T(8,128)(2,1)S(1)}, bf16[8,4096]{1,0:T(8,128)(2,1)S(1)}, u32[]{:S(2)}, u32[]{:S(2)}) collective-permute-start(bf16[8,4096]{1,0:T(8,128)(2,1)S(1)} %attend.1), channel_id=1, source_target_pairs={{0,4},{2,6},{4,0},{6,2},{8,12},{10,14},{12,8},{14,10},{1,3},{3,1},... | collective-permute-start | bytes 196616 | tf_op jit(solution)/shard_map/ppermute | solution.py:306
  28.8 1.7 %collective-permute-start.12 = (bf16[16,4096]{1,0:T(8,128)(2,1)S(1)}, bf16[16,4096]{1,0:T(8,128)(2,1)S(1)}, u32[]{:S(2)}, u32[]{:S(2)}) collective-permute-start(bf16[16,4096]{1,0:T(8,128)(2,1)S(1)} %pad_maximum_fusion), channel_id=1, source_target_pairs={{0,6},{2,4},{4,2},{6,0},{8,14},{10,12},{12,10},{14,8},{1,7},{3,5},... | collective-permute-start | bytes 393224 | tf_op jit(solution)/shard_map/ppermute | solution.py:306
  30.5 0.6 %collective-permute-start.9 = (bf16[8,4096]{1,0:T(8,128)(2,1)S(1)}, bf16[8,4096]{1,0:T(8,128)(2,1)S(1)}, u32[]{:S(2)}, u32[]{:S(2)}) collective-permute-start(bf16[8,4096]{1,0:T(8,128)(2,1)S(1)} %collective-permute-done.7), channel_id=1, source_target_pairs={{0,2},{2,0},{4,6},{6,4},{8,10},{10,8},{12,14},{14,12},{1,5},{3,7},... | collective-permute-start | bytes 196616 | tf_op jit(solution)/shard_map/ppermute | solution.py:306
  31.2 1.2 %collective-permute-start.11 = (bf16[8,4096]{1,0:T(8,128)(2,1)S(1)}, bf16[8,4096]{1,0:T(8,128)(2,1)S(1)}, u32[]{:S(2)}, u32[]{:S(2)}) collective-permute-start(bf16[8,4096]{1,0:T(8,128)(2,1)S(1)} %collective-permute-done.7), channel_id=1, source_target_pairs={{0,4},{2,6},{4,0},{6,2},{8,12},{10,14},{12,8},{14,10},{1,3},{3,1},... | collective-permute-start | bytes 196616 | tf_op jit(solution)/shard_map/ppermute | solution.py:306
  32.4 3.1 %collective-permute-done.9 = bf16[8,4096]{1,0:T(8,128)(2,1)S(1)} collective-permute-done((bf16[8,4096]{1,0:T(8,128)(2,1)S(1)}, bf16[8,4096]{1,0:T(8,128)(2,1)S(1)}, u32[]{:S(2)}, u32[]{:S(2)}) %collective-permute-start.9) | collective-permute-done | bytes 65568 | tf_op jit(solution)/shard_map/ppermute | solution.py:306
  35.6 1.8 %output.1 = f32[64,1024]{1,0:T(8,128)S(1)} custom-call(bf16[64,4096]{1,0:T(8,128)(2,1)S(1)} %constant_dynamic-update-slice_fusion.gathered, bf16[4096,1024]{1,0:T(8,128)(2,1)S(1)} %bitcast.1), custom_call_target="tpu_custom_call" | custom-call | tf_op jit(solution)/shard_map/output/pallas_call | solution.py:391
  37.4 1.3 %collective-permute-done.13 = f16[64,1024]{1,0:T(8,128)(2,1)S(1)} collective-permute-done((f16[64,1024]{1,0:T(8,128)(2,1)S(1)}, f16[64,1024]{1,0:T(8,128)(2,1)S(1)}, u32[]{:S(2)}, u32[]{:S(2)}) %collective-permute-start.13) | collective-permute-done | bytes 131104 | tf_op jit(solution)/shard_map/ppermute | solution.py:400
  38.8 0.7 %fusion = (bf16[32,1024]{1,0:T(8,128)(2,1)}, bf16[32,1024]{1,0:T(8,128)(2,1)}) fusion(f32[64,1024]{1,0:T(8,128)S(1)} %add_multiply_fusion, bf16[32,1024]{1,0:T(8,128)(2,1)S(1)} %copy-done.3, bf16[32,1024]{1,0:T(8,128)(2,1)S(1)} %copy-done.2), kind=kLoop, calls=%fused_computation.3 | loop fusion | flops 196608 | bytes 524288 | tf_op jit(solution)/shard_map/convert_element_type | solution.py:404
  (56 shorter events, 0.7 us)
Async XLA Ops:
  0.6 12.8 %copy-start.5 = (s32[4]{0:T(128)S(1)}, s32[4]{0:T(128)}, u32[]{:S(2)}) copy-start(s32[4]{0:T(128)} %param.21) | copy-start | bytes 52
  0.6 12.9 %copy-start.4 = (s32[4]{0:T(128)S(1)}, s32[4]{0:T(128)}, u32[]{:S(2)}) copy-start(s32[4]{0:T(128)} %param.20) | copy-start | bytes 52
  0.7 19.5 %copy-start = (bf16[4,2,2048,128]{3,2,1,0:T(8,128)(2,1)S(1)}, bf16[4,2,2048,128]{3,2,1,0:T(8,128)(2,1)}, u32[]{:S(2)}) copy-start(bf16[4,2,2048,128]{3,2,1,0:T(8,128)(2,1)} %refs_6_.1) | copy-start | bytes 12582916
  0.7 19.5 %copy-start.1 = (bf16[4,2,2048,128]{3,2,1,0:T(8,128)(2,1)S(1)}, bf16[4,2,2048,128]{3,2,1,0:T(8,128)(2,1)}, u32[]{:S(2)}) copy-start(bf16[4,2,2048,128]{3,2,1,0:T(8,128)(2,1)} %refs_7_.1) | copy-start | bytes 12582916
  0.7 34.9 %slice-start = ((s8[8388608]{0:T(1024)(128)(4,1)}), s8[4194304]{0:T(1024)(128)(4,1)S(1)}, s32[]{:S(2)}) async-start(s8[8388608]{0:T(1024)(128)(4,1)} %bitcast), calls=%async_computation | async-start | bytes 8388608
  5.1 8.7 %collective-permute-start.3 = (f16[8,4736]{1,0:T(8,128)(2,1)S(1)}, f16[8,4736]{1,0:T(8,128)(2,1)S(1)}, u32[]{:S(2)}, u32[]{:S(2)}) collective-permute-start(f16[8,4736]{1,0:T(8,128)(2,1)S(1)} %convert_element_type.77), channel_id=1, source_target_pairs={{0,6},{2,4},{4,2},{6,0},{8,14},{10,12},{12,10},{14,8},{1,7},{3,5},... | collective-permute-start | bytes 227336 | tf_op jit(solution)/shard_map/ppermute | solution.py:306
  9.2 5.3 %collective-permute-start.4 = (f16[8,4736]{1,0:T(8,128)(2,1)S(1)}, f16[8,4736]{1,0:T(8,128)(2,1)S(1)}, u32[]{:S(2)}, u32[]{:S(2)}) collective-permute-start(f16[8,4736]{1,0:T(8,128)(2,1)S(1)} %convert_element_type.79), channel_id=1, source_target_pairs={{0,2},{2,0},{4,6},{6,4},{8,10},{10,8},{12,14},{14,12},{1,3},{3,1},... | collective-permute-start | bytes 227336 | tf_op jit(solution)/shard_map/ppermute | solution.py:306
  9.8 4.8 %collective-permute-start.5 = (f16[8,4736]{1,0:T(8,128)(2,1)S(1)}, f16[8,4736]{1,0:T(8,128)(2,1)S(1)}, u32[]{:S(2)}, u32[]{:S(2)}) collective-permute-start(f16[8,4736]{1,0:T(8,128)(2,1)S(1)} %convert_element_type.81), channel_id=1, source_target_pairs={{0,4},{2,6},{4,0},{6,2},{8,12},{10,14},{12,8},{14,10},{1,5},{3,7},... | collective-permute-start | bytes 227336 | tf_op jit(solution)/shard_map/ppermute | solution.py:306
  9.9 7.5 %collective-permute-start = (f16[8,4736]{1,0:T(8,128)(2,1)S(1)}, f16[8,4736]{1,0:T(8,128)(2,1)S(1)}, u32[]{:S(2)}, u32[]{:S(2)}) collective-permute-start(f16[8,4736]{1,0:T(8,128)(2,1)S(1)} %convert_element_type.71), channel_id=1, source_target_pairs={{0,6},{2,4},{4,2},{6,0},{8,14},{10,12},{12,10},{14,8},{1,7},{3,5},... | collective-permute-start | bytes 227336 | tf_op jit(solution)/shard_map/ppermute | solution.py:306
  12.9 4.5 %collective-permute-start.1 = (f16[8,4736]{1,0:T(8,128)(2,1)S(1)}, f16[8,4736]{1,0:T(8,128)(2,1)S(1)}, u32[]{:S(2)}, u32[]{:S(2)}) collective-permute-start(f16[8,4736]{1,0:T(8,128)(2,1)S(1)} %convert_element_type.73), channel_id=1, source_target_pairs={{0,2},{2,0},{4,6},{6,4},{8,10},{10,8},{12,14},{14,12},{1,3},{3,1},... | collective-permute-start | bytes 227336 | tf_op jit(solution)/shard_map/ppermute | solution.py:306
  13.8 4.4 %collective-permute-start.2 = (f16[8,4736]{1,0:T(8,128)(2,1)S(1)}, f16[8,4736]{1,0:T(8,128)(2,1)S(1)}, u32[]{:S(2)}, u32[]{:S(2)}) collective-permute-start(f16[8,4736]{1,0:T(8,128)(2,1)S(1)} %convert_element_type.75), channel_id=1, source_target_pairs={{0,4},{2,6},{4,0},{6,2},{8,12},{10,14},{12,8},{14,10},{1,5},{3,7},... | collective-permute-start | bytes 227336 | tf_op jit(solution)/shard_map/ppermute | solution.py:306
  14.5 21.0 %slice-start.1 = ((s8[8388608]{0:T(1024)(128)(4,1)}), s8[4194304]{0:T(1024)(128)(4,1)S(1)}, s32[]{:S(2)}) async-start(s8[8388608]{0:T(1024)(128)(4,1)} %bitcast), calls=%async_computation.1 | async-start | bytes 8388608
  14.6 5.5 %collective-permute-start.6 = (f16[8,4736]{1,0:T(8,128)(2,1)S(1)}, f16[8,4736]{1,0:T(8,128)(2,1)S(1)}, u32[]{:S(2)}, u32[]{:S(2)}) collective-permute-start(f16[8,4736]{1,0:T(8,128)(2,1)S(1)} %convert_element_type.83), channel_id=1, source_target_pairs={{0,8},{2,10},{4,12},{6,14},{8,0},{10,2},{12,4},{14,6},{1,9},{3,11}... | collective-permute-start | bytes 227336 | tf_op jit(solution)/shard_map/ppermute | solution.py:306
  20.2 18.6 %copy-start.2 = (bf16[32,1024]{1,0:T(8,128)(2,1)S(1)}, bf16[32,1024]{1,0:T(8,128)(2,1)}, u32[]{:S(2)}) copy-start(bf16[32,1024]{1,0:T(8,128)(2,1)} %first.1) | copy-start | bytes 196612
  20.2 18.6 %copy-start.3 = (bf16[32,1024]{1,0:T(8,128)(2,1)S(1)}, bf16[32,1024]{1,0:T(8,128)(2,1)}, u32[]{:S(2)}) copy-start(bf16[32,1024]{1,0:T(8,128)(2,1)} %second.1) | copy-start | bytes 196612
  22.6 6.1 %collective-permute-start.7 = (bf16[8,4096]{1,0:T(8,128)(2,1)S(1)}, bf16[8,4096]{1,0:T(8,128)(2,1)S(1)}, u32[]{:S(2)}, u32[]{:S(2)}) collective-permute-start(bf16[8,4096]{1,0:T(8,128)(2,1)S(1)} %attend.1), channel_id=1, source_target_pairs={{0,8},{2,10},{4,12},{6,14},{8,0},{10,2},{12,4},{14,6},{1,9},{3,11}... | collective-permute-start | bytes 196616 | tf_op jit(solution)/shard_map/ppermute | solution.py:306
  25.3 7.1 %collective-permute-start.8 = (bf16[8,4096]{1,0:T(8,128)(2,1)S(1)}, bf16[8,4096]{1,0:T(8,128)(2,1)S(1)}, u32[]{:S(2)}, u32[]{:S(2)}) collective-permute-start(bf16[8,4096]{1,0:T(8,128)(2,1)S(1)} %attend.1), channel_id=1, source_target_pairs={{0,2},{2,0},{4,6},{6,4},{8,10},{10,8},{12,14},{14,12},{1,5},{3,7},... | collective-permute-start | bytes 196616 | tf_op jit(solution)/shard_map/ppermute | solution.py:306
  26.6 8.9 %collective-permute-start.10 = (bf16[8,4096]{1,0:T(8,128)(2,1)S(1)}, bf16[8,4096]{1,0:T(8,128)(2,1)S(1)}, u32[]{:S(2)}, u32[]{:S(2)}) collective-permute-start(bf16[8,4096]{1,0:T(8,128)(2,1)S(1)} %attend.1), channel_id=1, source_target_pairs={{0,4},{2,6},{4,0},{6,2},{8,12},{10,14},{12,8},{14,10},{1,3},{3,1},... | collective-permute-start | bytes 196616 | tf_op jit(solution)/shard_map/ppermute | solution.py:306
  28.8 6.7 %collective-permute-start.12 = (bf16[16,4096]{1,0:T(8,128)(2,1)S(1)}, bf16[16,4096]{1,0:T(8,128)(2,1)S(1)}, u32[]{:S(2)}, u32[]{:S(2)}) collective-permute-start(bf16[16,4096]{1,0:T(8,128)(2,1)S(1)} %pad_maximum_fusion), channel_id=1, source_target_pairs={{0,6},{2,4},{4,2},{6,0},{8,14},{10,12},{12,10},{14,8},{1,7},{3,5},... | collective-permute-start | bytes 393224 | tf_op jit(solution)/shard_map/ppermute | solution.py:306
  30.5 4.9 %collective-permute-start.9 = (bf16[8,4096]{1,0:T(8,128)(2,1)S(1)}, bf16[8,4096]{1,0:T(8,128)(2,1)S(1)}, u32[]{:S(2)}, u32[]{:S(2)}) collective-permute-start(bf16[8,4096]{1,0:T(8,128)(2,1)S(1)} %collective-permute-done.7), channel_id=1, source_target_pairs={{0,2},{2,0},{4,6},{6,4},{8,10},{10,8},{12,14},{14,12},{1,5},{3,7},... | collective-permute-start | bytes 196616 | tf_op jit(solution)/shard_map/ppermute | solution.py:306
  31.2 4.3 %collective-permute-start.11 = (bf16[8,4096]{1,0:T(8,128)(2,1)S(1)}, bf16[8,4096]{1,0:T(8,128)(2,1)S(1)}, u32[]{:S(2)}, u32[]{:S(2)}) collective-permute-start(bf16[8,4096]{1,0:T(8,128)(2,1)S(1)} %collective-permute-done.7), channel_id=1, source_target_pairs={{0,4},{2,6},{4,0},{6,2},{8,12},{10,14},{12,8},{14,10},{1,3},{3,1},... | collective-permute-start | bytes 196616 | tf_op jit(solution)/shard_map/ppermute | solution.py:306
  37.3 1.4 %collective-permute-start.13 = (f16[64,1024]{1,0:T(8,128)(2,1)S(1)}, f16[64,1024]{1,0:T(8,128)(2,1)S(1)}, u32[]{:S(2)}, u32[]{:S(2)}) collective-permute-start(f16[64,1024]{1,0:T(8,128)(2,1)S(1)} %multiply_convert_fusion), channel_id=1, source_target_pairs={{0,1},{1,0},{2,3},{3,2},{4,5},{5,4},{6,7},{7,6},{8,9},{9,8},{10,11... | collective-permute-start | bytes 393224 | tf_op jit(solution)/shard_map/ppermute | solution.py:400
